TPU v7x, 256 devices: a whole 4x4x8 slice. The times are simulated.
256 devices in a mesh: feat: 8 (over z_hi, y), node: 32 (over x, z_lo, core).
Axes of the slice: x: 4, y: 4, z: 8 (z_hi: 2, z_lo: 4; z = z_hi * 4 + z_lo), core: 2. Of those that a mesh axis runs over, the one named last changes fastest.
Arguments:
- features: bfloat16 [65536, 4096], P('node', 'feat'), may hold values from -6 to 6
- seed_feats: bfloat16 [4096, 4096], P('node', 'feat'), may hold values from -6 to 6
- patterns: int32 [1024, 8, 128, 8], P('node'), may hold values from 0 to 65535, as said below
- sources: int32 [1024, 8], P('node'), may hold values from 0 to 15
- counts: int32 [1024], P('node'), may hold values from 1 to 8
- w_self: bfloat16 [4096, 1024], P('feat'), may hold values from -0.09375 to 0.09375
- w_neigh: bfloat16 [4096, 1024], P('feat'), may hold values from -0.09375 to 0.09375
- bias_term: float32 [1024], replicated, may hold values from -3 to 3
- out_grad: bfloat16 [4096, 1024], P('node'), may hold values from -0.3125 to 0.3125
Outputs:
- hidden: bfloat16 [4096, 1024], P('node')
- grad_self: float32 [4096, 1024], P(('feat', 'node'))
- grad_neigh: float32 [4096, 1024], P(('feat', 'node'))
- grad_bias: float32 [1024], P('node')
Inputs may be any that keep to these rules, and one draw needn't show every extreme that they name: `patterns`: each word holds 16 entries of 0 or 1 in its 16 low bits.
All inputs are finite; a program needn't handle non-finite values.
Results may differ from a plain program's by a relative error of at most 0.024.
The roundings to bfloat16 on the way count: a program that leaves them out, or rounds other values in their place, can miss the bound.
Values may be sent and summed in bfloat16 or wider, within the bound.
No kernel may reach another device: no remote copies, remote signals or barrier semaphores. Data moves between devices by JAX's collectives and lax.ppermute only.
A program may use at most 128 MiB of HBM per device.

v0:
```python
import functools

import jax
import jax.numpy as jnp
from jax import lax
from jax.experimental import pallas as pl
from jax.experimental.pallas import tpu as pltpu
from jax.sharding import PartitionSpec as P

BLK = 128
HALF = 256
FAN = 8
TOP = 32700.0
NX, NZ, NY = 4, 4, 4
WIDE = 512
VMEM = pl.BlockSpec(memory_space=pltpu.VMEM)
SMEM = pl.BlockSpec(memory_space=pltpu.SMEM)
PARAMS = pltpu.CompilerParams(vmem_limit_bytes=40 * 1024 * 1024)
F32 = functools.partial(lax.dot_general, preferred_element_type=jnp.float32)


def node_of(x, z, c):
    return x * (NZ * 2) + z * 2 + c


NODES = [(x, z, c) for x in range(NX) for z in range(NZ) for c in range(2)]
SWAP_CORE = [(n, n ^ 1) for n in range(NX * NZ * 2)]
SWAP_FAR = [(f, f ^ 4) for f in range(8)]


def shift_x(d):
    return [(node_of(x, z, c), node_of((x + d) % NX, z, c)) for x, z, c in NODES]


def shift_z(d):
    return [(node_of(x, z, c), node_of(x, (z + d) % NZ, c)) for x, z, c in NODES]


def shift_y(d):
    return [(h * 4 + y, h * 4 + (y + d) % NY) for h in range(2) for y in range(NY)]


def step_of(mantissa, exponent):
    return mantissa * jnp.exp2(exponent)


def encode(sums, count):
    top = jnp.maximum(jnp.max(jnp.abs(sums), axis=0, keepdims=True), 1e-25) * (1.0 / TOP)
    exponent = jnp.floor(jnp.log2(top)) - 13.0
    mantissa = jnp.ceil(top * jnp.exp2(-exponent))
    coded = jnp.round(sums * (1.0 / step_of(mantissa, exponent))).astype(jnp.int32).astype(jnp.int16)
    row = lax.broadcasted_iota(jnp.int32, (16, BLK), 0)
    tail = jnp.where(row == 0, count, jnp.where(row == 1, exponent, jnp.where(row == 2, mantissa, 0.0)))
    return coded, tail.astype(jnp.int32).astype(jnp.int16)


def put_coded(ref, sums, count):
    rows = sums.shape[0]
    coded, tail = encode(sums, count)
    ref[pl.ds(0, rows), :] = coded
    ref[pl.ds(rows, 16), :] = tail


def put_plain(ref, sums, count):
    rows = sums.shape[0]
    ref[pl.ds(0, rows), :] = sums
    ref[pl.ds(rows, 8), :] = jnp.broadcast_to(count, (8, BLK))


def plain(ref):
    rows = ref.shape[0] - 8
    return ref[pl.ds(0, rows), :], ref[pl.ds(rows, 8), :][0:1]


def decode(ref):
    rows = ref.shape[0] - 16
    tail = ref[pl.ds(rows, 16), :].astype(jnp.int32).astype(jnp.float32)
    values = ref[pl.ds(0, rows), :].astype(jnp.int32).astype(jnp.float32)
    return values * step_of(tail[2:3], tail[1:2]), tail[0:1]


def gathered(plain_refs, coded_refs):
    pairs = [plain(ref) for ref in plain_refs] + [decode(ref) for ref in coded_refs]
    return sum(pair[0] for pair in pairs), sum(pair[1] for pair in pairs)


def sums_kernel(coded_out, meta_ref, pat0_ref, pat1_ref, feat0_ref, feat1_ref, out_ref, *scratch):
    tiles, accs, pops = scratch[0:2], scratch[2:4], scratch[4:7]
    pats, feats = (pat0_ref, pat1_ref), (feat0_ref, feat1_ref)
    blocks = pat0_ref.shape[0]
    slots = [(side, slot) for side in range(2) for slot in range(FAN)]
    put = put_coded if coded_out else put_plain

    def unpack(i, tile_ref, pop_ref):
        shifts = lax.broadcasted_iota(jnp.int32, (8, 16, BLK), 1)
        total = jnp.zeros((8, BLK), jnp.int32)
        for j, (side, slot) in enumerate(slots):
            live = meta_ref[2 + side * 32 + meta_ref[0] * blocks + i]
            words = pats[side][i, slot] * (slot < live).astype(jnp.int32)
            total += lax.population_count(words)
            bits = (jnp.broadcast_to(words[:, None, :], (8, 16, BLK)) >> shifts) & 1
            tile_ref[pl.ds(j * BLK, BLK), :] = bits.reshape(BLK, BLK).astype(jnp.float32).astype(jnp.bfloat16)
        pop_ref[...] = total

    def multiply(i, tile_ref, acc_ref):
        picked = []
        for side, slot in slots:
            source = meta_ref[66 + (side * 32 + meta_ref[0] * blocks + i) * FAN + slot]
            picked.append(feats[side][pl.ds(pl.multiple_of(source * BLK, BLK), BLK), :])
        acc_ref[...] = F32(tile_ref[...], jnp.concatenate(picked, axis=0), (((0,), (0,)), ((), ()))).T

    def finish(i, acc_ref, pop_ref):
        count = jnp.sum(pop_ref[...], axis=0, keepdims=True).astype(jnp.float32)
        put(out_ref.at[i], acc_ref[...], count)

    for step in range(blocks + 2):
        if step < blocks:
            unpack(step, tiles[step % 2], pops[step % 3])
        if 0 <= step - 1 < blocks:
            multiply(step - 1, tiles[(step - 1) % 2], accs[(step - 1) % 2])
        if 0 <= step - 2 < blocks:
            finish(step - 2, accs[(step - 2) % 2], pops[(step - 2) % 3])


def sums(coded_out, meta, pat0, pat1, feat0, feat1):
    blocks = 2 * NZ
    pats = pl.BlockSpec((blocks, FAN, 8, BLK), lambda i, m: (m[0], 0, 0, 0))
    rows, kind = (HALF + 16, jnp.int16) if coded_out else (HALF + 8, jnp.float32)
    return pl.pallas_call(
        functools.partial(sums_kernel, coded_out),
        out_shape=jax.ShapeDtypeStruct((blocks, rows, BLK), kind),
        grid_spec=pltpu.PrefetchScalarGridSpec(
            num_scalar_prefetch=1,
            grid=(1,),
            in_specs=[
                pats,
                pats,
                pl.BlockSpec((feat0.shape[0], HALF), lambda i, m: (0, m[1])),
                pl.BlockSpec(feat1.shape, lambda i, m: (0, 0)),
            ],
            out_specs=pl.BlockSpec((blocks, rows, BLK), lambda i, m: (0, 0, 0)),
            scratch_shapes=[pltpu.VMEM((2 * FAN * BLK, BLK), jnp.bfloat16)] * 2
            + [pltpu.VMEM((HALF, BLK), jnp.float32)] * 2
            + [pltpu.VMEM((8, BLK), jnp.int32)] * 3,
        ),
        compiler_params=PARAMS,
        cost_estimate=pl.CostEstimate(flops=2_000_000_000, bytes_accessed=3_000_000, transcendentals=0),
        name="sums",
    )(meta, pat0, pat1, feat0, feat1)


def call(kernel, name, outs, count, scratch=(), waits=0):
    return pl.pallas_call(
        kernel,
        out_shape=outs,
        in_specs=[SMEM] + [VMEM] * count + [pl.BlockSpec(memory_space=pl.ANY)] * waits,
        out_specs=[VMEM] * len(outs),
        scratch_shapes=list(scratch),
        compiler_params=PARAMS,
        name=name,
    )


def shaped(*dims):
    return jax.ShapeDtypeStruct(dims[:-1], dims[-1])


SUM_CODED = shaped(2, HALF + 16, BLK, jnp.int16)
SUM_PLAIN = shaped(2, HALF + 8, BLK, jnp.float32)
CODED = shaped(HALF + 16, BLK, jnp.int16)
PLAIN = shaped(HALF + 8, BLK, jnp.float32)
HALF16 = shaped(HALF, BLK, jnp.bfloat16)


def merge_x_kernel(pos_ref, r1_ref, r2_ref, r3_ref, own_ref, *rest):
    for d, out_ref in enumerate(rest[-4:]):
        for c in range(2):
            index = lax.rem(pos_ref[1] + d, NZ) * 2 + c
            total, count = gathered((own_ref.at[index],), [ref.at[index] for ref in (r1_ref, r2_ref, r3_ref)])
            (put_coded if d else put_plain)(out_ref.at[c], total, count)


def merge_z_kernel(pos_ref, r1_ref, r2_ref, r3_ref, own_ref, mine_ref, give_ref, rest_ref):
    core = pos_ref[2]
    for out_ref, index in ((mine_ref, core), (give_ref, 1 - core)):
        total, count = gathered((own_ref.at[index],), [ref.at[index] for ref in (r1_ref, r2_ref, r3_ref)])
        out_ref[pl.ds(0, HALF), :] = (total / jnp.sqrt(1.0 + count)).astype(jnp.bfloat16)
    for block in range(HALF // 32):
        keep = pl.ds(pl.multiple_of(block * 32 + core * 16, 16), 16)
        give = pl.ds(pl.multiple_of(block * 32 + 16 - core * 16, 16), 16)
        give_ref[pl.ds(HALF + block * 16, 16), :] = mine_ref[give, :]
        rest_ref[pl.ds(block * 16, 16), :] = give_ref[keep, :]


def pre_kernel(
    pos_ref, mine_ref, got_ref, rest_ref, w_ref, self_ref, own_ref, o1_ref, o2_ref, o3_ref, agg0_ref, agg1_ref, agg, acc
):
    core = pos_ref[2]
    agg[pl.ds(pl.multiple_of(core * HALF, HALF), HALF), :] = mine_ref[...]
    agg[pl.ds(pl.multiple_of((1 - core) * HALF, HALF), HALF), :] = got_ref[pl.ds(0, HALF), :]
    acc[...] = (self_ref[...] + F32(agg[...], w_ref[...], (((0,), (0,)), ((), ())))).T
    for d, out_ref in enumerate((own_ref, o1_ref, o2_ref, o3_ref)):
        terms = acc[pl.ds(pl.multiple_of(lax.rem(pos_ref[3] + d, NY) * HALF, HALF), HALF), :]
        (put_coded if d else put_plain)(out_ref, terms, jnp.zeros((1, BLK), jnp.float32))
    for block in range(WIDE // 32):
        rows = pl.ds(pl.multiple_of(block * 32 + core * 16, 16), 16)
        agg0_ref[pl.ds(block * 16, 16), :] = agg[rows, :]
    agg1_ref[pl.ds(pl.multiple_of(core * BLK, BLK), BLK), :] = rest_ref[...]
    agg1_ref[pl.ds(pl.multiple_of((1 - core) * BLK, BLK), BLK), :] = got_ref[pl.ds(HALF, BLK), :]


def merge_y_kernel(pos_ref, r1_ref, r2_ref, r3_ref, own_ref, out_ref):
    total, count = gathered((own_ref,), (r1_ref, r2_ref, r3_ref))
    put_coded(out_ref, total, count)


def hidden_kernel(pos_ref, own_ref, far_ref, out_ref):
    out_ref[...] = jnp.maximum(decode(own_ref)[0] + decode(far_ref)[0], 0.0).astype(jnp.bfloat16)


def grads_kernel(
    pos_ref, a0_ref, a1_ref, a2_ref, a3_ref, b0_ref, b1_ref, b2_ref, b3_ref, og0_ref, og1_ref,
    agg0_ref, agg1_ref, seed0_ref, seed1_ref,
    hidden_ref, own_ref, o1_ref, o2_ref, o3_ref, rows, self_acc, neigh_acc, bias,
):
    x, y = pos_ref[0], pos_ref[3]
    zero = jnp.zeros((BLK, HALF), jnp.bfloat16)
    for d in range(NY):
        place = pl.ds(pl.multiple_of(lax.rem(y + NY - d, NY) * HALF, HALF), HALF)
        for side, (refs, og_ref) in enumerate(
            (((a0_ref, a1_ref, a2_ref, a3_ref), og0_ref), ((b0_ref, b1_ref, b2_ref, b3_ref), og1_ref))
        ):
            value = refs[d][...].T
            if side == 0:
                hidden_ref[:, place] = value
            rows[pl.ds(side * BLK, BLK), place] = jnp.where(value > 0, og_ref[:, place], zero)
    hid = rows.shape[1]
    contract = (((1,), (0,)), ((), ()))
    self_acc[...] = F32(jnp.concatenate([seed0_ref[...], seed1_ref[...]], axis=1), rows[...], contract)
    neigh_acc[...] = F32(jnp.concatenate([agg0_ref[...], agg1_ref[...]], axis=1), rows[...], contract)
    total = F32(jnp.ones((8, 2 * BLK), jnp.bfloat16), rows[...], contract)[0:1]
    for part in range(hid // BLK):
        bias[pl.ds(part, 1), :] = total[:, part * BLK:(part + 1) * BLK]
    row = lax.broadcasted_iota(jnp.int32, (16, BLK), 0)
    for d, out_ref in enumerate((own_ref, o1_ref, o2_ref, o3_ref)):
        to = lax.rem(x + d, NX)
        take = pl.ds(pl.multiple_of(to * 64, 64), 64)
        out_ref[pl.ds(0, 64), pl.ds(0, hid)] = self_acc[take, :].astype(out_ref.dtype)
        out_ref[pl.ds(64, 64), pl.ds(0, hid)] = neigh_acc[take, :].astype(out_ref.dtype)
        left, right = bias[pl.ds(to * 2, 1), :], bias[pl.ds(to * 2 + 1, 1), :]
        left_top = left.astype(jnp.bfloat16).astype(jnp.float32)
        right_top = right.astype(jnp.bfloat16).astype(jnp.float32)
        mark = jnp.where(row == 0, left_top, jnp.where(row == 1, right_top, 0.0))
        mark = jnp.where(row == 2, left - left_top, jnp.where(row == 3, right - right_top, mark))
        out_ref[pl.ds(0, 16), pl.ds(hid, BLK)] = mark.astype(out_ref.dtype)
        out_ref[pl.ds(16, 112), pl.ds(hid, BLK)] = jnp.zeros((112, BLK), out_ref.dtype)


def fold_x_kernel(pos_ref, r1_ref, r2_ref, r3_ref, own_ref, kept_ref, o1_ref, o2_ref, o3_ref, total, bias):
    hid = total.shape[1]
    body, marks = pl.ds(0, hid), pl.ds(hid, BLK)
    refs = (r1_ref, r2_ref, r3_ref)
    total[...] = own_ref[:, body] + sum(ref[:, body].astype(jnp.float32) for ref in refs)
    top = pl.ds(0, 16)
    mark = own_ref[top, marks] + sum(ref[top, marks].astype(jnp.float32) for ref in refs)
    bias[pl.ds(0, 1), :] = mark[0:1] + mark[2:3]
    bias[pl.ds(1, 1), :] = mark[1:2] + mark[3:4]
    row = lax.broadcasted_iota(jnp.int32, (16, BLK), 0)
    for d, out_ref in enumerate((kept_ref, o1_ref, o2_ref, o3_ref)):
        to = lax.rem(pos_ref[1] + d, NZ)
        for kind in range(2):
            take = pl.ds(pl.multiple_of(kind * 64 + to * 16, 16), 16)
            out_ref[pl.ds(kind * 16, 16), body] = total[take, :].astype(out_ref.dtype)
        line = bias[pl.ds(to // 2, 1), :]
        high = line.astype(jnp.bfloat16).astype(jnp.float32)
        mark = jnp.where(row == 0, high, jnp.where(row == 1, line - high, 0.0))
        out_ref[top, marks] = mark.astype(out_ref.dtype)
        out_ref[pl.ds(16, 16), marks] = jnp.zeros((16, BLK), out_ref.dtype)


def last_kernel(pos_ref, r1_ref, r2_ref, r3_ref, own_ref, self_ref, neigh_ref, bias_ref):
    hid = self_ref.shape[1]
    body, marks = pl.ds(0, hid), pl.ds(hid, BLK)
    refs = (r1_ref, r2_ref, r3_ref)
    total = own_ref[:, body] + sum(ref[:, body].astype(jnp.float32) for ref in refs)
    top = pl.ds(0, 16)
    mark = own_ref[top, marks] + sum(ref[top, marks].astype(jnp.float32) for ref in refs)
    self_ref[...] = total[:16]
    neigh_ref[...] = total[16:]
    bias_ref[...] = jnp.broadcast_to(mark[0:1] + mark[1:2], (8, BLK))


def body(features, seed_feats, patterns, sources, counts, w_self, w_neigh, bias_term, out_grad):
    node = lax.axis_index("node")
    feat = lax.axis_index("feat")
    x, z, core = node // (NZ * 2), (node // 2) % NZ, node % 2
    y = feat % NY
    pos = jnp.stack([x, z, core, y]).astype(jnp.int32)
    hid = w_self.shape[1]
    swap = lambda value: lax.ppermute(value, "node", SWAP_CORE)

    packed = patterns.transpose(0, 1, 3, 2)
    table = jnp.concatenate([counts, sources.reshape(-1)])
    packed_other, table_other = swap(packed), swap(table)
    other = swap(jnp.where(core == 0, features[:, HALF:], features[:, :HALF]))
    lists = counts.shape[0]
    table = jnp.concatenate([table[:lists], table_other[:lists], table[lists:], table_other[lists:]])

    made = {}
    for d in (2, 1, 3, 0):
        meta = jnp.concatenate([jnp.stack([(x + d) % NX, core]).astype(jnp.int32), table])
        made[d] = sums(d > 0, meta, packed, packed_other, features, other)
    far = [lax.ppermute(made[d], "node", shift_x(d)) for d in (1, 2, 3)]

    seed_feats, w_self, bias_term, out_grad, own = lax.optimization_barrier(
        (seed_feats, w_self, bias_term, out_grad, made[0])
    )
    turned = seed_feats.T.reshape(WIDE // 32, 2, 16, BLK)
    pick = lambda c: lax.dynamic_index_in_dim(turned, c, 1, keepdims=False).reshape(HALF, BLK)
    seed_mine, seed_other = pick(core), swap(pick(1 - core))
    og_other = swap(out_grad)
    self_term = jnp.dot(seed_feats, w_self, preferred_element_type=jnp.float32)
    self_term = self_term + jnp.where(feat == 0, bias_term, 0.0)
    ready = (seed_mine, seed_other, og_other, self_term)

    own, *coded = call(merge_x_kernel, "merge_x", [SUM_PLAIN] + [SUM_CODED] * 3, 4, waits=len(ready))(
        pos, *far, own, *ready
    )
    arrived = [lax.ppermute(coded[d - 1], "node", shift_z(d)) for d in (2, 1, 3)]
    mine, give, rest = call(
        merge_z_kernel, "merge_z", [HALF16, shaped(HALF + BLK, BLK, jnp.bfloat16), shaped(BLK, BLK, jnp.bfloat16)], 4
    )(pos, *arrived, own)

    *coded, agg_mine, agg_other = call(
        pre_kernel, "pre_terms", [PLAIN] + [CODED] * 3 + [HALF16] * 2, 5,
        [pltpu.VMEM((WIDE, BLK), jnp.bfloat16), pltpu.VMEM((hid, BLK), jnp.float32)],
    )(pos, mine, swap(give), rest, w_neigh, self_term)
    own, *coded = coded
    received = [lax.ppermute(coded[d - 1], "feat", shift_y(d)) for d in (2, 1, 3)]
    (coded,) = call(merge_y_kernel, "merge_y", [CODED], 4)(pos, *received, own)
    far = lax.ppermute(coded, "feat", SWAP_FAR)
    (own,) = call(hidden_kernel, "hidden", [HALF16], 2)(pos, coded, far)
    chunks = [own] + [lax.ppermute(own, "feat", shift_y(d)) for d in (1, 2, 3)]
    chunks_other = [swap(chunk) for chunk in chunks]

    wide = hid + BLK
    scratch = [
        pltpu.VMEM((2 * BLK, hid), jnp.bfloat16),
        pltpu.VMEM((HALF, hid), jnp.float32),
        pltpu.VMEM((HALF, hid), jnp.float32),
        pltpu.VMEM((8, BLK), jnp.float32),
    ]
    outs = [shaped(BLK, hid, jnp.bfloat16), shaped(BLK, wide, jnp.float32)] + [shaped(BLK, wide, jnp.bfloat16)] * 3
    hidden, own, *parts = call(grads_kernel, "grads", outs, 14, scratch)(
        pos, *chunks, *chunks_other, out_grad, og_other, agg_mine, agg_other, seed_mine, seed_other
    )
    received = [lax.ppermute(parts[d - 1], "node", shift_x(d)) for d in (2, 1, 3)]
    own, *parts = call(
        fold_x_kernel, "fold_x", [shaped(32, wide, jnp.float32)] + [shaped(32, wide, jnp.bfloat16)] * 3, 4,
        [pltpu.VMEM((BLK, hid), jnp.float32), pltpu.VMEM((8, BLK), jnp.float32)],
    )(pos, *received, own)
    received = [lax.ppermute(parts[d - 1], "node", shift_z(d)) for d in (2, 1, 3)]
    part = shaped(16, hid, jnp.float32)
    grad_self, grad_neigh, bias = call(last_kernel, "last", [part, part, shaped(8, BLK, jnp.float32)], 4)(
        pos, *received, own
    )
    grad_bias = lax.dynamic_slice(bias[0], (z % 2 * 64 + core * 32,), (32,))
    return (hidden, grad_self, grad_neigh, grad_bias)


def solution(mesh):
    return jax.shard_map(
        body,
        mesh=mesh,
        in_specs=(
            P("node", "feat"),
            P("node", "feat"),
            P("node", None, None, None),
            P("node", None),
            P("node"),
            P("feat", None),
            P("feat", None),
            P(),
            P("node", None),
        ),
        out_specs=(
            P("node", None),
            P(("feat", "node"), None),
            P(("feat", "node"), None),
            P("node"),
        ),
        check_vma=False,
    )
```

profile of v0, /device:TPU:6, one launch (start us, length us, event | category | flops | bytes accessed | tf_op | source)
XLA Modules:
  0.0 127.8 jit_solution(10987581005110882989)
XLA Ops:
  0.7 0.1 collective-permute-start.1
  0.8 2.8 %slice_select_fusion = bf16[2048,256]{1,0:T(8,128)(2,1)} fusion(bf16[2048,512]{1,0:T(8,128)(2,1)} %feat0_ref.7, pred[]{:T(512)S(6)} %eq.15), kind=kLoop, calls=%fused_computation.1 | loop fusion | flops 524288 | bytes 3145729 | tf_op jit(solution)/shard_map/jit(_where)/select_n | solution.py:305
  3.6 0.4 collective-permute-start.2
  4.0 0.1 reshape.24
  4.2 0.1 collective-permute-start
  4.4 1.8 %collective-permute-done = s32[288]{0:T(512)S(1)} collective-permute-done((s32[288]{0:T(512)S(1)}, s32[288]{0:T(512)S(1)}, u32[]{:S(2)}, u32[]{:S(2)}) %collective-permute-start) | collective-permute-done | bytes 1184 | tf_op jit(solution)/shard_map/ppermute | solution.py:300
  6.5 0.1 concatenate.23.meta_ref
  6.6 0.1 concatenate.24.meta_ref
  6.7 1.2 copy-done.6
  7.9 5.2 %sums.4 = s16[8,272,128]{2,1,0:T(8,128)(2,1)} custom-call(s32[578]{0:T(1024)S(1)} %concatenate.21.meta_ref, s32[32,8,8,128]{3,2,1,0:T(8,128)S(1)} %bitcast.21, s32[32,8,8,128]{3,2,1,0:T(8,128)} %collective-permute-done.1.pat1_ref, bf16[2048,512]{1,0:T(8,128)(2,1)S(1)} %copy-done.1, bf16[2048,256]{1,0:T(8,128)(2,1)} %collective-permute-done.2.feat1_ref), custom_call_target="tpu_custom_call" | custom-call | flops 2000000000 | bytes 3000000 | tf_op jit(solution)/shard_map/sums/pallas_call | solution.py:129
  13.1 2.2 %collective-permute-start.3 = (s16[8,272,128]{2,1,0:T(8,128)(2,1)}, s16[8,272,128]{2,1,0:T(8,128)(2,1)}, u32[]{:S(2)}, u32[]{:S(2)}) collective-permute-start(s16[8,272,128]{2,1,0:T(8,128)(2,1)} %sums.4), channel_id=1, source_target_pairs={{0,8},{1,9},{2,10},{3,11},{4,12},{5,13},{6,14},{7,15},{8,16},{9,17... | collective-permute-start | bytes 1671176 | tf_op jit(solution)/shard_map/ppermute | solution.py:313
  15.3 5.2 %sums.5 = s16[8,272,128]{2,1,0:T(8,128)(2,1)} custom-call(s32[578]{0:T(1024)S(1)} %concatenate.22.meta_ref, s32[32,8,8,128]{3,2,1,0:T(8,128)S(1)} %bitcast.22, s32[32,8,8,128]{3,2,1,0:T(8,128)} %collective-permute-done.1.pat1_ref, bf16[2048,512]{1,0:T(8,128)(2,1)S(1)} %copy-done.1, bf16[2048,256]{1,0:T(8,128)(2,1)} %collective-permute-done.2.feat1_ref), custom_call_target="tpu_custom_call" | custom-call | flops 2000000000 | bytes 3000000 | tf_op jit(solution)/shard_map/sums/pallas_call | solution.py:129
  20.6 0.7 collective-permute-start.4
  21.3 5.2 %sums.6 = s16[8,272,128]{2,1,0:T(8,128)(2,1)} custom-call(s32[578]{0:T(1024)S(1)} %concatenate.23.meta_ref, s32[32,8,8,128]{3,2,1,0:T(8,128)S(1)} %bitcast.23, s32[32,8,8,128]{3,2,1,0:T(8,128)} %collective-permute-done.1.pat1_ref, bf16[2048,512]{1,0:T(8,128)(2,1)S(1)} %copy-done.1, bf16[2048,256]{1,0:T(8,128)(2,1)} %collective-permute-done.2.feat1_ref), custom_call_target="tpu_custom_call" | custom-call | flops 2000000000 | bytes 3000000 | tf_op jit(solution)/shard_map/sums/pallas_call | solution.py:129
  26.5 0.2 collective-permute-start.5
  26.7 4.4 %sums.7.own_ref = f32[8,264,128]{2,1,0:T(8,128)S(1)} custom-call(s32[578]{0:T(1024)S(1)} %concatenate.24.meta_ref, s32[32,8,8,128]{3,2,1,0:T(8,128)S(1)} %bitcast.24, s32[32,8,8,128]{3,2,1,0:T(8,128)} %collective-permute-done.1.pat1_ref, bf16[2048,512]{1,0:T(8,128)(2,1)S(1)} %copy-done.1, bf16[2048,256]{1,0:T(8,128)(2,1)} %collective-permute-done.2.feat1_ref), custom_call_target="tpu_custom_call" | custom-call | flops 2000000000 | bytes 3000000 | tf_op jit(solution)/shard_map/sums/pallas_call | solution.py:129
  31.1 1.0 copy-done.2
  32.1 0.1 copy.16
  32.3 0.1 collective-permute-start.6
  32.4 0.5 collective-permute-start.7
  32.9 0.3 convolution_add_fusion.rest_3_.self_ref
  33.2 0.4 collective-permute-done.6.rest_1_.seed1_ref
  33.6 0.4 collective-permute-done.7.rest_2_.og1_ref
  34.0 5.9 %collective-permute-done.3.r1_ref = s16[8,272,128]{2,1,0:T(8,128)(2,1)} collective-permute-done((s16[8,272,128]{2,1,0:T(8,128)(2,1)}, s16[8,272,128]{2,1,0:T(8,128)(2,1)}, u32[]{:S(2)}, u32[]{:S(2)}) %collective-permute-start.3) | collective-permute-done | bytes 557088 | tf_op jit(solution)/shard_map/ppermute | solution.py:313
  40.0 8.9 %collective-permute-done.5.r3_ref = s16[8,272,128]{2,1,0:T(8,128)(2,1)} collective-permute-done((s16[8,272,128]{2,1,0:T(8,128)(2,1)}, s16[8,272,128]{2,1,0:T(8,128)(2,1)}, u32[]{:S(2)}, u32[]{:S(2)}) %collective-permute-start.5) | collective-permute-done | bytes 557088 | tf_op jit(solution)/shard_map/ppermute | solution.py:313
  48.9 2.1 %merge_x.1 = (f32[2,264,128]{2,1,0:T(8,128)S(1)}, s16[2,272,128]{2,1,0:T(8,128)(2,1)S(1)}, s16[2,272,128]{2,1,0:T(8,128)(2,1)S(1)}, s16[2,272,128]{2,1,0:T(8,128)(2,1)S(1)}) custom-call(s32[4]{0:T(128)S(1)} %pad_add_fusion.1.pos_ref, s16[8,272,128]{2,1,0:T(8,128)(2,1)} %collective-permute-done.3.r1_ref, s16[8,272,128]{2,1,0:T(8,128)(2,1)} %collective-permute-done.4.r2_ref, ...), custom_call_target="tpu_custom_call" | custom-call | tf_op jit(solution)/shard_map/merge_x/pallas_call | solution.py:326
  51.0 1.7 %collective-permute-start.8 = (s16[2,272,128]{2,1,0:T(8,128)(2,1)S(1)}, s16[2,272,128]{2,1,0:T(8,128)(2,1)S(1)}, u32[]{:S(2)}, u32[]{:S(2)}) collective-permute-start(s16[2,272,128]{2,1,0:T(8,128)(2,1)S(1)} %get-tuple-element.39), channel_id=1, source_target_pairs={{0,4},{1,5},{2,6},{3,7},{4,0},{5,1},{6,2},{7,3},{8,12},{9,13},{10,... | collective-permute-start | bytes 417800 | tf_op jit(solution)/shard_map/ppermute | solution.py:329
  52.7 1.9 %collective-permute-start.9 = (s16[2,272,128]{2,1,0:T(8,128)(2,1)S(1)}, s16[2,272,128]{2,1,0:T(8,128)(2,1)S(1)}, u32[]{:S(2)}, u32[]{:S(2)}) collective-permute-start(s16[2,272,128]{2,1,0:T(8,128)(2,1)S(1)} %get-tuple-element.40), channel_id=1, source_target_pairs={{0,2},{1,3},{2,4},{3,5},{4,6},{5,7},{6,0},{7,1},{8,10},{9,11},{10,... | collective-permute-start | bytes 417800 | tf_op jit(solution)/shard_map/ppermute | solution.py:329
  54.6 1.9 %collective-permute-start.10 = (s16[2,272,128]{2,1,0:T(8,128)(2,1)S(1)}, s16[2,272,128]{2,1,0:T(8,128)(2,1)S(1)}, u32[]{:S(2)}, u32[]{:S(2)}) collective-permute-start(s16[2,272,128]{2,1,0:T(8,128)(2,1)S(1)} %get-tuple-element.41), channel_id=1, source_target_pairs={{0,6},{1,7},{2,0},{3,1},{4,2},{5,3},{6,4},{7,5},{8,14},{9,15},{10,... | collective-permute-start | bytes 417800 | tf_op jit(solution)/shard_map/ppermute | solution.py:329
  56.5 7.5 %collective-permute-done.8.r1_ref = s16[2,272,128]{2,1,0:T(8,128)(2,1)S(1)} collective-permute-done((s16[2,272,128]{2,1,0:T(8,128)(2,1)S(1)}, s16[2,272,128]{2,1,0:T(8,128)(2,1)S(1)}, u32[]{:S(2)}, u32[]{:S(2)}) %collective-permute-start.8) | collective-permute-done | bytes 139296 | tf_op jit(solution)/shard_map/ppermute | solution.py:329
  64.0 1.2 collective-permute-done.10.r3_ref
  65.2 0.7 merge_z.1
  65.9 0.1 collective-permute-start.11
  66.0 1.3 %collective-permute-done.11.got_ref = bf16[384,128]{1,0:T(8,128)(2,1)S(1)} collective-permute-done((bf16[384,128]{1,0:T(8,128)(2,1)S(1)}, bf16[384,128]{1,0:T(8,128)(2,1)S(1)}, u32[]{:S(2)}, u32[]{:S(2)}) %collective-permute-start.11) | collective-permute-done | bytes 98336 | tf_op jit(solution)/shard_map/ppermute | solution.py:300
  67.3 1.1 pre_terms.1
  68.4 2.2 %collective-permute-start.12 = (s16[272,128]{1,0:T(8,128)(2,1)S(1)}, s16[272,128]{1,0:T(8,128)(2,1)S(1)}, u32[]{:S(2)}, u32[]{:S(2)}) collective-permute-start(s16[272,128]{1,0:T(8,128)(2,1)S(1)} %get-tuple-element.46), channel_id=1, source_target_pairs={{0,64},{32,96},{64,0},{96,32},{128,192},{160,224},{192,128},{224,1... | collective-permute-start | bytes 208904 | tf_op jit(solution)/shard_map/ppermute | solution.py:339
  70.7 0.7 collective-permute-start.13
  71.4 2.5 %collective-permute-start.14 = (s16[272,128]{1,0:T(8,128)(2,1)S(1)}, s16[272,128]{1,0:T(8,128)(2,1)S(1)}, u32[]{:S(2)}, u32[]{:S(2)}) collective-permute-start(s16[272,128]{1,0:T(8,128)(2,1)S(1)} %get-tuple-element.48), channel_id=1, source_target_pairs={{0,96},{32,0},{64,32},{96,64},{128,224},{160,128},{192,160},{224,1... | collective-permute-start | bytes 208904 | tf_op jit(solution)/shard_map/ppermute | solution.py:339
  73.9 1.1 collective-permute-done.12.r1_ref
  75.0 1.2 collective-permute-done.13.r2_ref
  76.2 0.6 merge_y.1.own_ref
  76.8 5.6 %collective-permute-start.15 = (s16[272,128]{1,0:T(8,128)(2,1)S(1)}, s16[272,128]{1,0:T(8,128)(2,1)S(1)}, u32[]{:S(2)}, u32[]{:S(2)}) collective-permute-start(s16[272,128]{1,0:T(8,128)(2,1)S(1)} %merge_y.1.own_ref), channel_id=1, source_target_pairs={{0,128},{32,160},{64,192},{96,224},{128,0},{160,32},{192,64},{224,... | collective-permute-start | bytes 208904 | tf_op jit(solution)/shard_map/ppermute | solution.py:341
  82.4 2.8 %collective-permute-done.15.far_ref = s16[272,128]{1,0:T(8,128)(2,1)S(1)} collective-permute-done((s16[272,128]{1,0:T(8,128)(2,1)S(1)}, s16[272,128]{1,0:T(8,128)(2,1)S(1)}, u32[]{:S(2)}, u32[]{:S(2)}) %collective-permute-start.15) | collective-permute-done | bytes 69664 | tf_op jit(solution)/shard_map/ppermute | solution.py:341
  85.2 0.6 hidden.1.a0_ref
  85.8 0.2 collective-permute-start.16
  86.1 4.5 %collective-permute-start.17 = (bf16[256,128]{1,0:T(8,128)(2,1)S(1)}, bf16[256,128]{1,0:T(8,128)(2,1)S(1)}, u32[]{:S(2)}, u32[]{:S(2)}) collective-permute-start(bf16[256,128]{1,0:T(8,128)(2,1)S(1)} %hidden.1.a0_ref), channel_id=1, source_target_pairs={{0,64},{32,96},{64,0},{96,32},{128,192},{160,224},{192,128},{224,1... | collective-permute-start | bytes 196616 | tf_op jit(solution)/shard_map/ppermute | solution.py:343
  90.5 0.9 collective-permute-done.16.a1_ref
  91.4 2.1 %collective-permute-done.17.a2_ref = bf16[256,128]{1,0:T(8,128)(2,1)S(1)} collective-permute-done((bf16[256,128]{1,0:T(8,128)(2,1)S(1)}, bf16[256,128]{1,0:T(8,128)(2,1)S(1)}, u32[]{:S(2)}, u32[]{:S(2)}) %collective-permute-start.17) | collective-permute-done | bytes 65568 | tf_op jit(solution)/shard_map/ppermute | solution.py:343
  93.5 1.3 %collective-permute-done.18.a3_ref = bf16[256,128]{1,0:T(8,128)(2,1)S(1)} collective-permute-done((bf16[256,128]{1,0:T(8,128)(2,1)S(1)}, bf16[256,128]{1,0:T(8,128)(2,1)S(1)}, u32[]{:S(2)}, u32[]{:S(2)}) %collective-permute-start.18) | collective-permute-done | bytes 65568 | tf_op jit(solution)/shard_map/ppermute | solution.py:343
  94.8 1.2 collective-permute-done.22.b3_ref
  96.0 1.6 %grads.1 = (bf16[128,1024]{1,0:T(8,128)(2,1)}, f32[128,1152]{1,0:T(8,128)S(1)}, bf16[128,1152]{1,0:T(8,128)(2,1)S(1)}, bf16[128,1152]{1,0:T(8,128)(2,1)S(1)}, bf16[128,1152]{1,0:T(8,128)(2,1)S(1)}) custom-call(s32[4]{0:T(128)S(1)} %pad_add_fusion.1.pos_ref, bf16[256,128]{1,0:T(8,128)(2,1)S(1)} %hidden.1.a0_ref, ...), custom_call_target="tpu_custom_call" | custom-call | tf_op jit(solution)/shard_map/grads/pallas_call | solution.py:354
  97.6 2.4 %collective-permute-start.23 = (bf16[128,1152]{1,0:T(8,128)(2,1)S(1)}, bf16[128,1152]{1,0:T(8,128)(2,1)S(1)}, u32[]{:S(2)}, u32[]{:S(2)}) collective-permute-start(bf16[128,1152]{1,0:T(8,128)(2,1)S(1)} %get-tuple-element.53), channel_id=1, source_target_pairs={{0,16},{1,17},{2,18},{3,19},{4,20},{5,21},{6,22},{7,23},{8,24},{9,... | collective-permute-start | bytes 884744 | tf_op jit(solution)/shard_map/ppermute | solution.py:357
  100.0 0.4 collective-permute-start.24
  100.5 1.6 %collective-permute-start.25 = (bf16[128,1152]{1,0:T(8,128)(2,1)S(1)}, bf16[128,1152]{1,0:T(8,128)(2,1)S(1)}, u32[]{:S(2)}, u32[]{:S(2)}) collective-permute-start(bf16[128,1152]{1,0:T(8,128)(2,1)S(1)} %get-tuple-element.55), channel_id=1, source_target_pairs={{0,24},{1,25},{2,26},{3,27},{4,28},{5,29},{6,30},{7,31},{8,0},{9,1... | collective-permute-start | bytes 884744 | tf_op jit(solution)/shard_map/ppermute | solution.py:357
  102.1 7.0 %collective-permute-done.23.r1_ref = bf16[128,1152]{1,0:T(8,128)(2,1)S(1)} collective-permute-done((bf16[128,1152]{1,0:T(8,128)(2,1)S(1)}, bf16[128,1152]{1,0:T(8,128)(2,1)S(1)}, u32[]{:S(2)}, u32[]{:S(2)}) %collective-permute-start.23) | collective-permute-done | bytes 294944 | tf_op jit(solution)/shard_map/ppermute | solution.py:357
  109.0 2.7 %collective-permute-done.24.r2_ref = bf16[128,1152]{1,0:T(8,128)(2,1)S(1)} collective-permute-done((bf16[128,1152]{1,0:T(8,128)(2,1)S(1)}, bf16[128,1152]{1,0:T(8,128)(2,1)S(1)}, u32[]{:S(2)}, u32[]{:S(2)}) %collective-permute-start.24) | collective-permute-done | bytes 294944 | tf_op jit(solution)/shard_map/ppermute | solution.py:357
  111.7 2.8 %collective-permute-done.25.r3_ref = bf16[128,1152]{1,0:T(8,128)(2,1)S(1)} collective-permute-done((bf16[128,1152]{1,0:T(8,128)(2,1)S(1)}, bf16[128,1152]{1,0:T(8,128)(2,1)S(1)}, u32[]{:S(2)}, u32[]{:S(2)}) %collective-permute-start.25) | collective-permute-done | bytes 294944 | tf_op jit(solution)/shard_map/ppermute | solution.py:357
  114.5 0.8 fold_x.1
  115.3 4.1 %collective-permute-start.26 = (bf16[32,1152]{1,0:T(8,128)(2,1)S(1)}, bf16[32,1152]{1,0:T(8,128)(2,1)S(1)}, u32[]{:S(2)}, u32[]{:S(2)}) collective-permute-start(bf16[32,1152]{1,0:T(8,128)(2,1)S(1)} %get-tuple-element.57), channel_id=1, source_target_pairs={{0,4},{1,5},{2,6},{3,7},{4,0},{5,1},{6,2},{7,3},{8,12},{9,13},{10,... | collective-permute-start | bytes 221192 | tf_op jit(solution)/shard_map/ppermute | solution.py:362
  119.4 3.8 %collective-permute-start.28 = (bf16[32,1152]{1,0:T(8,128)(2,1)S(1)}, bf16[32,1152]{1,0:T(8,128)(2,1)S(1)}, u32[]{:S(2)}, u32[]{:S(2)}) collective-permute-start(bf16[32,1152]{1,0:T(8,128)(2,1)S(1)} %get-tuple-element.59), channel_id=1, source_target_pairs={{0,6},{1,7},{2,0},{3,1},{4,2},{5,3},{6,4},{7,5},{8,14},{9,15},{10,... | collective-permute-start | bytes 221192 | tf_op jit(solution)/shard_map/ppermute | solution.py:362
  123.2 1.6 %collective-permute-done.26.r1_ref = bf16[32,1152]{1,0:T(8,128)(2,1)S(1)} collective-permute-done((bf16[32,1152]{1,0:T(8,128)(2,1)S(1)}, bf16[32,1152]{1,0:T(8,128)(2,1)S(1)}, u32[]{:S(2)}, u32[]{:S(2)}) %collective-permute-start.26) | collective-permute-done | bytes 73760 | tf_op jit(solution)/shard_map/ppermute | solution.py:362
  124.8 1.1 collective-permute-done.27.r2_ref
  126.0 1.2 last.1
  127.2 0.6 fusion
  (45 shorter events, 0.6 us)
Async XLA Ops:
  0.6 32.3 %copy-start = (bf16[512,1024]{1,0:T(8,128)(2,1)S(1)}, bf16[512,1024]{1,0:T(8,128)(2,1)}, u32[]{:S(2)}) copy-start(bf16[512,1024]{1,0:T(8,128)(2,1)} %param.14) | copy-start | bytes 3145732
  0.6 6.0 %copy-start.1 = (bf16[2048,512]{1,0:T(8,128)(2,1)S(1)}, bf16[2048,512]{1,0:T(8,128)(2,1)}, u32[]{:S(2)}) copy-start(bf16[2048,512]{1,0:T(8,128)(2,1)} %feat0_ref.7) | copy-start | bytes 6291460
  0.7 3.3 %copy-start.9 = (s32[32,8]{0,1:T(8,128)S(1)}, s32[32,8]{0,1:T(8,128)}, u32[]{:S(2)}) copy-start(s32[32,8]{0,1:T(8,128)} %param.12) | copy-start | bytes 3076
  0.7 3.5 %copy-start.8 = (s32[32]{0:T(128)S(1)}, s32[32]{0:T(128)}, u32[]{:S(2)}) copy-start(s32[32]{0:T(128)} %param.13) | copy-start | bytes 388
  0.7 6.0 %collective-permute-start.1 = (s32[32,8,8,128]{3,2,1,0:T(8,128)}, s32[32,8,8,128]{3,2,1,0:T(8,128)}, u32[]{:S(2)}, u32[]{:S(2)}) collective-permute-start(s32[32,8,8,128]{3,2,1,0:T(8,128)} %bitcast.20), channel_id=1, source_target_pairs={{0,1},{1,0},{2,3},{3,2},{4,5},{5,4},{6,7},{7,6},{8,9},{9,8},{10,11... | collective-permute-start | bytes 3145736 | tf_op jit(solution)/shard_map/ppermute | solution.py:300
  3.6 3.1 %collective-permute-start.2 = (bf16[2048,256]{1,0:T(8,128)(2,1)}, bf16[2048,256]{1,0:T(8,128)(2,1)}, u32[]{:S(2)}, u32[]{:S(2)}) collective-permute-start(bf16[2048,256]{1,0:T(8,128)(2,1)} %slice_select_fusion), channel_id=1, source_target_pairs={{0,1},{1,0},{2,3},{3,2},{4,5},{5,4},{6,7},{7,6},{8,9},{9,8},{10,11... | collective-permute-start | bytes 3145736 | tf_op jit(solution)/shard_map/ppermute | solution.py:300
  4.2 2.0 %collective-permute-start = (s32[288]{0:T(512)S(1)}, s32[288]{0:T(512)S(1)}, u32[]{:S(2)}, u32[]{:S(2)}) collective-permute-start(s32[288]{0:T(512)S(1)} %pad_add_fusion), channel_id=1, source_target_pairs={{0,1},{1,0},{2,3},{3,2},{4,5},{5,4},{6,7},{7,6},{8,9},{9,8},{10,11... | collective-permute-start | bytes 3464 | tf_op jit(solution)/shard_map/ppermute | solution.py:300
  6.7 1.2 copy-start.6
  13.1 26.9 %collective-permute-start.3 = (s16[8,272,128]{2,1,0:T(8,128)(2,1)}, s16[8,272,128]{2,1,0:T(8,128)(2,1)}, u32[]{:S(2)}, u32[]{:S(2)}) collective-permute-start(s16[8,272,128]{2,1,0:T(8,128)(2,1)} %sums.4), channel_id=1, source_target_pairs={{0,8},{1,9},{2,10},{3,11},{4,12},{5,13},{6,14},{7,15},{8,16},{9,17... | collective-permute-start | bytes 1671176 | tf_op jit(solution)/shard_map/ppermute | solution.py:313
  20.6 19.4 %collective-permute-start.4 = (s16[8,272,128]{2,1,0:T(8,128)(2,1)}, s16[8,272,128]{2,1,0:T(8,128)(2,1)}, u32[]{:S(2)}, u32[]{:S(2)}) collective-permute-start(s16[8,272,128]{2,1,0:T(8,128)(2,1)} %sums.5), channel_id=1, source_target_pairs={{0,16},{1,17},{2,18},{3,19},{4,20},{5,21},{6,22},{7,23},{8,24},{9,... | collective-permute-start | bytes 1671176 | tf_op jit(solution)/shard_map/ppermute | solution.py:313
  26.5 5.6 %copy-start.7 = (bf16[128,512]{1,0:T(8,128)(2,1)S(1)}, bf16[128,512]{1,0:T(8,128)(2,1)}, u32[]{:S(2)}) copy-start(bf16[128,512]{1,0:T(8,128)(2,1)} %param.10) | copy-start | bytes 393220
  26.5 5.9 %copy-start.5 = (bf16[128,1024]{1,0:T(8,128)(2,1)S(1)}, bf16[128,1024]{1,0:T(8,128)(2,1)}, u32[]{:S(2)}) copy-start(bf16[128,1024]{1,0:T(8,128)(2,1)} %og0_ref) | copy-start | bytes 786436
  26.5 6.4 %copy-start.10 = (f32[1024]{0:T(1024)S(1)}, f32[1024]{0:T(1024)}, u32[]{:S(2)}) copy-start(f32[1024]{0:T(1024)} %param.16) | copy-start | bytes 12292
  26.5 22.4 %collective-permute-start.5 = (s16[8,272,128]{2,1,0:T(8,128)(2,1)}, s16[8,272,128]{2,1,0:T(8,128)(2,1)}, u32[]{:S(2)}, u32[]{:S(2)}) collective-permute-start(s16[8,272,128]{2,1,0:T(8,128)(2,1)} %sums.6), channel_id=1, source_target_pairs={{0,24},{1,25},{2,26},{3,27},{4,28},{5,29},{6,30},{7,31},{8,0},{9,1... | collective-permute-start | bytes 1671176 | tf_op jit(solution)/shard_map/ppermute | solution.py:313
  31.1 1.0 copy-start.2
  32.2 16.6 %copy-start.3 = (f32[8,264,128]{2,1,0:T(8,128)S(1)}, f32[8,264,128]{2,1,0:T(8,128)}, u32[]{:S(2)}) copy-start(f32[8,264,128]{2,1,0:T(8,128)} %copy-done.2) | copy-start | bytes 3244036
  32.3 1.3 %collective-permute-start.6 = (bf16[256,128]{1,0:T(8,128)(2,1)S(1)}, bf16[256,128]{1,0:T(8,128)(2,1)S(1)}, u32[]{:S(2)}, u32[]{:S(2)}) collective-permute-start(bf16[256,128]{1,0:T(8,128)(2,1)S(1)} %bitcast.26), channel_id=1, source_target_pairs={{0,1},{1,0},{2,3},{3,2},{4,5},{5,4},{6,7},{7,6},{8,9},{9,8},{10,11... | collective-permute-start | bytes 196616 | tf_op jit(solution)/shard_map/ppermute | solution.py:300
  32.4 1.7 %collective-permute-start.7 = (bf16[128,1024]{1,0:T(8,128)(2,1)S(1)}, bf16[128,1024]{1,0:T(8,128)(2,1)S(1)}, u32[]{:S(2)}, u32[]{:S(2)}) collective-permute-start(bf16[128,1024]{1,0:T(8,128)(2,1)S(1)} %copy-done.5), channel_id=1, source_target_pairs={{0,1},{1,0},{2,3},{3,2},{4,5},{5,4},{6,7},{7,6},{8,9},{9,8},{10,11... | collective-permute-start | bytes 786440 | tf_op jit(solution)/shard_map/ppermute | solution.py:300
  48.9 18.4 %copy-start.4 = (bf16[512,1024]{1,0:T(8,128)(2,1)S(1)}, bf16[512,1024]{1,0:T(8,128)(2,1)}, u32[]{:S(2)}) copy-start(bf16[512,1024]{1,0:T(8,128)(2,1)} %w_ref.1) | copy-start | bytes 3145732
  51.0 13.0 %collective-permute-start.8 = (s16[2,272,128]{2,1,0:T(8,128)(2,1)S(1)}, s16[2,272,128]{2,1,0:T(8,128)(2,1)S(1)}, u32[]{:S(2)}, u32[]{:S(2)}) collective-permute-start(s16[2,272,128]{2,1,0:T(8,128)(2,1)S(1)} %get-tuple-element.39), channel_id=1, source_target_pairs={{0,4},{1,5},{2,6},{3,7},{4,0},{5,1},{6,2},{7,3},{8,12},{9,13},{10,... | collective-permute-start | bytes 417800 | tf_op jit(solution)/shard_map/ppermute | solution.py:329
  52.7 11.3 %collective-permute-start.9 = (s16[2,272,128]{2,1,0:T(8,128)(2,1)S(1)}, s16[2,272,128]{2,1,0:T(8,128)(2,1)S(1)}, u32[]{:S(2)}, u32[]{:S(2)}) collective-permute-start(s16[2,272,128]{2,1,0:T(8,128)(2,1)S(1)} %get-tuple-element.40), channel_id=1, source_target_pairs={{0,2},{1,3},{2,4},{3,5},{4,6},{5,7},{6,0},{7,1},{8,10},{9,11},{10,... | collective-permute-start | bytes 417800 | tf_op jit(solution)/shard_map/ppermute | solution.py:329
  54.6 10.6 %collective-permute-start.10 = (s16[2,272,128]{2,1,0:T(8,128)(2,1)S(1)}, s16[2,272,128]{2,1,0:T(8,128)(2,1)S(1)}, u32[]{:S(2)}, u32[]{:S(2)}) collective-permute-start(s16[2,272,128]{2,1,0:T(8,128)(2,1)S(1)} %get-tuple-element.41), channel_id=1, source_target_pairs={{0,6},{1,7},{2,0},{3,1},{4,2},{5,3},{6,4},{7,5},{8,14},{9,15},{10,... | collective-permute-start | bytes 417800 | tf_op jit(solution)/shard_map/ppermute | solution.py:329
  65.9 1.4 %collective-permute-start.11 = (bf16[384,128]{1,0:T(8,128)(2,1)S(1)}, bf16[384,128]{1,0:T(8,128)(2,1)S(1)}, u32[]{:S(2)}, u32[]{:S(2)}) collective-permute-start(bf16[384,128]{1,0:T(8,128)(2,1)S(1)} %get-tuple-element.44), channel_id=1, source_target_pairs={{0,1},{1,0},{2,3},{3,2},{4,5},{5,4},{6,7},{7,6},{8,9},{9,8},{10,11... | collective-permute-start | bytes 294920 | tf_op jit(solution)/shard_map/ppermute | solution.py:300
  68.4 6.6 %collective-permute-start.12 = (s16[272,128]{1,0:T(8,128)(2,1)S(1)}, s16[272,128]{1,0:T(8,128)(2,1)S(1)}, u32[]{:S(2)}, u32[]{:S(2)}) collective-permute-start(s16[272,128]{1,0:T(8,128)(2,1)S(1)} %get-tuple-element.46), channel_id=1, source_target_pairs={{0,64},{32,96},{64,0},{96,32},{128,192},{160,224},{192,128},{224,1... | collective-permute-start | bytes 208904 | tf_op jit(solution)/shard_map/ppermute | solution.py:339
  70.7 5.5 %collective-permute-start.13 = (s16[272,128]{1,0:T(8,128)(2,1)S(1)}, s16[272,128]{1,0:T(8,128)(2,1)S(1)}, u32[]{:S(2)}, u32[]{:S(2)}) collective-permute-start(s16[272,128]{1,0:T(8,128)(2,1)S(1)} %get-tuple-element.47), channel_id=1, source_target_pairs={{0,32},{32,64},{64,96},{96,0},{128,160},{160,192},{192,224},{224,1... | collective-permute-start | bytes 208904 | tf_op jit(solution)/shard_map/ppermute | solution.py:339
  71.4 4.8 %collective-permute-start.14 = (s16[272,128]{1,0:T(8,128)(2,1)S(1)}, s16[272,128]{1,0:T(8,128)(2,1)S(1)}, u32[]{:S(2)}, u32[]{:S(2)}) collective-permute-start(s16[272,128]{1,0:T(8,128)(2,1)S(1)} %get-tuple-element.48), channel_id=1, source_target_pairs={{0,96},{32,0},{64,32},{96,64},{128,224},{160,128},{192,160},{224,1... | collective-permute-start | bytes 208904 | tf_op jit(solution)/shard_map/ppermute | solution.py:339
  76.8 8.4 %collective-permute-start.15 = (s16[272,128]{1,0:T(8,128)(2,1)S(1)}, s16[272,128]{1,0:T(8,128)(2,1)S(1)}, u32[]{:S(2)}, u32[]{:S(2)}) collective-permute-start(s16[272,128]{1,0:T(8,128)(2,1)S(1)} %merge_y.1.own_ref), channel_id=1, source_target_pairs={{0,128},{32,160},{64,192},{96,224},{128,0},{160,32},{192,64},{224,... | collective-permute-start | bytes 208904 | tf_op jit(solution)/shard_map/ppermute | solution.py:341
  85.8 5.6 %collective-permute-start.16 = (bf16[256,128]{1,0:T(8,128)(2,1)S(1)}, bf16[256,128]{1,0:T(8,128)(2,1)S(1)}, u32[]{:S(2)}, u32[]{:S(2)}) collective-permute-start(bf16[256,128]{1,0:T(8,128)(2,1)S(1)} %hidden.1.a0_ref), channel_id=1, source_target_pairs={{0,32},{32,64},{64,96},{96,0},{128,160},{160,192},{192,224},{224,1... | collective-permute-start | bytes 196616 | tf_op jit(solution)/shard_map/ppermute | solution.py:343
  86.1 7.4 %collective-permute-start.17 = (bf16[256,128]{1,0:T(8,128)(2,1)S(1)}, bf16[256,128]{1,0:T(8,128)(2,1)S(1)}, u32[]{:S(2)}, u32[]{:S(2)}) collective-permute-start(bf16[256,128]{1,0:T(8,128)(2,1)S(1)} %hidden.1.a0_ref), channel_id=1, source_target_pairs={{0,64},{32,96},{64,0},{96,32},{128,192},{160,224},{192,128},{224,1... | collective-permute-start | bytes 196616 | tf_op jit(solution)/shard_map/ppermute | solution.py:343
  90.5 4.3 %collective-permute-start.18 = (bf16[256,128]{1,0:T(8,128)(2,1)S(1)}, bf16[256,128]{1,0:T(8,128)(2,1)S(1)}, u32[]{:S(2)}, u32[]{:S(2)}) collective-permute-start(bf16[256,128]{1,0:T(8,128)(2,1)S(1)} %hidden.1.a0_ref), channel_id=1, source_target_pairs={{0,96},{32,0},{64,32},{96,64},{128,224},{160,128},{192,160},{224,1... | collective-permute-start | bytes 196616 | tf_op jit(solution)/shard_map/ppermute | solution.py:343
  90.5 4.3 %collective-permute-start.19 = (bf16[256,128]{1,0:T(8,128)(2,1)S(1)}, bf16[256,128]{1,0:T(8,128)(2,1)S(1)}, u32[]{:S(2)}, u32[]{:S(2)}) collective-permute-start(bf16[256,128]{1,0:T(8,128)(2,1)S(1)} %hidden.1.a0_ref), channel_id=1, source_target_pairs={{0,1},{1,0},{2,3},{3,2},{4,5},{5,4},{6,7},{7,6},{8,9},{9,8},{10,11... | collective-permute-start | bytes 196616 | tf_op jit(solution)/shard_map/ppermute | solution.py:300
  91.4 3.4 %collective-permute-start.20 = (bf16[256,128]{1,0:T(8,128)(2,1)S(1)}, bf16[256,128]{1,0:T(8,128)(2,1)S(1)}, u32[]{:S(2)}, u32[]{:S(2)}) collective-permute-start(bf16[256,128]{1,0:T(8,128)(2,1)S(1)} %collective-permute-done.16.a1_ref), channel_id=1, source_target_pairs={{0,1},{1,0},{2,3},{3,2},{4,5},{5,4},{6,7},{7,6},{8,9},{9,8},{10,11... | collective-permute-start | bytes 196616 | tf_op jit(solution)/shard_map/ppermute | solution.py:300
  93.5 1.3 %collective-permute-start.21 = (bf16[256,128]{1,0:T(8,128)(2,1)S(1)}, bf16[256,128]{1,0:T(8,128)(2,1)S(1)}, u32[]{:S(2)}, u32[]{:S(2)}) collective-permute-start(bf16[256,128]{1,0:T(8,128)(2,1)S(1)} %collective-permute-done.17.a2_ref), channel_id=1, source_target_pairs={{0,1},{1,0},{2,3},{3,2},{4,5},{5,4},{6,7},{7,6},{8,9},{9,8},{10,11... | collective-permute-start | bytes 196616 | tf_op jit(solution)/shard_map/ppermute | solution.py:300
  94.8 1.3 collective-permute-start.22
  97.6 11.4 %collective-permute-start.23 = (bf16[128,1152]{1,0:T(8,128)(2,1)S(1)}, bf16[128,1152]{1,0:T(8,128)(2,1)S(1)}, u32[]{:S(2)}, u32[]{:S(2)}) collective-permute-start(bf16[128,1152]{1,0:T(8,128)(2,1)S(1)} %get-tuple-element.53), channel_id=1, source_target_pairs={{0,16},{1,17},{2,18},{3,19},{4,20},{5,21},{6,22},{7,23},{8,24},{9,... | collective-permute-start | bytes 884744 | tf_op jit(solution)/shard_map/ppermute | solution.py:357
  100.0 11.7 %collective-permute-start.24 = (bf16[128,1152]{1,0:T(8,128)(2,1)S(1)}, bf16[128,1152]{1,0:T(8,128)(2,1)S(1)}, u32[]{:S(2)}, u32[]{:S(2)}) collective-permute-start(bf16[128,1152]{1,0:T(8,128)(2,1)S(1)} %get-tuple-element.54), channel_id=1, source_target_pairs={{0,8},{1,9},{2,10},{3,11},{4,12},{5,13},{6,14},{7,15},{8,16},{9,17... | collective-permute-start | bytes 884744 | tf_op jit(solution)/shard_map/ppermute | solution.py:357
  100.5 14.1 %collective-permute-start.25 = (bf16[128,1152]{1,0:T(8,128)(2,1)S(1)}, bf16[128,1152]{1,0:T(8,128)(2,1)S(1)}, u32[]{:S(2)}, u32[]{:S(2)}) collective-permute-start(bf16[128,1152]{1,0:T(8,128)(2,1)S(1)} %get-tuple-element.55), channel_id=1, source_target_pairs={{0,24},{1,25},{2,26},{3,27},{4,28},{5,29},{6,30},{7,31},{8,0},{9,1... | collective-permute-start | bytes 884744 | tf_op jit(solution)/shard_map/ppermute | solution.py:357
  115.3 9.5 %collective-permute-start.26 = (bf16[32,1152]{1,0:T(8,128)(2,1)S(1)}, bf16[32,1152]{1,0:T(8,128)(2,1)S(1)}, u32[]{:S(2)}, u32[]{:S(2)}) collective-permute-start(bf16[32,1152]{1,0:T(8,128)(2,1)S(1)} %get-tuple-element.57), channel_id=1, source_target_pairs={{0,4},{1,5},{2,6},{3,7},{4,0},{5,1},{6,2},{7,3},{8,12},{9,13},{10,... | collective-permute-start | bytes 221192 | tf_op jit(solution)/shard_map/ppermute | solution.py:362
  119.4 6.5 %collective-permute-start.27 = (bf16[32,1152]{1,0:T(8,128)(2,1)S(1)}, bf16[32,1152]{1,0:T(8,128)(2,1)S(1)}, u32[]{:S(2)}, u32[]{:S(2)}) collective-permute-start(bf16[32,1152]{1,0:T(8,128)(2,1)S(1)} %get-tuple-element.58), channel_id=1, source_target_pairs={{0,2},{1,3},{2,4},{3,5},{4,6},{5,7},{6,0},{7,1},{8,10},{9,11},{10,... | collective-permute-start | bytes 221192 | tf_op jit(solution)/shard_map/ppermute | solution.py:362
  119.4 6.5 %collective-permute-start.28 = (bf16[32,1152]{1,0:T(8,128)(2,1)S(1)}, bf16[32,1152]{1,0:T(8,128)(2,1)S(1)}, u32[]{:S(2)}, u32[]{:S(2)}) collective-permute-start(bf16[32,1152]{1,0:T(8,128)(2,1)S(1)} %get-tuple-element.59), channel_id=1, source_target_pairs={{0,6},{1,7},{2,0},{3,1},{4,2},{5,3},{6,4},{7,5},{8,14},{9,15},{10,... | collective-permute-start | bytes 221192 | tf_op jit(solution)/shard_map/ppermute | solution.py:362
where the time goes:
time: 129 us; the launch traced here: 128 us
  waiting for transfers between devices  53.2 us (41%)
  starting transfers between devices  38 us (29%)
  Pallas kernels  28.9 us (22%)
  local copies, waits for them, and re-layouts  3.54 us (3%)
  other arithmetic  2.93 us (2%)
    pallas_call x4, Pallas kernels, sums(): pl.pallas_call(functools.partial(sums_kernel, coded_out), out_shape=jax.S...  20.1 us
    ppermute x3, waiting for transfers between devices, body(): far = [lax.ppermute(made[d], 'node', shift_x(d)) for d in (1, 2, 3)]  14.8 us
    ppermute x3, waiting for transfers between devices, body(): lax.ppermute(parts[d - 1], 'node', shift_x(d))  12.5 us
    ppermute x3, waiting for transfers between devices, body(): lax.ppermute(coded[d - 1], 'node', shift_z(d))  8.68 us
    ppermute x3, starting transfers between devices, body(): lax.ppermute(parts[d - 1], 'node', shift_z(d))  7.9 us
    ppermute x1, starting transfers between devices, body(): far = lax.ppermute(coded, 'feat', SWAP_FAR)  5.6 us
    ppermute x3, starting transfers between devices, body(): lax.ppermute(coded[d - 1], 'node', shift_z(d))  5.51 us
    ppermute x3, starting transfers between devices, body(): lax.ppermute(coded[d - 1], 'feat', shift_y(d))  5.48 us
  transfers between devices with their start and end apart: 29, of which 20 were waited for; matrix products, arithmetic and copies ran while one was open for 3% of the time, Pallas kernels for 12%

commit v1 on v0

--- a/solution.py
+++ b/solution.py
@@ -84,7 +84,32 @@
     return sum(pair[0] for pair in pairs), sum(pair[1] for pair in pairs)
 
 
-def sums_kernel(coded_out, meta_ref, pat0_ref, pat1_ref, feat0_ref, feat1_ref, out_ref, *scratch):
+def half_kernel(side_ref, features_ref, out_ref, done):
+    parts = done.shape[0]
+    step = out_ref.shape[0] // parts
+    cols = pl.ds(pl.multiple_of(side_ref[0] * HALF, HALF), HALF)
+    copies = []
+    for part in range(parts):
+        rows = pl.ds(part * step, step)
+        copies.append(pltpu.make_async_copy(features_ref.at[rows, cols], out_ref.at[rows, :], done.at[part]))
+    for copy in copies:
+        copy.start()
+    for copy in copies:
+        copy.wait()
+
+
+def half_columns(side, features):
+    return pl.pallas_call(
+        half_kernel,
+        out_shape=jax.ShapeDtypeStruct((features.shape[0], HALF), features.dtype),
+        in_specs=[SMEM, pl.BlockSpec(memory_space=pl.ANY)],
+        out_specs=pl.BlockSpec(memory_space=pl.ANY),
+        scratch_shapes=[pltpu.SemaphoreType.DMA((4,))],
+        name="half_columns",
+    )(side, features)
+
+
+def sums_kernel(coded_out, meta_ref, pat0_ref, pat1_ref, feat0_ref, feat1_ref, even_ref, odd_ref, *scratch):
     tiles, accs, pops = scratch[0:2], scratch[2:4], scratch[4:7]
     pats, feats = (pat0_ref, pat1_ref), (feat0_ref, feat1_ref)
     blocks = pat0_ref.shape[0]
@@ -111,7 +136,7 @@
 
     def finish(i, acc_ref, pop_ref):
         count = jnp.sum(pop_ref[...], axis=0, keepdims=True).astype(jnp.float32)
-        put(out_ref.at[i], acc_ref[...], count)
+        put((even_ref, odd_ref)[i % 2].at[i // 2], acc_ref[...], count)
 
     for step in range(blocks + 2):
         if step < blocks:
@@ -128,7 +153,7 @@
     rows, kind = (HALF + 16, jnp.int16) if coded_out else (HALF + 8, jnp.float32)
     return pl.pallas_call(
         functools.partial(sums_kernel, coded_out),
-        out_shape=jax.ShapeDtypeStruct((blocks, rows, BLK), kind),
+        out_shape=[jax.ShapeDtypeStruct((NZ, rows, BLK), kind)] * 2,
         grid_spec=pltpu.PrefetchScalarGridSpec(
             num_scalar_prefetch=1,
             grid=(1,),
@@ -138,7 +163,7 @@
                 pl.BlockSpec((feat0.shape[0], HALF), lambda i, m: (0, m[1])),
                 pl.BlockSpec(feat1.shape, lambda i, m: (0, 0)),
             ],
-            out_specs=pl.BlockSpec((blocks, rows, BLK), lambda i, m: (0, 0, 0)),
+            out_specs=[pl.BlockSpec((NZ, rows, BLK), lambda i, m: (0, 0, 0))] * 2,
             scratch_shapes=[pltpu.VMEM((2 * FAN * BLK, BLK), jnp.bfloat16)] * 2
             + [pltpu.VMEM((HALF, BLK), jnp.float32)] * 2
             + [pltpu.VMEM((8, BLK), jnp.int32)] * 3,
@@ -172,11 +197,11 @@
 HALF16 = shaped(HALF, BLK, jnp.bfloat16)
 
 
-def merge_x_kernel(pos_ref, r1_ref, r2_ref, r3_ref, own_ref, *rest):
+def merge_x_kernel(pos_ref, *rest):
     for d, out_ref in enumerate(rest[-4:]):
         for c in range(2):
-            index = lax.rem(pos_ref[1] + d, NZ) * 2 + c
-            total, count = gathered((own_ref.at[index],), [ref.at[index] for ref in (r1_ref, r2_ref, r3_ref)])
+            index = lax.rem(pos_ref[1] + d, NZ)
+            total, count = gathered((rest[6 + c].at[index],), [ref.at[index] for ref in rest[c:6:2]])
             (put_coded if d else put_plain)(out_ref.at[c], total, count)
 
 
@@ -287,7 +312,11 @@
     mark = own_ref[top, marks] + sum(ref[top, marks].astype(jnp.float32) for ref in refs)
     self_ref[...] = total[:16]
     neigh_ref[...] = total[16:]
-    bias_ref[...] = jnp.broadcast_to(mark[0:1] + mark[1:2], (8, BLK))
+    line = mark[0:1] + mark[1:2]
+    for place in range(BLK // 32):
+        @pl.when(lax.rem(pos_ref[1], 2) * 2 + pos_ref[2] == place)
+        def _():
+            bias_ref[...] = line[:, place * 32:place * 32 + 32]
 
 
 def body(features, seed_feats, patterns, sources, counts, w_self, w_neigh, bias_term, out_grad):
@@ -302,7 +331,7 @@
     packed = patterns.transpose(0, 1, 3, 2)
     table = jnp.concatenate([counts, sources.reshape(-1)])
     packed_other, table_other = swap(packed), swap(table)
-    other = swap(jnp.where(core == 0, features[:, HALF:], features[:, :HALF]))
+    other = swap(half_columns((1 - core)[None].astype(jnp.int32), features))
     lists = counts.shape[0]
     table = jnp.concatenate([table[:lists], table_other[:lists], table[lists:], table_other[lists:]])
 
@@ -310,7 +339,7 @@
     for d in (2, 1, 3, 0):
         meta = jnp.concatenate([jnp.stack([(x + d) % NX, core]).astype(jnp.int32), table])
         made[d] = sums(d > 0, meta, packed, packed_other, features, other)
-    far = [lax.ppermute(made[d], "node", shift_x(d)) for d in (1, 2, 3)]
+    far = [lax.ppermute(part, "node", shift_x(d)) for d in (2, 1, 3) for part in made[d]]
 
     seed_feats, w_self, bias_term, out_grad, own = lax.optimization_barrier(
         (seed_feats, w_self, bias_term, out_grad, made[0])
@@ -321,10 +350,9 @@
     og_other = swap(out_grad)
     self_term = jnp.dot(seed_feats, w_self, preferred_element_type=jnp.float32)
     self_term = self_term + jnp.where(feat == 0, bias_term, 0.0)
-    ready = (seed_mine, seed_other, og_other, self_term)
-
-    own, *coded = call(merge_x_kernel, "merge_x", [SUM_PLAIN] + [SUM_CODED] * 3, 4, waits=len(ready))(
-        pos, *far, own, *ready
+
+    own, *coded = call(merge_x_kernel, "merge_x", [SUM_PLAIN] + [SUM_CODED] * 3, 8)(
+        pos, *far, *own
     )
     arrived = [lax.ppermute(coded[d - 1], "node", shift_z(d)) for d in (2, 1, 3)]
     mine, give, rest = call(
@@ -361,11 +389,10 @@
     )(pos, *received, own)
     received = [lax.ppermute(parts[d - 1], "node", shift_z(d)) for d in (2, 1, 3)]
     part = shaped(16, hid, jnp.float32)
-    grad_self, grad_neigh, bias = call(last_kernel, "last", [part, part, shaped(8, BLK, jnp.float32)], 4)(
+    grad_self, grad_neigh, bias = call(last_kernel, "last", [part, part, shaped(1, 32, jnp.float32)], 4)(
         pos, *received, own
     )
-    grad_bias = lax.dynamic_slice(bias[0], (z % 2 * 64 + core * 32,), (32,))
-    return (hidden, grad_self, grad_neigh, grad_bias)
+    return (hidden, grad_self, grad_neigh, bias[0])
 
 
 def solution(mesh):

time: 129 us -> 153 us (1.19)
  Pallas kernels: 28.9 us -> 61.3 us
  waiting for transfers between devices: 53.2 us -> 43.3 us
  starting transfers between devices: 38 us -> 43.4 us
  other arithmetic: 2.93 us -> 0.16 us
    pallas_call x6 -> x7, Pallas kernels: 23.4 us -> 55.9 us  [the longest x1 32.9 us: half_columns(): pl.pallas_call(half_kernel, out_shape=jax.ShapeDtypeStruct((features.shap...]
    ppermute x3 -> x6, waiting for transfers between devices: 14.8 us -> 7.62 us  [body(): lax.ppermute(part, 'node', shift_x(d))]
    ppermute x3 -> x6, starting transfers between devices: 3.08 us -> 7.86 us  [body(): lax.ppermute(part, 'node', shift_x(d))]
    select_n x1 -> x0, other arithmetic: 2.77 us -> none  [body(): other = swap(jnp.where(core == 0, features[:, HALF:], features[:, :HALF]))]
    ppermute x3, waiting for transfers between devices: 8.68 us -> 6 us  [body(): lax.ppermute(coded[d - 1], 'node', shift_z(d))]
  transfers between devices with their start and end apart: 29 -> 32, of which waited for: 20 -> 17; matrix products, arithmetic and copies ran while one was open for 3% -> 1% of each run, Pallas kernels for 12% -> 32%
where the time goes in v1:
time: 153 us
  Pallas kernels  61.3 us (40%)
  starting transfers between devices  43.4 us (28%)
  waiting for transfers between devices  43.3 us (28%)
  local copies, waits for them, and re-layouts  3.17 us (2%)
    pallas_call x1, Pallas kernels, half_columns(): pl.pallas_call(half_kernel, out_shape=jax.ShapeDtypeStruct((features.shap...  32.9 us
    pallas_call x4, Pallas kernels, sums(): pl.pallas_call(functools.partial(sums_kernel, coded_out), out_shape=[jax....  19.8 us
    ppermute x3, waiting for transfers between devices, body(): lax.ppermute(parts[d - 1], 'node', shift_x(d))  14 us
    ppermute x3, starting transfers between devices, body(): lax.ppermute(parts[d - 1], 'node', shift_z(d))  7.95 us
    ppermute x6, starting transfers between devices, body(): lax.ppermute(part, 'node', shift_x(d))  7.86 us
    ppermute x6, waiting for transfers between devices, body(): lax.ppermute(part, 'node', shift_x(d))  7.62 us
    ppermute x3, starting transfers between devices, body(): lax.ppermute(coded[d - 1], 'node', shift_z(d))  6.61 us
    ppermute x3, starting transfers between devices, body(): lax.ppermute(coded[d - 1], 'feat', shift_y(d))  6.41 us
  transfers between devices with their start and end apart: 32, of which 17 were waited for; matrix products, arithmetic and copies ran while one was open for 1% of the time, Pallas kernels for 32%

profile of v1, /device:TPU:6, one launch (start us, length us, event | category | flops | bytes accessed | tf_op | source)
XLA Modules:
  0.0 152.6 jit_solution(16971551719508957544)
XLA Ops:
  0.7 0.1 collective-permute-start.1
  0.8 32.9 %half_columns.1 = bf16[2048,256]{1,0:T(8,128)(2,1)} custom-call(s32[1]{0:T(128)} %bitcast.6.side_ref, bf16[2048,512]{1,0:T(8,128)(2,1)} %feat0_ref.7), custom_call_target="tpu_custom_call" | custom-call | tf_op jit(solution)/shard_map/half_columns/pallas_call | solution.py:102
  33.7 0.6 collective-permute-start.2
  34.3 0.1 reshape.23
  34.4 0.1 pad_add_fusion
  34.7 1.9 %collective-permute-done = s32[288]{0:T(512)S(1)} collective-permute-done((s32[288]{0:T(512)S(1)}, s32[288]{0:T(512)S(1)}, u32[]{:S(2)}, u32[]{:S(2)}) %collective-permute-start) | collective-permute-done | bytes 1184 | tf_op jit(solution)/shard_map/ppermute | solution.py:329
  36.6 0.1 concatenate.21.meta_ref
  36.7 0.1 concatenate.22.meta_ref
  36.8 0.1 concatenate.23.meta_ref
  36.9 1.2 copy-done.4
  38.1 5.1 %sums.4 = (s16[4,272,128]{2,1,0:T(8,128)(2,1)S(1)}, s16[4,272,128]{2,1,0:T(8,128)(2,1)}) custom-call(s32[578]{0:T(1024)S(1)} %concatenate.21.meta_ref, s32[32,8,8,128]{3,2,1,0:T(8,128)S(1)} %bitcast.20, s32[32,8,8,128]{3,2,1,0:T(8,128)} %collective-permute-done.1.pat1_ref, bf16[2048,512]{1,0:T(8,128)(2,1)S(1)} %copy-done.1, ...), custom_call_target="tpu_custom_call" | custom-call | flops 2000000000 | bytes 3000000 | tf_op jit(solution)/shard_map/sums/pallas_call | solution.py:154
  43.3 1.4 collective-permute-start.3
  44.7 2.1 %collective-permute-start.4 = (s16[4,272,128]{2,1,0:T(8,128)(2,1)}, s16[4,272,128]{2,1,0:T(8,128)(2,1)}, u32[]{:S(2)}, u32[]{:S(2)}) collective-permute-start(s16[4,272,128]{2,1,0:T(8,128)(2,1)} %get-tuple-element.44), channel_id=1, source_target_pairs={{0,16},{1,17},{2,18},{3,19},{4,20},{5,21},{6,22},{7,23},{8,24},{9,... | collective-permute-start | bytes 835592 | tf_op jit(solution)/shard_map/ppermute | solution.py:342
  46.8 5.1 %sums.5 = (s16[4,272,128]{2,1,0:T(8,128)(2,1)}, s16[4,272,128]{2,1,0:T(8,128)(2,1)}) custom-call(s32[578]{0:T(1024)S(1)} %concatenate.22.meta_ref, s32[32,8,8,128]{3,2,1,0:T(8,128)S(1)} %bitcast.21, s32[32,8,8,128]{3,2,1,0:T(8,128)} %collective-permute-done.1.pat1_ref, bf16[2048,512]{1,0:T(8,128)(2,1)S(1)} %copy-done.1, ...), custom_call_target="tpu_custom_call" | custom-call | flops 2000000000 | bytes 3000000 | tf_op jit(solution)/shard_map/sums/pallas_call | solution.py:154
  51.9 2.2 %collective-permute-start.5 = (s16[4,272,128]{2,1,0:T(8,128)(2,1)}, s16[4,272,128]{2,1,0:T(8,128)(2,1)}, u32[]{:S(2)}, u32[]{:S(2)}) collective-permute-start(s16[4,272,128]{2,1,0:T(8,128)(2,1)} %get-tuple-element.45), channel_id=1, source_target_pairs={{0,8},{1,9},{2,10},{3,11},{4,12},{5,13},{6,14},{7,15},{8,16},{9,17... | collective-permute-start | bytes 835592 | tf_op jit(solution)/shard_map/ppermute | solution.py:342
  54.2 5.1 %sums.6 = (s16[4,272,128]{2,1,0:T(8,128)(2,1)}, s16[4,272,128]{2,1,0:T(8,128)(2,1)}) custom-call(s32[578]{0:T(1024)S(1)} %concatenate.23.meta_ref, s32[32,8,8,128]{3,2,1,0:T(8,128)S(1)} %bitcast.22, s32[32,8,8,128]{3,2,1,0:T(8,128)} %collective-permute-done.1.pat1_ref, bf16[2048,512]{1,0:T(8,128)(2,1)S(1)} %copy-done.1, ...), custom_call_target="tpu_custom_call" | custom-call | flops 2000000000 | bytes 3000000 | tf_op jit(solution)/shard_map/sums/pallas_call | solution.py:154
  59.3 2.0 %collective-permute-start.7 = (s16[4,272,128]{2,1,0:T(8,128)(2,1)}, s16[4,272,128]{2,1,0:T(8,128)(2,1)}, u32[]{:S(2)}, u32[]{:S(2)}) collective-permute-start(s16[4,272,128]{2,1,0:T(8,128)(2,1)} %get-tuple-element.47), channel_id=1, source_target_pairs={{0,24},{1,25},{2,26},{3,27},{4,28},{5,29},{6,30},{7,31},{8,0},{9,1... | collective-permute-start | bytes 835592 | tf_op jit(solution)/shard_map/ppermute | solution.py:342
  61.3 0.1 collective-permute-start.8
  61.4 0.1 pad_add_fusion.1.pos_ref
  61.5 0.1 concatenate.24.meta_ref
  61.5 1.2 copy-done.5
  62.8 4.4 %sums.7 = (f32[4,264,128]{2,1,0:T(8,128)S(1)}, f32[4,264,128]{2,1,0:T(8,128)S(1)}) custom-call(s32[578]{0:T(1024)S(1)} %concatenate.24.meta_ref, s32[32,8,8,128]{3,2,1,0:T(8,128)S(1)} %bitcast.23, s32[32,8,8,128]{3,2,1,0:T(8,128)} %collective-permute-done.1.pat1_ref, bf16[2048,512]{1,0:T(8,128)(2,1)S(1)} %copy-done.1, ...), custom_call_target="tpu_custom_call" | custom-call | flops 2000000000 | bytes 3000000 | tf_op jit(solution)/shard_map/sums/pallas_call | solution.py:154
  67.3 4.0 %collective-permute-done.6.rest_3_ = s16[4,272,128]{2,1,0:T(8,128)(2,1)} collective-permute-done((s16[4,272,128]{2,1,0:T(8,128)(2,1)}, s16[4,272,128]{2,1,0:T(8,128)(2,1)}, u32[]{:S(2)}, u32[]{:S(2)}) %collective-permute-start.6) | collective-permute-done | bytes 278560 | tf_op jit(solution)/shard_map/ppermute | solution.py:342
  71.3 3.6 %collective-permute-done.8.rest_5_ = s16[4,272,128]{2,1,0:T(8,128)(2,1)} collective-permute-done((s16[4,272,128]{2,1,0:T(8,128)(2,1)}, s16[4,272,128]{2,1,0:T(8,128)(2,1)}, u32[]{:S(2)}, u32[]{:S(2)}) %collective-permute-start.8) | collective-permute-done | bytes 278560 | tf_op jit(solution)/shard_map/ppermute | solution.py:342
  74.9 1.9 %merge_x.1 = (f32[2,264,128]{2,1,0:T(8,128)S(1)}, s16[2,272,128]{2,1,0:T(8,128)(2,1)S(1)}, s16[2,272,128]{2,1,0:T(8,128)(2,1)S(1)}, s16[2,272,128]{2,1,0:T(8,128)(2,1)S(1)}) custom-call(s32[4]{0:T(128)S(1)} %pad_add_fusion.1.pos_ref, s16[4,272,128]{2,1,0:T(8,128)(2,1)S(1)} %collective-permute-done.3.rest_0_, ...), custom_call_target="tpu_custom_call" | custom-call | tf_op jit(solution)/shard_map/merge_x/pallas_call | solution.py:354
  76.8 2.8 %collective-permute-start.9 = (s16[2,272,128]{2,1,0:T(8,128)(2,1)S(1)}, s16[2,272,128]{2,1,0:T(8,128)(2,1)S(1)}, u32[]{:S(2)}, u32[]{:S(2)}) collective-permute-start(s16[2,272,128]{2,1,0:T(8,128)(2,1)S(1)} %get-tuple-element.53), channel_id=1, source_target_pairs={{0,4},{1,5},{2,6},{3,7},{4,0},{5,1},{6,2},{7,3},{8,12},{9,13},{10,... | collective-permute-start | bytes 417800 | tf_op jit(solution)/shard_map/ppermute | solution.py:357
  79.6 1.9 %collective-permute-start.10 = (s16[2,272,128]{2,1,0:T(8,128)(2,1)S(1)}, s16[2,272,128]{2,1,0:T(8,128)(2,1)S(1)}, u32[]{:S(2)}, u32[]{:S(2)}) collective-permute-start(s16[2,272,128]{2,1,0:T(8,128)(2,1)S(1)} %get-tuple-element.54), channel_id=1, source_target_pairs={{0,2},{1,3},{2,4},{3,5},{4,6},{5,7},{6,0},{7,1},{8,10},{9,11},{10,... | collective-permute-start | bytes 417800 | tf_op jit(solution)/shard_map/ppermute | solution.py:357
  81.5 1.9 %collective-permute-start.11 = (s16[2,272,128]{2,1,0:T(8,128)(2,1)S(1)}, s16[2,272,128]{2,1,0:T(8,128)(2,1)S(1)}, u32[]{:S(2)}, u32[]{:S(2)}) collective-permute-start(s16[2,272,128]{2,1,0:T(8,128)(2,1)S(1)} %get-tuple-element.55), channel_id=1, source_target_pairs={{0,6},{1,7},{2,0},{3,1},{4,2},{5,3},{6,4},{7,5},{8,14},{9,15},{10,... | collective-permute-start | bytes 417800 | tf_op jit(solution)/shard_map/ppermute | solution.py:357
  83.4 5.8 %collective-permute-done.9.r1_ref = s16[2,272,128]{2,1,0:T(8,128)(2,1)S(1)} collective-permute-done((s16[2,272,128]{2,1,0:T(8,128)(2,1)S(1)}, s16[2,272,128]{2,1,0:T(8,128)(2,1)S(1)}, u32[]{:S(2)}, u32[]{:S(2)}) %collective-permute-start.9) | collective-permute-done | bytes 139296 | tf_op jit(solution)/shard_map/ppermute | solution.py:357
  89.3 0.2 collective-permute-done.11.r3_ref
  89.4 0.7 merge_z.1
  90.2 0.1 collective-permute-start.12
  90.3 0.3 convolution_add_fusion.self_ref
  90.6 1.0 collective-permute-done.12.got_ref
  91.6 1.1 pre_terms.1
  92.7 3.2 %collective-permute-start.13 = (s16[272,128]{1,0:T(8,128)(2,1)S(1)}, s16[272,128]{1,0:T(8,128)(2,1)S(1)}, u32[]{:S(2)}, u32[]{:S(2)}) collective-permute-start(s16[272,128]{1,0:T(8,128)(2,1)S(1)} %get-tuple-element.63), channel_id=1, source_target_pairs={{0,64},{32,96},{64,0},{96,32},{128,192},{160,224},{192,128},{224,1... | collective-permute-start | bytes 208904 | tf_op jit(solution)/shard_map/ppermute | solution.py:367
  95.9 0.7 collective-permute-start.14
  96.5 2.5 %collective-permute-start.15 = (s16[272,128]{1,0:T(8,128)(2,1)S(1)}, s16[272,128]{1,0:T(8,128)(2,1)S(1)}, u32[]{:S(2)}, u32[]{:S(2)}) collective-permute-start(s16[272,128]{1,0:T(8,128)(2,1)S(1)} %get-tuple-element.65), channel_id=1, source_target_pairs={{0,96},{32,0},{64,32},{96,64},{128,224},{160,128},{192,160},{224,1... | collective-permute-start | bytes 208904 | tf_op jit(solution)/shard_map/ppermute | solution.py:367
  99.1 0.1 copy.16
  99.2 2.1 %collective-permute-done.14.r2_ref = s16[272,128]{1,0:T(8,128)(2,1)S(1)} collective-permute-done((s16[272,128]{1,0:T(8,128)(2,1)S(1)}, s16[272,128]{1,0:T(8,128)(2,1)S(1)}, u32[]{:S(2)}, u32[]{:S(2)}) %collective-permute-start.14) | collective-permute-done | bytes 69664 | tf_op jit(solution)/shard_map/ppermute | solution.py:367
  101.4 0.6 merge_y.1.own_ref
  102.0 5.8 %collective-permute-start.16 = (s16[272,128]{1,0:T(8,128)(2,1)S(1)}, s16[272,128]{1,0:T(8,128)(2,1)S(1)}, u32[]{:S(2)}, u32[]{:S(2)}) collective-permute-start(s16[272,128]{1,0:T(8,128)(2,1)S(1)} %merge_y.1.own_ref), channel_id=1, source_target_pairs={{0,128},{32,160},{64,192},{96,224},{128,0},{160,32},{192,64},{224,... | collective-permute-start | bytes 208904 | tf_op jit(solution)/shard_map/ppermute | solution.py:369
  107.8 0.1 collective-permute-start.25
  107.9 2.5 %collective-permute-done.16.far_ref = s16[272,128]{1,0:T(8,128)(2,1)S(1)} collective-permute-done((s16[272,128]{1,0:T(8,128)(2,1)S(1)}, s16[272,128]{1,0:T(8,128)(2,1)S(1)}, u32[]{:S(2)}, u32[]{:S(2)}) %collective-permute-start.16) | collective-permute-done | bytes 69664 | tf_op jit(solution)/shard_map/ppermute | solution.py:369
  110.4 0.6 hidden.1.a0_ref
  111.0 0.5 collective-permute-start.17
  111.5 4.4 %collective-permute-start.18 = (bf16[256,128]{1,0:T(8,128)(2,1)S(1)}, bf16[256,128]{1,0:T(8,128)(2,1)S(1)}, u32[]{:S(2)}, u32[]{:S(2)}) collective-permute-start(bf16[256,128]{1,0:T(8,128)(2,1)S(1)} %hidden.1.a0_ref), channel_id=1, source_target_pairs={{0,64},{32,96},{64,0},{96,32},{128,192},{160,224},{192,128},{224,1... | collective-permute-start | bytes 196616 | tf_op jit(solution)/shard_map/ppermute | solution.py:371
  115.9 0.9 collective-permute-done.17.a1_ref
  116.8 2.1 %collective-permute-done.18.a2_ref = bf16[256,128]{1,0:T(8,128)(2,1)S(1)} collective-permute-done((bf16[256,128]{1,0:T(8,128)(2,1)S(1)}, bf16[256,128]{1,0:T(8,128)(2,1)S(1)}, u32[]{:S(2)}, u32[]{:S(2)}) %collective-permute-start.18) | collective-permute-done | bytes 65568 | tf_op jit(solution)/shard_map/ppermute | solution.py:371
  118.9 1.3 collective-permute-done.19.a3_ref
  120.2 1.2 collective-permute-done.23.b3_ref
  121.4 1.6 %grads.1 = (bf16[128,1024]{1,0:T(8,128)(2,1)}, f32[128,1152]{1,0:T(8,128)S(1)}, bf16[128,1152]{1,0:T(8,128)(2,1)S(1)}, bf16[128,1152]{1,0:T(8,128)(2,1)S(1)}, bf16[128,1152]{1,0:T(8,128)(2,1)S(1)}) custom-call(s32[4]{0:T(128)S(1)} %pad_add_fusion.1.pos_ref, bf16[256,128]{1,0:T(8,128)(2,1)S(1)} %hidden.1.a0_ref, ...), custom_call_target="tpu_custom_call" | custom-call | tf_op jit(solution)/shard_map/grads/pallas_call | solution.py:382
  123.0 0.9 collective-permute-start.26
  123.9 1.6 %collective-permute-start.27 = (bf16[128,1152]{1,0:T(8,128)(2,1)S(1)}, bf16[128,1152]{1,0:T(8,128)(2,1)S(1)}, u32[]{:S(2)}, u32[]{:S(2)}) collective-permute-start(bf16[128,1152]{1,0:T(8,128)(2,1)S(1)} %get-tuple-element.72), channel_id=1, source_target_pairs={{0,8},{1,9},{2,10},{3,11},{4,12},{5,13},{6,14},{7,15},{8,16},{9,17... | collective-permute-start | bytes 884744 | tf_op jit(solution)/shard_map/ppermute | solution.py:385
  125.6 0.4 collective-permute-start.28
  126.0 8.5 %collective-permute-done.26.r1_ref = bf16[128,1152]{1,0:T(8,128)(2,1)S(1)} collective-permute-done((bf16[128,1152]{1,0:T(8,128)(2,1)S(1)}, bf16[128,1152]{1,0:T(8,128)(2,1)S(1)}, u32[]{:S(2)}, u32[]{:S(2)}) %collective-permute-start.26) | collective-permute-done | bytes 294944 | tf_op jit(solution)/shard_map/ppermute | solution.py:385
  134.4 3.1 %collective-permute-done.27.r2_ref = bf16[128,1152]{1,0:T(8,128)(2,1)S(1)} collective-permute-done((bf16[128,1152]{1,0:T(8,128)(2,1)S(1)}, bf16[128,1152]{1,0:T(8,128)(2,1)S(1)}, u32[]{:S(2)}, u32[]{:S(2)}) %collective-permute-start.27) | collective-permute-done | bytes 294944 | tf_op jit(solution)/shard_map/ppermute | solution.py:385
  137.6 2.4 %collective-permute-done.28.r3_ref = bf16[128,1152]{1,0:T(8,128)(2,1)S(1)} collective-permute-done((bf16[128,1152]{1,0:T(8,128)(2,1)S(1)}, bf16[128,1152]{1,0:T(8,128)(2,1)S(1)}, u32[]{:S(2)}, u32[]{:S(2)}) %collective-permute-start.28) | collective-permute-done | bytes 294944 | tf_op jit(solution)/shard_map/ppermute | solution.py:385
  139.9 0.8 fold_x.1
  140.7 4.1 %collective-permute-start.29 = (bf16[32,1152]{1,0:T(8,128)(2,1)S(1)}, bf16[32,1152]{1,0:T(8,128)(2,1)S(1)}, u32[]{:S(2)}, u32[]{:S(2)}) collective-permute-start(bf16[32,1152]{1,0:T(8,128)(2,1)S(1)} %get-tuple-element.75), channel_id=1, source_target_pairs={{0,4},{1,5},{2,6},{3,7},{4,0},{5,1},{6,2},{7,3},{8,12},{9,13},{10,... | collective-permute-start | bytes 221192 | tf_op jit(solution)/shard_map/ppermute | solution.py:390
  144.8 3.8 %collective-permute-start.31 = (bf16[32,1152]{1,0:T(8,128)(2,1)S(1)}, bf16[32,1152]{1,0:T(8,128)(2,1)S(1)}, u32[]{:S(2)}, u32[]{:S(2)}) collective-permute-start(bf16[32,1152]{1,0:T(8,128)(2,1)S(1)} %get-tuple-element.77), channel_id=1, source_target_pairs={{0,6},{1,7},{2,0},{3,1},{4,2},{5,3},{6,4},{7,5},{8,14},{9,15},{10,... | collective-permute-start | bytes 221192 | tf_op jit(solution)/shard_map/ppermute | solution.py:390
  148.7 1.5 collective-permute-done.29.r1_ref
  150.2 1.2 collective-permute-done.30.r2_ref
  151.4 1.3 last.1
  (49 shorter events, 0.4 us)
Async XLA Ops:
  0.6 89.6 %copy-start = (bf16[512,1024]{1,0:T(8,128)(2,1)S(1)}, bf16[512,1024]{1,0:T(8,128)(2,1)}, u32[]{:S(2)}) copy-start(bf16[512,1024]{1,0:T(8,128)(2,1)} %param.14) | copy-start | bytes 3145732
  0.6 36.3 %copy-start.1 = (bf16[2048,512]{1,0:T(8,128)(2,1)S(1)}, bf16[2048,512]{1,0:T(8,128)(2,1)}, u32[]{:S(2)}) copy-start(bf16[2048,512]{1,0:T(8,128)(2,1)} %feat0_ref.7) | copy-start | bytes 6291460
  0.7 33.6 %copy-start.9 = (s32[32,8]{0,1:T(8,128)S(1)}, s32[32,8]{0,1:T(8,128)}, u32[]{:S(2)}) copy-start(s32[32,8]{0,1:T(8,128)} %param.12) | copy-start | bytes 3076
  0.7 33.8 %copy-start.8 = (s32[32]{0:T(128)S(1)}, s32[32]{0:T(128)}, u32[]{:S(2)}) copy-start(s32[32]{0:T(128)} %param.13) | copy-start | bytes 388
  0.7 36.2 %collective-permute-start.1 = (s32[32,8,8,128]{3,2,1,0:T(8,128)}, s32[32,8,8,128]{3,2,1,0:T(8,128)}, u32[]{:S(2)}, u32[]{:S(2)}) collective-permute-start(s32[32,8,8,128]{3,2,1,0:T(8,128)} %bitcast.19), channel_id=1, source_target_pairs={{0,1},{1,0},{2,3},{3,2},{4,5},{5,4},{6,7},{7,6},{8,9},{9,8},{10,11... | collective-permute-start | bytes 3145736 | tf_op jit(solution)/shard_map/ppermute | solution.py:329
  33.7 3.2 %collective-permute-start.2 = (bf16[2048,256]{1,0:T(8,128)(2,1)}, bf16[2048,256]{1,0:T(8,128)(2,1)}, u32[]{:S(2)}, u32[]{:S(2)}) collective-permute-start(bf16[2048,256]{1,0:T(8,128)(2,1)} %half_columns.1), channel_id=1, source_target_pairs={{0,1},{1,0},{2,3},{3,2},{4,5},{5,4},{6,7},{7,6},{8,9},{9,8},{10,11... | collective-permute-start | bytes 3145736 | tf_op jit(solution)/shard_map/ppermute | solution.py:329
  34.5 2.0 %collective-permute-start = (s32[288]{0:T(512)S(1)}, s32[288]{0:T(512)S(1)}, u32[]{:S(2)}, u32[]{:S(2)}) collective-permute-start(s32[288]{0:T(512)S(1)} %pad_add_fusion), channel_id=1, source_target_pairs={{0,1},{1,0},{2,3},{3,2},{4,5},{5,4},{6,7},{7,6},{8,9},{9,8},{10,11... | collective-permute-start | bytes 3464 | tf_op jit(solution)/shard_map/ppermute | solution.py:329
  36.9 1.2 copy-start.4
  43.3 18.0 %collective-permute-start.3 = (s16[4,272,128]{2,1,0:T(8,128)(2,1)S(1)}, s16[4,272,128]{2,1,0:T(8,128)(2,1)S(1)}, u32[]{:S(2)}, u32[]{:S(2)}) collective-permute-start(s16[4,272,128]{2,1,0:T(8,128)(2,1)S(1)} %get-tuple-element.43), channel_id=1, source_target_pairs={{0,16},{1,17},{2,18},{3,19},{4,20},{5,21},{6,22},{7,23},{8,24},{9,... | collective-permute-start | bytes 835592 | tf_op jit(solution)/shard_map/ppermute | solution.py:342
  44.7 22.6 %collective-permute-start.4 = (s16[4,272,128]{2,1,0:T(8,128)(2,1)}, s16[4,272,128]{2,1,0:T(8,128)(2,1)}, u32[]{:S(2)}, u32[]{:S(2)}) collective-permute-start(s16[4,272,128]{2,1,0:T(8,128)(2,1)} %get-tuple-element.44), channel_id=1, source_target_pairs={{0,16},{1,17},{2,18},{3,19},{4,20},{5,21},{6,22},{7,23},{8,24},{9,... | collective-permute-start | bytes 835592 | tf_op jit(solution)/shard_map/ppermute | solution.py:342
  51.9 15.3 %collective-permute-start.5 = (s16[4,272,128]{2,1,0:T(8,128)(2,1)}, s16[4,272,128]{2,1,0:T(8,128)(2,1)}, u32[]{:S(2)}, u32[]{:S(2)}) collective-permute-start(s16[4,272,128]{2,1,0:T(8,128)(2,1)} %get-tuple-element.45), channel_id=1, source_target_pairs={{0,8},{1,9},{2,10},{3,11},{4,12},{5,13},{6,14},{7,15},{8,16},{9,17... | collective-permute-start | bytes 835592 | tf_op jit(solution)/shard_map/ppermute | solution.py:342
  54.1 17.1 %collective-permute-start.6 = (s16[4,272,128]{2,1,0:T(8,128)(2,1)}, s16[4,272,128]{2,1,0:T(8,128)(2,1)}, u32[]{:S(2)}, u32[]{:S(2)}) collective-permute-start(s16[4,272,128]{2,1,0:T(8,128)(2,1)} %get-tuple-element.46), channel_id=1, source_target_pairs={{0,8},{1,9},{2,10},{3,11},{4,12},{5,13},{6,14},{7,15},{8,16},{9,17... | collective-permute-start | bytes 835592 | tf_op jit(solution)/shard_map/ppermute | solution.py:342
  59.3 12.0 %collective-permute-start.7 = (s16[4,272,128]{2,1,0:T(8,128)(2,1)}, s16[4,272,128]{2,1,0:T(8,128)(2,1)}, u32[]{:S(2)}, u32[]{:S(2)}) collective-permute-start(s16[4,272,128]{2,1,0:T(8,128)(2,1)} %get-tuple-element.47), channel_id=1, source_target_pairs={{0,24},{1,25},{2,26},{3,27},{4,28},{5,29},{6,30},{7,31},{8,0},{9,1... | collective-permute-start | bytes 835592 | tf_op jit(solution)/shard_map/ppermute | solution.py:342
  61.3 13.6 %collective-permute-start.8 = (s16[4,272,128]{2,1,0:T(8,128)(2,1)}, s16[4,272,128]{2,1,0:T(8,128)(2,1)}, u32[]{:S(2)}, u32[]{:S(2)}) collective-permute-start(s16[4,272,128]{2,1,0:T(8,128)(2,1)} %get-tuple-element.48), channel_id=1, source_target_pairs={{0,24},{1,25},{2,26},{3,27},{4,28},{5,29},{6,30},{7,31},{8,0},{9,1... | collective-permute-start | bytes 835592 | tf_op jit(solution)/shard_map/ppermute | solution.py:342
  61.5 1.2 copy-start.5
  67.2 16.2 %copy-start.10 = (f32[1024]{0:T(1024)S(1)}, f32[1024]{0:T(1024)}, u32[]{:S(2)}) copy-start(f32[1024]{0:T(1024)} %param.16) | copy-start | bytes 12292
  67.2 23.0 %copy-start.6 = (bf16[128,512]{1,0:T(8,128)(2,1)S(1)}, bf16[128,512]{1,0:T(8,128)(2,1)}, u32[]{:S(2)}) copy-start(bf16[128,512]{1,0:T(8,128)(2,1)} %param.10) | copy-start | bytes 393220
  67.2 24.3 %copy-start.2 = (bf16[512,1024]{1,0:T(8,128)(2,1)S(1)}, bf16[512,1024]{1,0:T(8,128)(2,1)}, u32[]{:S(2)}) copy-start(bf16[512,1024]{1,0:T(8,128)(2,1)} %w_ref.1) | copy-start | bytes 3145732
  76.8 22.3 %copy-start.3 = (bf16[128,1024]{1,0:T(8,128)(2,1)S(1)}, bf16[128,1024]{1,0:T(8,128)(2,1)}, u32[]{:S(2)}) copy-start(bf16[128,1024]{1,0:T(8,128)(2,1)} %og0_ref) | copy-start | bytes 786436
  76.8 12.4 %collective-permute-start.9 = (s16[2,272,128]{2,1,0:T(8,128)(2,1)S(1)}, s16[2,272,128]{2,1,0:T(8,128)(2,1)S(1)}, u32[]{:S(2)}, u32[]{:S(2)}) collective-permute-start(s16[2,272,128]{2,1,0:T(8,128)(2,1)S(1)} %get-tuple-element.53), channel_id=1, source_target_pairs={{0,4},{1,5},{2,6},{3,7},{4,0},{5,1},{6,2},{7,3},{8,12},{9,13},{10,... | collective-permute-start | bytes 417800 | tf_op jit(solution)/shard_map/ppermute | solution.py:357
  79.6 9.7 %collective-permute-start.10 = (s16[2,272,128]{2,1,0:T(8,128)(2,1)S(1)}, s16[2,272,128]{2,1,0:T(8,128)(2,1)S(1)}, u32[]{:S(2)}, u32[]{:S(2)}) collective-permute-start(s16[2,272,128]{2,1,0:T(8,128)(2,1)S(1)} %get-tuple-element.54), channel_id=1, source_target_pairs={{0,2},{1,3},{2,4},{3,5},{4,6},{5,7},{6,0},{7,1},{8,10},{9,11},{10,... | collective-permute-start | bytes 417800 | tf_op jit(solution)/shard_map/ppermute | solution.py:357
  81.5 7.9 %collective-permute-start.11 = (s16[2,272,128]{2,1,0:T(8,128)(2,1)S(1)}, s16[2,272,128]{2,1,0:T(8,128)(2,1)S(1)}, u32[]{:S(2)}, u32[]{:S(2)}) collective-permute-start(s16[2,272,128]{2,1,0:T(8,128)(2,1)S(1)} %get-tuple-element.55), channel_id=1, source_target_pairs={{0,6},{1,7},{2,0},{3,1},{4,2},{5,3},{6,4},{7,5},{8,14},{9,15},{10,... | collective-permute-start | bytes 417800 | tf_op jit(solution)/shard_map/ppermute | solution.py:357
  83.4 15.7 %copy-start.7 = (bf16[128,512]{1,0:T(8,128)(2,1)S(1)}, bf16[128,512]{1,0:T(8,128)(2,1)}, u32[]{:S(2)}) copy-start(bf16[128,512]{1,0:T(8,128)(2,1)} %param.10) | copy-start | bytes 393220
  90.2 1.4 collective-permute-start.12
  92.7 6.5 %collective-permute-start.13 = (s16[272,128]{1,0:T(8,128)(2,1)S(1)}, s16[272,128]{1,0:T(8,128)(2,1)S(1)}, u32[]{:S(2)}, u32[]{:S(2)}) collective-permute-start(s16[272,128]{1,0:T(8,128)(2,1)S(1)} %get-tuple-element.63), channel_id=1, source_target_pairs={{0,64},{32,96},{64,0},{96,32},{128,192},{160,224},{192,128},{224,1... | collective-permute-start | bytes 208904 | tf_op jit(solution)/shard_map/ppermute | solution.py:367
  95.9 5.5 %collective-permute-start.14 = (s16[272,128]{1,0:T(8,128)(2,1)S(1)}, s16[272,128]{1,0:T(8,128)(2,1)S(1)}, u32[]{:S(2)}, u32[]{:S(2)}) collective-permute-start(s16[272,128]{1,0:T(8,128)(2,1)S(1)} %get-tuple-element.64), channel_id=1, source_target_pairs={{0,32},{32,64},{64,96},{96,0},{128,160},{160,192},{192,224},{224,1... | collective-permute-start | bytes 208904 | tf_op jit(solution)/shard_map/ppermute | solution.py:367
  96.5 4.8 %collective-permute-start.15 = (s16[272,128]{1,0:T(8,128)(2,1)S(1)}, s16[272,128]{1,0:T(8,128)(2,1)S(1)}, u32[]{:S(2)}, u32[]{:S(2)}) collective-permute-start(s16[272,128]{1,0:T(8,128)(2,1)S(1)} %get-tuple-element.65), channel_id=1, source_target_pairs={{0,96},{32,0},{64,32},{96,64},{128,224},{160,128},{192,160},{224,1... | collective-permute-start | bytes 208904 | tf_op jit(solution)/shard_map/ppermute | solution.py:367
  99.1 21.1 %collective-permute-start.24 = (bf16[128,1024]{1,0:T(8,128)(2,1)S(1)}, bf16[128,1024]{1,0:T(8,128)(2,1)S(1)}, u32[]{:S(2)}, u32[]{:S(2)}) collective-permute-start(bf16[128,1024]{1,0:T(8,128)(2,1)S(1)} %copy-done.3), channel_id=1, source_target_pairs={{0,1},{1,0},{2,3},{3,2},{4,5},{5,4},{6,7},{7,6},{8,9},{9,8},{10,11... | collective-permute-start | bytes 786440 | tf_op jit(solution)/shard_map/ppermute | solution.py:329
  102.0 8.4 %collective-permute-start.16 = (s16[272,128]{1,0:T(8,128)(2,1)S(1)}, s16[272,128]{1,0:T(8,128)(2,1)S(1)}, u32[]{:S(2)}, u32[]{:S(2)}) collective-permute-start(s16[272,128]{1,0:T(8,128)(2,1)S(1)} %merge_y.1.own_ref), channel_id=1, source_target_pairs={{0,128},{32,160},{64,192},{96,224},{128,0},{160,32},{192,64},{224,... | collective-permute-start | bytes 208904 | tf_op jit(solution)/shard_map/ppermute | solution.py:369
  107.8 8.1 %collective-permute-start.25 = (bf16[256,128]{1,0:T(8,128)(2,1)S(1)}, bf16[256,128]{1,0:T(8,128)(2,1)S(1)}, u32[]{:S(2)}, u32[]{:S(2)}) collective-permute-start(bf16[256,128]{1,0:T(8,128)(2,1)S(1)} %bitcast.25), channel_id=1, source_target_pairs={{0,1},{1,0},{2,3},{3,2},{4,5},{5,4},{6,7},{7,6},{8,9},{9,8},{10,11... | collective-permute-start | bytes 196616 | tf_op jit(solution)/shard_map/ppermute | solution.py:329
  111.0 5.8 %collective-permute-start.17 = (bf16[256,128]{1,0:T(8,128)(2,1)S(1)}, bf16[256,128]{1,0:T(8,128)(2,1)S(1)}, u32[]{:S(2)}, u32[]{:S(2)}) collective-permute-start(bf16[256,128]{1,0:T(8,128)(2,1)S(1)} %hidden.1.a0_ref), channel_id=1, source_target_pairs={{0,32},{32,64},{64,96},{96,0},{128,160},{160,192},{192,224},{224,1... | collective-permute-start | bytes 196616 | tf_op jit(solution)/shard_map/ppermute | solution.py:371
  111.5 7.4 %collective-permute-start.18 = (bf16[256,128]{1,0:T(8,128)(2,1)S(1)}, bf16[256,128]{1,0:T(8,128)(2,1)S(1)}, u32[]{:S(2)}, u32[]{:S(2)}) collective-permute-start(bf16[256,128]{1,0:T(8,128)(2,1)S(1)} %hidden.1.a0_ref), channel_id=1, source_target_pairs={{0,64},{32,96},{64,0},{96,32},{128,192},{160,224},{192,128},{224,1... | collective-permute-start | bytes 196616 | tf_op jit(solution)/shard_map/ppermute | solution.py:371
  115.9 4.3 %collective-permute-start.19 = (bf16[256,128]{1,0:T(8,128)(2,1)S(1)}, bf16[256,128]{1,0:T(8,128)(2,1)S(1)}, u32[]{:S(2)}, u32[]{:S(2)}) collective-permute-start(bf16[256,128]{1,0:T(8,128)(2,1)S(1)} %hidden.1.a0_ref), channel_id=1, source_target_pairs={{0,96},{32,0},{64,32},{96,64},{128,224},{160,128},{192,160},{224,1... | collective-permute-start | bytes 196616 | tf_op jit(solution)/shard_map/ppermute | solution.py:371
  115.9 4.3 %collective-permute-start.20 = (bf16[256,128]{1,0:T(8,128)(2,1)S(1)}, bf16[256,128]{1,0:T(8,128)(2,1)S(1)}, u32[]{:S(2)}, u32[]{:S(2)}) collective-permute-start(bf16[256,128]{1,0:T(8,128)(2,1)S(1)} %hidden.1.a0_ref), channel_id=1, source_target_pairs={{0,1},{1,0},{2,3},{3,2},{4,5},{5,4},{6,7},{7,6},{8,9},{9,8},{10,11... | collective-permute-start | bytes 196616 | tf_op jit(solution)/shard_map/ppermute | solution.py:329
  116.8 3.4 %collective-permute-start.21 = (bf16[256,128]{1,0:T(8,128)(2,1)S(1)}, bf16[256,128]{1,0:T(8,128)(2,1)S(1)}, u32[]{:S(2)}, u32[]{:S(2)}) collective-permute-start(bf16[256,128]{1,0:T(8,128)(2,1)S(1)} %collective-permute-done.17.a1_ref), channel_id=1, source_target_pairs={{0,1},{1,0},{2,3},{3,2},{4,5},{5,4},{6,7},{7,6},{8,9},{9,8},{10,11... | collective-permute-start | bytes 196616 | tf_op jit(solution)/shard_map/ppermute | solution.py:329
  118.9 1.4 collective-permute-start.22
  120.2 1.3 collective-permute-start.23
  123.0 11.4 %collective-permute-start.26 = (bf16[128,1152]{1,0:T(8,128)(2,1)S(1)}, bf16[128,1152]{1,0:T(8,128)(2,1)S(1)}, u32[]{:S(2)}, u32[]{:S(2)}) collective-permute-start(bf16[128,1152]{1,0:T(8,128)(2,1)S(1)} %get-tuple-element.71), channel_id=1, source_target_pairs={{0,16},{1,17},{2,18},{3,19},{4,20},{5,21},{6,22},{7,23},{8,24},{9,... | collective-permute-start | bytes 884744 | tf_op jit(solution)/shard_map/ppermute | solution.py:385
  123.9 13.6 %collective-permute-start.27 = (bf16[128,1152]{1,0:T(8,128)(2,1)S(1)}, bf16[128,1152]{1,0:T(8,128)(2,1)S(1)}, u32[]{:S(2)}, u32[]{:S(2)}) collective-permute-start(bf16[128,1152]{1,0:T(8,128)(2,1)S(1)} %get-tuple-element.72), channel_id=1, source_target_pairs={{0,8},{1,9},{2,10},{3,11},{4,12},{5,13},{6,14},{7,15},{8,16},{9,17... | collective-permute-start | bytes 884744 | tf_op jit(solution)/shard_map/ppermute | solution.py:385
  125.6 14.3 %collective-permute-start.28 = (bf16[128,1152]{1,0:T(8,128)(2,1)S(1)}, bf16[128,1152]{1,0:T(8,128)(2,1)S(1)}, u32[]{:S(2)}, u32[]{:S(2)}) collective-permute-start(bf16[128,1152]{1,0:T(8,128)(2,1)S(1)} %get-tuple-element.73), channel_id=1, source_target_pairs={{0,24},{1,25},{2,26},{3,27},{4,28},{5,29},{6,30},{7,31},{8,0},{9,1... | collective-permute-start | bytes 884744 | tf_op jit(solution)/shard_map/ppermute | solution.py:385
  140.7 9.5 %collective-permute-start.29 = (bf16[32,1152]{1,0:T(8,128)(2,1)S(1)}, bf16[32,1152]{1,0:T(8,128)(2,1)S(1)}, u32[]{:S(2)}, u32[]{:S(2)}) collective-permute-start(bf16[32,1152]{1,0:T(8,128)(2,1)S(1)} %get-tuple-element.75), channel_id=1, source_target_pairs={{0,4},{1,5},{2,6},{3,7},{4,0},{5,1},{6,2},{7,3},{8,12},{9,13},{10,... | collective-permute-start | bytes 221192 | tf_op jit(solution)/shard_map/ppermute | solution.py:390
  144.8 6.5 %collective-permute-start.30 = (bf16[32,1152]{1,0:T(8,128)(2,1)S(1)}, bf16[32,1152]{1,0:T(8,128)(2,1)S(1)}, u32[]{:S(2)}, u32[]{:S(2)}) collective-permute-start(bf16[32,1152]{1,0:T(8,128)(2,1)S(1)} %get-tuple-element.76), channel_id=1, source_target_pairs={{0,2},{1,3},{2,4},{3,5},{4,6},{5,7},{6,0},{7,1},{8,10},{9,11},{10,... | collective-permute-start | bytes 221192 | tf_op jit(solution)/shard_map/ppermute | solution.py:390
  144.8 6.5 %collective-permute-start.31 = (bf16[32,1152]{1,0:T(8,128)(2,1)S(1)}, bf16[32,1152]{1,0:T(8,128)(2,1)S(1)}, u32[]{:S(2)}, u32[]{:S(2)}) collective-permute-start(bf16[32,1152]{1,0:T(8,128)(2,1)S(1)} %get-tuple-element.77), channel_id=1, source_target_pairs={{0,6},{1,7},{2,0},{3,1},{4,2},{5,3},{6,4},{7,5},{8,14},{9,15},{10,... | collective-permute-start | bytes 221192 | tf_op jit(solution)/shard_map/ppermute | solution.py:390

commit v2 on v1

--- a/solution.py
+++ b/solution.py
@@ -16,6 +16,7 @@
 VMEM = pl.BlockSpec(memory_space=pltpu.VMEM)
 SMEM = pl.BlockSpec(memory_space=pltpu.SMEM)
 PARAMS = pltpu.CompilerParams(vmem_limit_bytes=40 * 1024 * 1024)
+ALONE = pltpu.CompilerParams(vmem_limit_bytes=63 * 1024 * 1024)
 F32 = functools.partial(lax.dot_general, preferred_element_type=jnp.float32)
 
 
@@ -84,43 +85,61 @@
     return sum(pair[0] for pair in pairs), sum(pair[1] for pair in pairs)
 
 
-def half_kernel(side_ref, features_ref, out_ref, done):
-    parts = done.shape[0]
-    step = out_ref.shape[0] // parts
+def half_kernel(side_ref, features_ref, out_ref, held, came, went):
+    parts = came.shape[0]
+    step = held.shape[0] // parts
     cols = pl.ds(pl.multiple_of(side_ref[0] * HALF, HALF), HALF)
-    copies = []
+    take, give = [], []
     for part in range(parts):
         rows = pl.ds(part * step, step)
-        copies.append(pltpu.make_async_copy(features_ref.at[rows, cols], out_ref.at[rows, :], done.at[part]))
+        take.append(pltpu.make_async_copy(features_ref.at[rows, cols], held.at[rows, :], came.at[part]))
+        give.append(pltpu.make_async_copy(held.at[rows, :], out_ref.at[rows, :], went.at[part]))
+    for copy in take:
+        copy.start()
+    for part in range(parts):
+        take[part].wait()
+        give[part].start()
+    for copy in give:
+        copy.wait()
+
+
+def half_columns(side, features):
+    nodes = features.shape[0]
+    return pl.pallas_call(
+        half_kernel,
+        out_shape=jax.ShapeDtypeStruct((nodes, HALF), features.dtype),
+        in_specs=[SMEM, pl.BlockSpec(memory_space=pl.ANY)],
+        out_specs=pl.BlockSpec(memory_space=pl.ANY),
+        scratch_shapes=[pltpu.VMEM((nodes, HALF), features.dtype)] + [pltpu.SemaphoreType.DMA((8,))] * 2,
+        compiler_params=ALONE,
+        name="half_columns",
+    )(side, features)
+
+
+def sums_kernel(d, pos_ref, table_ref, pat0_ref, pat1_ref, feat0_ref, feat1_ref, even_ref, odd_ref, *scratch):
+    tiles, accs, pops, pats, feats, done = scratch[0:2], scratch[2:4], scratch[4:7], scratch[7:9], scratch[9:11], scratch[11]
+    blocks = pats[0].shape[0]
+    first = lax.rem(pos_ref[0] + d, NX) * blocks
+    group = pl.ds(first, blocks)
+    half = pl.ds(pl.multiple_of(pos_ref[2] * HALF, HALF), HALF)
+    copies = [
+        pltpu.make_async_copy(pat0_ref.at[group], pats[0], done.at[0]),
+        pltpu.make_async_copy(pat1_ref.at[group], pats[1], done.at[1]),
+        pltpu.make_async_copy(feat0_ref.at[:, half], feats[0], done.at[2]),
+        pltpu.make_async_copy(feat1_ref, feats[1], done.at[3]),
+    ]
     for copy in copies:
         copy.start()
-    for copy in copies:
-        copy.wait()
-
-
-def half_columns(side, features):
-    return pl.pallas_call(
-        half_kernel,
-        out_shape=jax.ShapeDtypeStruct((features.shape[0], HALF), features.dtype),
-        in_specs=[SMEM, pl.BlockSpec(memory_space=pl.ANY)],
-        out_specs=pl.BlockSpec(memory_space=pl.ANY),
-        scratch_shapes=[pltpu.SemaphoreType.DMA((4,))],
-        name="half_columns",
-    )(side, features)
-
-
-def sums_kernel(coded_out, meta_ref, pat0_ref, pat1_ref, feat0_ref, feat1_ref, even_ref, odd_ref, *scratch):
-    tiles, accs, pops = scratch[0:2], scratch[2:4], scratch[4:7]
-    pats, feats = (pat0_ref, pat1_ref), (feat0_ref, feat1_ref)
-    blocks = pat0_ref.shape[0]
+    copies[0].wait()
+    copies[1].wait()
     slots = [(side, slot) for side in range(2) for slot in range(FAN)]
-    put = put_coded if coded_out else put_plain
+    put = put_coded if d else put_plain
 
     def unpack(i, tile_ref, pop_ref):
         shifts = lax.broadcasted_iota(jnp.int32, (8, 16, BLK), 1)
         total = jnp.zeros((8, BLK), jnp.int32)
         for j, (side, slot) in enumerate(slots):
-            live = meta_ref[2 + side * 32 + meta_ref[0] * blocks + i]
+            live = table_ref[side * 32 + first + i]
             words = pats[side][i, slot] * (slot < live).astype(jnp.int32)
             total += lax.population_count(words)
             bits = (jnp.broadcast_to(words[:, None, :], (8, 16, BLK)) >> shifts) & 1
@@ -130,7 +149,7 @@
     def multiply(i, tile_ref, acc_ref):
         picked = []
         for side, slot in slots:
-            source = meta_ref[66 + (side * 32 + meta_ref[0] * blocks + i) * FAN + slot]
+            source = table_ref[64 + (side * 32 + first + i) * FAN + slot]
             picked.append(feats[side][pl.ds(pl.multiple_of(source * BLK, BLK), BLK), :])
         acc_ref[...] = F32(tile_ref[...], jnp.concatenate(picked, axis=0), (((0,), (0,)), ((), ()))).T
 
@@ -141,47 +160,44 @@
     for step in range(blocks + 2):
         if step < blocks:
             unpack(step, tiles[step % 2], pops[step % 3])
+        if step == 0:
+            copies[2].wait()
+            copies[3].wait()
         if 0 <= step - 1 < blocks:
             multiply(step - 1, tiles[(step - 1) % 2], accs[(step - 1) % 2])
         if 0 <= step - 2 < blocks:
             finish(step - 2, accs[(step - 2) % 2], pops[(step - 2) % 3])
 
 
-def sums(coded_out, meta, pat0, pat1, feat0, feat1):
+def sums(d, pos, table, pat0, pat1, feat0, feat1):
     blocks = 2 * NZ
-    pats = pl.BlockSpec((blocks, FAN, 8, BLK), lambda i, m: (m[0], 0, 0, 0))
-    rows, kind = (HALF + 16, jnp.int16) if coded_out else (HALF + 8, jnp.float32)
+    rows, kind = (HALF + 16, jnp.int16) if d else (HALF + 8, jnp.float32)
+    nodes = feat0.shape[0]
     return pl.pallas_call(
-        functools.partial(sums_kernel, coded_out),
+        functools.partial(sums_kernel, d),
         out_shape=[jax.ShapeDtypeStruct((NZ, rows, BLK), kind)] * 2,
-        grid_spec=pltpu.PrefetchScalarGridSpec(
-            num_scalar_prefetch=1,
-            grid=(1,),
-            in_specs=[
-                pats,
-                pats,
-                pl.BlockSpec((feat0.shape[0], HALF), lambda i, m: (0, m[1])),
-                pl.BlockSpec(feat1.shape, lambda i, m: (0, 0)),
-            ],
-            out_specs=[pl.BlockSpec((NZ, rows, BLK), lambda i, m: (0, 0, 0))] * 2,
-            scratch_shapes=[pltpu.VMEM((2 * FAN * BLK, BLK), jnp.bfloat16)] * 2
-            + [pltpu.VMEM((HALF, BLK), jnp.float32)] * 2
-            + [pltpu.VMEM((8, BLK), jnp.int32)] * 3,
-        ),
-        compiler_params=PARAMS,
+        in_specs=[SMEM] * 2 + [pl.BlockSpec(memory_space=pl.ANY)] * 4,
+        out_specs=[VMEM] * 2,
+        scratch_shapes=[pltpu.VMEM((2 * FAN * BLK, BLK), jnp.bfloat16)] * 2
+        + [pltpu.VMEM((HALF, BLK), jnp.float32)] * 2
+        + [pltpu.VMEM((8, BLK), jnp.int32)] * 3
+        + [pltpu.VMEM((blocks,) + pat0.shape[1:], jnp.int32)] * 2
+        + [pltpu.VMEM((nodes, HALF), jnp.bfloat16)] * 2
+        + [pltpu.SemaphoreType.DMA((4,))],
+        compiler_params=ALONE,
         cost_estimate=pl.CostEstimate(flops=2_000_000_000, bytes_accessed=3_000_000, transcendentals=0),
         name="sums",
-    )(meta, pat0, pat1, feat0, feat1)
-
-
-def call(kernel, name, outs, count, scratch=(), waits=0):
+    )(pos, table, pat0, pat1, feat0, feat1)
+
+
+def call(kernel, name, outs, count, scratch=(), waits=0, params=PARAMS):
     return pl.pallas_call(
         kernel,
         out_shape=outs,
         in_specs=[SMEM] + [VMEM] * count + [pl.BlockSpec(memory_space=pl.ANY)] * waits,
         out_specs=[VMEM] * len(outs),
         scratch_shapes=list(scratch),
-        compiler_params=PARAMS,
+        compiler_params=params,
         name=name,
     )
 
@@ -205,7 +221,8 @@
             (put_coded if d else put_plain)(out_ref.at[c], total, count)
 
 
-def merge_z_kernel(pos_ref, r1_ref, r2_ref, r3_ref, own_ref, mine_ref, give_ref, rest_ref):
+def merge_z_kernel(pos_ref, r1_ref, r2_ref, r3_ref, own_ref, *rest):
+    mine_ref, give_ref, rest_ref = rest[-3:]
     core = pos_ref[2]
     for out_ref, index in ((mine_ref, core), (give_ref, 1 - core)):
         total, count = gathered((own_ref.at[index],), [ref.at[index] for ref in (r1_ref, r2_ref, r3_ref)])
@@ -337,8 +354,7 @@
 
     made = {}
     for d in (2, 1, 3, 0):
-        meta = jnp.concatenate([jnp.stack([(x + d) % NX, core]).astype(jnp.int32), table])
-        made[d] = sums(d > 0, meta, packed, packed_other, features, other)
+        made[d] = sums(d, pos, table, packed, packed_other, features, other)
     far = [lax.ppermute(part, "node", shift_x(d)) for d in (2, 1, 3) for part in made[d]]
 
     seed_feats, w_self, bias_term, out_grad, own = lax.optimization_barrier(
@@ -351,7 +367,7 @@
     self_term = jnp.dot(seed_feats, w_self, preferred_element_type=jnp.float32)
     self_term = self_term + jnp.where(feat == 0, bias_term, 0.0)
 
-    own, *coded = call(merge_x_kernel, "merge_x", [SUM_PLAIN] + [SUM_CODED] * 3, 8)(
+    own, *coded = call(merge_x_kernel, "merge_x", [SUM_PLAIN] + [SUM_CODED] * 3, 8, params=ALONE)(
         pos, *far, *own
     )
     arrived = [lax.ppermute(coded[d - 1], "node", shift_z(d)) for d in (2, 1, 3)]

time: 153 us -> 126 us (0.82)
  Pallas kernels: 61.3 us -> 34.1 us
  local copies, waits for them, and re-layouts: 3.17 us -> 1.36 us
    pallas_call x6, Pallas kernels: 54.6 us -> 27.4 us  [the longest x4 22.2 us: sums(): pl.pallas_call(functools.partial(sums_kernel, d), out_shape=[jax.ShapeDty...]
    ppermute x10, waiting for transfers between devices: 4.09 us -> 2.54 us  [body(): swap = lambda value: lax.ppermute(value, 'node', SWAP_CORE)]
  transfers between devices with their start and end apart: 32 -> 32, of which waited for: 17 -> 17; matrix products, arithmetic and copies ran while one was open for 1% -> 3% of each run, Pallas kernels for 32% -> 16%
where the time goes in v2:
time: 126 us; the launch traced here: 125 us
  starting transfers between devices  43.7 us (35%)
  waiting for transfers between devices  42.2 us (33%)
  Pallas kernels  34.1 us (27%)
  matrix products  1.54 us (1%)
  other arithmetic  1.4 us (1%)
  local copies, waits for them, and re-layouts  1.36 us (1%)
    pallas_call x4, Pallas kernels, sums(): pl.pallas_call(functools.partial(sums_kernel, d), out_shape=[jax.ShapeDty...  22.2 us
    ppermute x3, waiting for transfers between devices, body(): lax.ppermute(parts[d - 1], 'node', shift_x(d))  14 us
    ppermute x6, starting transfers between devices, body(): lax.ppermute(part, 'node', shift_x(d))  8.31 us
    ppermute x3, starting transfers between devices, body(): lax.ppermute(parts[d - 1], 'node', shift_z(d))  7.85 us
    ppermute x6, waiting for transfers between devices, body(): lax.ppermute(part, 'node', shift_x(d))  7.77 us
    ppermute x3, starting transfers between devices, body(): lax.ppermute(coded[d - 1], 'node', shift_z(d))  6.56 us
    ppermute x3, starting transfers between devices, body(): lax.ppermute(coded[d - 1], 'feat', shift_y(d))  6.37 us
    ppermute x3, waiting for transfers between devices, body(): lax.ppermute(coded[d - 1], 'node', shift_z(d))  6.25 us
  transfers between devices with their start and end apart: 32, of which 17 were waited for; matrix products, arithmetic and copies ran while one was open for 3% of the time, Pallas kernels for 16%

profile of v2, /device:TPU:6, one launch (start us, length us, event | category | flops | bytes accessed | tf_op | source)
XLA Modules:
  0.0 125.2 jit_solution(5623687087072164873)
XLA Ops:
  0.7 0.1 collective-permute-start.1
  0.8 2.1 %half_columns.1 = bf16[2048,256]{1,0:T(8,128)(2,1)} custom-call(s32[1]{0:T(128)} %bitcast.5.side_ref, bf16[2048,512]{1,0:T(8,128)(2,1)} %feat0_ref.7), custom_call_target="tpu_custom_call" | custom-call | tf_op jit(solution)/shard_map/half_columns/pallas_call | solution.py:108
  2.9 0.6 collective-permute-start.2
  3.4 0.1 copy.15
  3.5 0.1 reshape.23
  3.6 0.1 pad_add_fusion.1
  3.7 0.1 collective-permute-start
  3.8 0.7 pad_add_fusion.2.pos_ref
  4.4 1.3 %collective-permute-done = s32[288]{0:T(512)S(1)} collective-permute-done((s32[288]{0:T(512)S(1)}, s32[288]{0:T(512)S(1)}, u32[]{:S(2)}, u32[]{:S(2)}) %collective-permute-start) | collective-permute-done | bytes 1184 | tf_op jit(solution)/shard_map/ppermute | solution.py:346
  5.7 0.1 slice.7
  5.8 0.7 pad_add_fusion.table_ref
  6.5 5.5 %sums.4 = (s16[4,272,128]{2,1,0:T(8,128)(2,1)}, s16[4,272,128]{2,1,0:T(8,128)(2,1)}) custom-call(s32[4]{0:T(128)} %pad_add_fusion.2.pos_ref, s32[576]{0:T(1024)} %pad_add_fusion.table_ref, s32[32,8,8,128]{3,2,1,0:T(8,128)} %bitcast.18, s32[32,8,8,128]{3,2,1,0:T(8,128)} %collective-permute-done.1.pat1_ref, bf16[2048,512]{1,0:T(8,128)(2,1)} %feat0_ref.7, ...), custom_call_target="tpu_custom_call" | custom-call | flops 2000000000 | bytes 3000000 | tf_op jit(solution)/shard_map/sums/pallas_call | solution.py:176
  12.0 1.5 %collective-permute-start.3 = (s16[4,272,128]{2,1,0:T(8,128)(2,1)}, s16[4,272,128]{2,1,0:T(8,128)(2,1)S(1)}, u32[]{:S(2)}, u32[]{:S(2)}) collective-permute-start(s16[4,272,128]{2,1,0:T(8,128)(2,1)} %get-tuple-element.43), channel_id=1, source_target_pairs={{0,16},{1,17},{2,18},{3,19},{4,20},{5,21},{6,22},{7,23},{8,24},{9,... | collective-permute-start | bytes 835592 | tf_op jit(solution)/shard_map/ppermute | solution.py:358
  13.5 2.1 %collective-permute-start.4 = (s16[4,272,128]{2,1,0:T(8,128)(2,1)}, s16[4,272,128]{2,1,0:T(8,128)(2,1)S(1)}, u32[]{:S(2)}, u32[]{:S(2)}) collective-permute-start(s16[4,272,128]{2,1,0:T(8,128)(2,1)} %get-tuple-element.44), channel_id=1, source_target_pairs={{0,16},{1,17},{2,18},{3,19},{4,20},{5,21},{6,22},{7,23},{8,24},{9,... | collective-permute-start | bytes 835592 | tf_op jit(solution)/shard_map/ppermute | solution.py:358
  15.6 5.5 %sums.5 = (s16[4,272,128]{2,1,0:T(8,128)(2,1)}, s16[4,272,128]{2,1,0:T(8,128)(2,1)}) custom-call(s32[4]{0:T(128)} %pad_add_fusion.2.pos_ref, s32[576]{0:T(1024)} %pad_add_fusion.table_ref, s32[32,8,8,128]{3,2,1,0:T(8,128)} %bitcast.19, s32[32,8,8,128]{3,2,1,0:T(8,128)} %collective-permute-done.1.pat1_ref, bf16[2048,512]{1,0:T(8,128)(2,1)} %feat0_ref.7, ...), custom_call_target="tpu_custom_call" | custom-call | flops 2000000000 | bytes 3000000 | tf_op jit(solution)/shard_map/sums/pallas_call | solution.py:176
  21.2 2.3 %collective-permute-start.5 = (s16[4,272,128]{2,1,0:T(8,128)(2,1)}, s16[4,272,128]{2,1,0:T(8,128)(2,1)}, u32[]{:S(2)}, u32[]{:S(2)}) collective-permute-start(s16[4,272,128]{2,1,0:T(8,128)(2,1)} %get-tuple-element.45), channel_id=1, source_target_pairs={{0,8},{1,9},{2,10},{3,11},{4,12},{5,13},{6,14},{7,15},{8,16},{9,17... | collective-permute-start | bytes 835592 | tf_op jit(solution)/shard_map/ppermute | solution.py:358
  23.5 0.1 collective-permute-start.6
  23.6 5.5 %sums.6 = (s16[4,272,128]{2,1,0:T(8,128)(2,1)}, s16[4,272,128]{2,1,0:T(8,128)(2,1)}) custom-call(s32[4]{0:T(128)} %pad_add_fusion.2.pos_ref, s32[576]{0:T(1024)} %pad_add_fusion.table_ref, s32[32,8,8,128]{3,2,1,0:T(8,128)} %bitcast.20, s32[32,8,8,128]{3,2,1,0:T(8,128)} %collective-permute-done.1.pat1_ref, bf16[2048,512]{1,0:T(8,128)(2,1)} %feat0_ref.7, ...), custom_call_target="tpu_custom_call" | custom-call | flops 2000000000 | bytes 3000000 | tf_op jit(solution)/shard_map/sums/pallas_call | solution.py:176
  29.1 2.2 %collective-permute-start.7 = (s16[4,272,128]{2,1,0:T(8,128)(2,1)}, s16[4,272,128]{2,1,0:T(8,128)(2,1)}, u32[]{:S(2)}, u32[]{:S(2)}) collective-permute-start(s16[4,272,128]{2,1,0:T(8,128)(2,1)} %get-tuple-element.47), channel_id=1, source_target_pairs={{0,24},{1,25},{2,26},{3,27},{4,28},{5,29},{6,30},{7,31},{8,0},{9,1... | collective-permute-start | bytes 835592 | tf_op jit(solution)/shard_map/ppermute | solution.py:358
  31.3 0.1 collective-permute-start.8
  31.4 5.7 %sums.7 = (f32[4,264,128]{2,1,0:T(8,128)}, f32[4,264,128]{2,1,0:T(8,128)}) custom-call(s32[4]{0:T(128)} %pad_add_fusion.2.pos_ref, s32[576]{0:T(1024)} %pad_add_fusion.table_ref, s32[32,8,8,128]{3,2,1,0:T(8,128)} %bitcast.21, s32[32,8,8,128]{3,2,1,0:T(8,128)} %collective-permute-done.1.pat1_ref, bf16[2048,512]{1,0:T(8,128)(2,1)} %feat0_ref.7, ...), custom_call_target="tpu_custom_call" | custom-call | flops 2000000000 | bytes 3000000 | tf_op jit(solution)/shard_map/sums/pallas_call | solution.py:176
  37.1 3.2 %collective-permute-done.6.rest_3_ = s16[4,272,128]{2,1,0:T(8,128)(2,1)} collective-permute-done((s16[4,272,128]{2,1,0:T(8,128)(2,1)}, s16[4,272,128]{2,1,0:T(8,128)(2,1)}, u32[]{:S(2)}, u32[]{:S(2)}) %collective-permute-start.6) | collective-permute-done | bytes 278560 | tf_op jit(solution)/shard_map/ppermute | solution.py:358
  40.3 0.1 collective-permute-done.7.rest_4_
  40.5 4.5 %collective-permute-done.8.rest_5_ = s16[4,272,128]{2,1,0:T(8,128)(2,1)} collective-permute-done((s16[4,272,128]{2,1,0:T(8,128)(2,1)}, s16[4,272,128]{2,1,0:T(8,128)(2,1)}, u32[]{:S(2)}, u32[]{:S(2)}) %collective-permute-start.8) | collective-permute-done | bytes 278560 | tf_op jit(solution)/shard_map/ppermute | solution.py:358
  44.9 3.1 %merge_x.1 = (f32[2,264,128]{2,1,0:T(8,128)}, s16[2,272,128]{2,1,0:T(8,128)(2,1)}, s16[2,272,128]{2,1,0:T(8,128)(2,1)}, s16[2,272,128]{2,1,0:T(8,128)(2,1)}) custom-call(s32[4]{0:T(128)} %pad_add_fusion.2.pos_ref, s16[4,272,128]{2,1,0:T(8,128)(2,1)} %copy-done.5, s16[4,272,128]{2,1,0:T(8,128)(2,1)} %copy-done.6, ...), custom_call_target="tpu_custom_call" | custom-call | tf_op jit(solution)/shard_map/merge_x/pallas_call | solution.py:370
  48.0 2.7 %collective-permute-start.9 = (s16[2,272,128]{2,1,0:T(8,128)(2,1)}, s16[2,272,128]{2,1,0:T(8,128)(2,1)S(1)}, u32[]{:S(2)}, u32[]{:S(2)}) collective-permute-start(s16[2,272,128]{2,1,0:T(8,128)(2,1)} %get-tuple-element.53), channel_id=1, source_target_pairs={{0,4},{1,5},{2,6},{3,7},{4,0},{5,1},{6,2},{7,3},{8,12},{9,13},{10,... | collective-permute-start | bytes 417800 | tf_op jit(solution)/shard_map/ppermute | solution.py:373
  50.7 1.9 %collective-permute-start.10 = (s16[2,272,128]{2,1,0:T(8,128)(2,1)}, s16[2,272,128]{2,1,0:T(8,128)(2,1)S(1)}, u32[]{:S(2)}, u32[]{:S(2)}) collective-permute-start(s16[2,272,128]{2,1,0:T(8,128)(2,1)} %get-tuple-element.54), channel_id=1, source_target_pairs={{0,2},{1,3},{2,4},{3,5},{4,6},{5,7},{6,0},{7,1},{8,10},{9,11},{10,... | collective-permute-start | bytes 417800 | tf_op jit(solution)/shard_map/ppermute | solution.py:373
  52.7 1.9 %collective-permute-start.11 = (s16[2,272,128]{2,1,0:T(8,128)(2,1)}, s16[2,272,128]{2,1,0:T(8,128)(2,1)S(1)}, u32[]{:S(2)}, u32[]{:S(2)}) collective-permute-start(s16[2,272,128]{2,1,0:T(8,128)(2,1)} %get-tuple-element.55), channel_id=1, source_target_pairs={{0,6},{1,7},{2,0},{3,1},{4,2},{5,3},{6,4},{7,5},{8,14},{9,15},{10,... | collective-permute-start | bytes 417800 | tf_op jit(solution)/shard_map/ppermute | solution.py:373
  54.6 6.0 %collective-permute-done.9.r1_ref = s16[2,272,128]{2,1,0:T(8,128)(2,1)S(1)} collective-permute-done((s16[2,272,128]{2,1,0:T(8,128)(2,1)}, s16[2,272,128]{2,1,0:T(8,128)(2,1)S(1)}, u32[]{:S(2)}, u32[]{:S(2)}) %collective-permute-start.9) | collective-permute-done | bytes 139296 | tf_op jit(solution)/shard_map/ppermute | solution.py:373
  60.6 0.2 collective-permute-done.11.r3_ref
  60.8 1.0 copy-done.1
  61.8 0.7 merge_z.1
  62.5 0.1 collective-permute-start.12
  62.6 1.5 %convolution_add_fusion.self_ref = f32[128,1024]{1,0:T(8,128)S(1)} fusion(bf16[128,512]{1,0:T(8,128)(2,1)S(1)} %copy-done.4, bf16[512,1024]{1,0:T(8,128)(2,1)} %param.14, f32[1024]{0:T(1024)S(1)} %broadcast_select_fusion), kind=kOutput, calls=%fused_computation | convolution fusion | flops 134348800 | bytes 1708032 | tf_op jit(solution)/shard_map/dot_general | solution.py:367
  64.2 1.1 pre_terms.1
  65.3 3.1 %collective-permute-start.13 = (s16[272,128]{1,0:T(8,128)(2,1)S(1)}, s16[272,128]{1,0:T(8,128)(2,1)S(1)}, u32[]{:S(2)}, u32[]{:S(2)}) collective-permute-start(s16[272,128]{1,0:T(8,128)(2,1)S(1)} %get-tuple-element.63), channel_id=1, source_target_pairs={{0,64},{32,96},{64,0},{96,32},{128,192},{160,224},{192,128},{224,1... | collective-permute-start | bytes 208904 | tf_op jit(solution)/shard_map/ppermute | solution.py:383
  68.4 0.7 collective-permute-start.14
  69.1 2.5 %collective-permute-start.15 = (s16[272,128]{1,0:T(8,128)(2,1)S(1)}, s16[272,128]{1,0:T(8,128)(2,1)S(1)}, u32[]{:S(2)}, u32[]{:S(2)}) collective-permute-start(s16[272,128]{1,0:T(8,128)(2,1)S(1)} %get-tuple-element.65), channel_id=1, source_target_pairs={{0,96},{32,0},{64,32},{96,64},{128,224},{160,128},{192,160},{224,1... | collective-permute-start | bytes 208904 | tf_op jit(solution)/shard_map/ppermute | solution.py:383
  71.7 0.1 copy.16
  71.8 2.1 %collective-permute-done.14.r2_ref = s16[272,128]{1,0:T(8,128)(2,1)S(1)} collective-permute-done((s16[272,128]{1,0:T(8,128)(2,1)S(1)}, s16[272,128]{1,0:T(8,128)(2,1)S(1)}, u32[]{:S(2)}, u32[]{:S(2)}) %collective-permute-start.14) | collective-permute-done | bytes 69664 | tf_op jit(solution)/shard_map/ppermute | solution.py:383
  74.0 0.7 merge_y.1.own_ref
  74.6 5.8 %collective-permute-start.16 = (s16[272,128]{1,0:T(8,128)(2,1)S(1)}, s16[272,128]{1,0:T(8,128)(2,1)S(1)}, u32[]{:S(2)}, u32[]{:S(2)}) collective-permute-start(s16[272,128]{1,0:T(8,128)(2,1)S(1)} %merge_y.1.own_ref), channel_id=1, source_target_pairs={{0,128},{32,160},{64,192},{96,224},{128,0},{160,32},{192,64},{224,... | collective-permute-start | bytes 208904 | tf_op jit(solution)/shard_map/ppermute | solution.py:385
  80.4 0.1 collective-permute-start.25
  80.5 2.5 %collective-permute-done.16.far_ref = s16[272,128]{1,0:T(8,128)(2,1)S(1)} collective-permute-done((s16[272,128]{1,0:T(8,128)(2,1)S(1)}, s16[272,128]{1,0:T(8,128)(2,1)S(1)}, u32[]{:S(2)}, u32[]{:S(2)}) %collective-permute-start.16) | collective-permute-done | bytes 69664 | tf_op jit(solution)/shard_map/ppermute | solution.py:385
  83.0 0.6 hidden.1.a0_ref
  83.6 0.9 collective-permute-start.17
  84.5 4.1 %collective-permute-start.18 = (bf16[256,128]{1,0:T(8,128)(2,1)S(1)}, bf16[256,128]{1,0:T(8,128)(2,1)S(1)}, u32[]{:S(2)}, u32[]{:S(2)}) collective-permute-start(bf16[256,128]{1,0:T(8,128)(2,1)S(1)} %hidden.1.a0_ref), channel_id=1, source_target_pairs={{0,64},{32,96},{64,0},{96,32},{128,192},{160,224},{192,128},{224,1... | collective-permute-start | bytes 196616 | tf_op jit(solution)/shard_map/ppermute | solution.py:387
  88.6 0.8 collective-permute-done.17.a1_ref
  89.4 2.2 %collective-permute-done.18.a2_ref = bf16[256,128]{1,0:T(8,128)(2,1)S(1)} collective-permute-done((bf16[256,128]{1,0:T(8,128)(2,1)S(1)}, bf16[256,128]{1,0:T(8,128)(2,1)S(1)}, u32[]{:S(2)}, u32[]{:S(2)}) %collective-permute-start.18) | collective-permute-done | bytes 65568 | tf_op jit(solution)/shard_map/ppermute | solution.py:387
  91.6 1.3 %collective-permute-done.19.a3_ref = bf16[256,128]{1,0:T(8,128)(2,1)S(1)} collective-permute-done((bf16[256,128]{1,0:T(8,128)(2,1)S(1)}, bf16[256,128]{1,0:T(8,128)(2,1)S(1)}, u32[]{:S(2)}, u32[]{:S(2)}) %collective-permute-start.19) | collective-permute-done | bytes 65568 | tf_op jit(solution)/shard_map/ppermute | solution.py:387
  92.9 1.2 collective-permute-done.23.b3_ref
  94.1 1.6 %grads.1 = (bf16[128,1024]{1,0:T(8,128)(2,1)}, f32[128,1152]{1,0:T(8,128)S(1)}, bf16[128,1152]{1,0:T(8,128)(2,1)S(1)}, bf16[128,1152]{1,0:T(8,128)(2,1)S(1)}, bf16[128,1152]{1,0:T(8,128)(2,1)S(1)}) custom-call(s32[4]{0:T(128)S(1)} %copy-done.3, bf16[256,128]{1,0:T(8,128)(2,1)S(1)} %hidden.1.a0_ref, bf16[256,128]{1,0:T(8,128)(2,1)S(1)} %collective-permute-done.17.a1_ref, ...), custom_call_target="tpu_custom_call" | custom-call | tf_op jit(solution)/shard_map/grads/pallas_call | solution.py:398
  95.7 0.9 collective-permute-start.26
  96.6 1.1 collective-permute-start.27
  97.7 0.9 collective-permute-start.28
  98.7 8.5 %collective-permute-done.26.r1_ref = bf16[128,1152]{1,0:T(8,128)(2,1)S(1)} collective-permute-done((bf16[128,1152]{1,0:T(8,128)(2,1)S(1)}, bf16[128,1152]{1,0:T(8,128)(2,1)S(1)}, u32[]{:S(2)}, u32[]{:S(2)}) %collective-permute-start.26) | collective-permute-done | bytes 294944 | tf_op jit(solution)/shard_map/ppermute | solution.py:401
  107.1 3.1 %collective-permute-done.27.r2_ref = bf16[128,1152]{1,0:T(8,128)(2,1)S(1)} collective-permute-done((bf16[128,1152]{1,0:T(8,128)(2,1)S(1)}, bf16[128,1152]{1,0:T(8,128)(2,1)S(1)}, u32[]{:S(2)}, u32[]{:S(2)}) %collective-permute-start.27) | collective-permute-done | bytes 294944 | tf_op jit(solution)/shard_map/ppermute | solution.py:401
  110.3 2.4 %collective-permute-done.28.r3_ref = bf16[128,1152]{1,0:T(8,128)(2,1)S(1)} collective-permute-done((bf16[128,1152]{1,0:T(8,128)(2,1)S(1)}, bf16[128,1152]{1,0:T(8,128)(2,1)S(1)}, u32[]{:S(2)}, u32[]{:S(2)}) %collective-permute-start.28) | collective-permute-done | bytes 294944 | tf_op jit(solution)/shard_map/ppermute | solution.py:401
  112.6 0.8 fold_x.1
  113.4 4.0 %collective-permute-start.29 = (bf16[32,1152]{1,0:T(8,128)(2,1)S(1)}, bf16[32,1152]{1,0:T(8,128)(2,1)S(1)}, u32[]{:S(2)}, u32[]{:S(2)}) collective-permute-start(bf16[32,1152]{1,0:T(8,128)(2,1)S(1)} %get-tuple-element.75), channel_id=1, source_target_pairs={{0,4},{1,5},{2,6},{3,7},{4,0},{5,1},{6,2},{7,3},{8,12},{9,13},{10,... | collective-permute-start | bytes 221192 | tf_op jit(solution)/shard_map/ppermute | solution.py:406
  117.4 3.8 %collective-permute-start.31 = (bf16[32,1152]{1,0:T(8,128)(2,1)S(1)}, bf16[32,1152]{1,0:T(8,128)(2,1)S(1)}, u32[]{:S(2)}, u32[]{:S(2)}) collective-permute-start(bf16[32,1152]{1,0:T(8,128)(2,1)S(1)} %get-tuple-element.77), channel_id=1, source_target_pairs={{0,6},{1,7},{2,0},{3,1},{4,2},{5,3},{6,4},{7,5},{8,14},{9,15},{10,... | collective-permute-start | bytes 221192 | tf_op jit(solution)/shard_map/ppermute | solution.py:406
  121.3 1.5 %collective-permute-done.29.r1_ref = bf16[32,1152]{1,0:T(8,128)(2,1)S(1)} collective-permute-done((bf16[32,1152]{1,0:T(8,128)(2,1)S(1)}, bf16[32,1152]{1,0:T(8,128)(2,1)S(1)}, u32[]{:S(2)}, u32[]{:S(2)}) %collective-permute-start.29) | collective-permute-done | bytes 73760 | tf_op jit(solution)/shard_map/ppermute | solution.py:406
  122.8 1.2 collective-permute-done.30.r2_ref
  124.0 1.3 %last.1 = (f32[16,1024]{1,0:T(8,128)}, f32[16,1024]{1,0:T(8,128)}, f32[1,32]{1,0:T(1,128)}) custom-call(s32[4]{0:T(128)S(1)} %copy-done.3, bf16[32,1152]{1,0:T(8,128)(2,1)S(1)} %collective-permute-done.29.r1_ref, bf16[32,1152]{1,0:T(8,128)(2,1)S(1)} %collective-permute-done.30.r2_ref, bf16[32,1152]{1,0:T(8,128)(2,1)S(1)} %collective-permute-done.31.r3_ref, ...), custom_call_target="tpu_custom_call" | custom-call | tf_op jit(solution)/shard_map/last/pallas_call | solution.py:408
  (44 shorter events, 0.1 us)
Async XLA Ops:
  0.6 2.8 %copy-start.7 = (s32[32,8]{0,1:T(8,128)S(1)}, s32[32,8]{0,1:T(8,128)}, u32[]{:S(2)}) copy-start(s32[32,8]{0,1:T(8,128)} %param.12) | copy-start | bytes 3076
  0.6 3.0 %copy-start.9 = (s32[32]{0:T(128)S(1)}, s32[32]{0:T(128)}, u32[]{:S(2)}) copy-start(s32[32]{0:T(128)} %param.13) | copy-start | bytes 388
  0.7 5.8 %collective-permute-start.1 = (s32[32,8,8,128]{3,2,1,0:T(8,128)}, s32[32,8,8,128]{3,2,1,0:T(8,128)}, u32[]{:S(2)}, u32[]{:S(2)}) collective-permute-start(s32[32,8,8,128]{3,2,1,0:T(8,128)} %bitcast.17), channel_id=1, source_target_pairs={{0,1},{1,0},{2,3},{3,2},{4,5},{5,4},{6,7},{7,6},{8,9},{9,8},{10,11... | collective-permute-start | bytes 3145736 | tf_op jit(solution)/shard_map/ppermute | solution.py:346
  2.9 3.6 %collective-permute-start.2 = (bf16[2048,256]{1,0:T(8,128)(2,1)}, bf16[2048,256]{1,0:T(8,128)(2,1)}, u32[]{:S(2)}, u32[]{:S(2)}) collective-permute-start(bf16[2048,256]{1,0:T(8,128)(2,1)} %half_columns.1), channel_id=1, source_target_pairs={{0,1},{1,0},{2,3},{3,2},{4,5},{5,4},{6,7},{7,6},{8,9},{9,8},{10,11... | collective-permute-start | bytes 3145736 | tf_op jit(solution)/shard_map/ppermute | solution.py:346
  3.7 2.0 %collective-permute-start = (s32[288]{0:T(512)S(1)}, s32[288]{0:T(512)S(1)}, u32[]{:S(2)}, u32[]{:S(2)}) collective-permute-start(s32[288]{0:T(512)S(1)} %pad_add_fusion.1), channel_id=1, source_target_pairs={{0,1},{1,0},{2,3},{3,2},{4,5},{5,4},{6,7},{7,6},{8,9},{9,8},{10,11... | collective-permute-start | bytes 3464 | tf_op jit(solution)/shard_map/ppermute | solution.py:346
  12.0 19.3 %collective-permute-start.3 = (s16[4,272,128]{2,1,0:T(8,128)(2,1)}, s16[4,272,128]{2,1,0:T(8,128)(2,1)S(1)}, u32[]{:S(2)}, u32[]{:S(2)}) collective-permute-start(s16[4,272,128]{2,1,0:T(8,128)(2,1)} %get-tuple-element.43), channel_id=1, source_target_pairs={{0,16},{1,17},{2,18},{3,19},{4,20},{5,21},{6,22},{7,23},{8,24},{9,... | collective-permute-start | bytes 835592 | tf_op jit(solution)/shard_map/ppermute | solution.py:358
  13.5 23.6 %collective-permute-start.4 = (s16[4,272,128]{2,1,0:T(8,128)(2,1)}, s16[4,272,128]{2,1,0:T(8,128)(2,1)S(1)}, u32[]{:S(2)}, u32[]{:S(2)}) collective-permute-start(s16[4,272,128]{2,1,0:T(8,128)(2,1)} %get-tuple-element.44), channel_id=1, source_target_pairs={{0,16},{1,17},{2,18},{3,19},{4,20},{5,21},{6,22},{7,23},{8,24},{9,... | collective-permute-start | bytes 835592 | tf_op jit(solution)/shard_map/ppermute | solution.py:358
  21.2 15.9 %collective-permute-start.5 = (s16[4,272,128]{2,1,0:T(8,128)(2,1)}, s16[4,272,128]{2,1,0:T(8,128)(2,1)}, u32[]{:S(2)}, u32[]{:S(2)}) collective-permute-start(s16[4,272,128]{2,1,0:T(8,128)(2,1)} %get-tuple-element.45), channel_id=1, source_target_pairs={{0,8},{1,9},{2,10},{3,11},{4,12},{5,13},{6,14},{7,15},{8,16},{9,17... | collective-permute-start | bytes 835592 | tf_op jit(solution)/shard_map/ppermute | solution.py:358
  23.5 16.9 %collective-permute-start.6 = (s16[4,272,128]{2,1,0:T(8,128)(2,1)}, s16[4,272,128]{2,1,0:T(8,128)(2,1)}, u32[]{:S(2)}, u32[]{:S(2)}) collective-permute-start(s16[4,272,128]{2,1,0:T(8,128)(2,1)} %get-tuple-element.46), channel_id=1, source_target_pairs={{0,8},{1,9},{2,10},{3,11},{4,12},{5,13},{6,14},{7,15},{8,16},{9,17... | collective-permute-start | bytes 835592 | tf_op jit(solution)/shard_map/ppermute | solution.py:358
  29.1 11.4 %collective-permute-start.7 = (s16[4,272,128]{2,1,0:T(8,128)(2,1)}, s16[4,272,128]{2,1,0:T(8,128)(2,1)}, u32[]{:S(2)}, u32[]{:S(2)}) collective-permute-start(s16[4,272,128]{2,1,0:T(8,128)(2,1)} %get-tuple-element.47), channel_id=1, source_target_pairs={{0,24},{1,25},{2,26},{3,27},{4,28},{5,29},{6,30},{7,31},{8,0},{9,1... | collective-permute-start | bytes 835592 | tf_op jit(solution)/shard_map/ppermute | solution.py:358
  31.3 5.8 %copy-start.5 = (s16[4,272,128]{2,1,0:T(8,128)(2,1)}, s16[4,272,128]{2,1,0:T(8,128)(2,1)S(1)}, u32[]{:S(2)}) copy-start(s16[4,272,128]{2,1,0:T(8,128)(2,1)S(1)} %collective-permute-done.3.rest_0_) | copy-start | bytes 835588
  31.3 13.6 %collective-permute-start.8 = (s16[4,272,128]{2,1,0:T(8,128)(2,1)}, s16[4,272,128]{2,1,0:T(8,128)(2,1)}, u32[]{:S(2)}, u32[]{:S(2)}) collective-permute-start(s16[4,272,128]{2,1,0:T(8,128)(2,1)} %get-tuple-element.48), channel_id=1, source_target_pairs={{0,24},{1,25},{2,26},{3,27},{4,28},{5,29},{6,30},{7,31},{8,0},{9,1... | collective-permute-start | bytes 835592 | tf_op jit(solution)/shard_map/ppermute | solution.py:358
  37.1 17.5 %copy-start.8 = (f32[1024]{0:T(1024)S(1)}, f32[1024]{0:T(1024)}, u32[]{:S(2)}) copy-start(f32[1024]{0:T(1024)} %param.16) | copy-start | bytes 12292
  37.1 23.7 %copy-start.3 = (s32[4]{0:T(128)S(1)}, s32[4]{0:T(128)}, u32[]{:S(2)}) copy-start(s32[4]{0:T(128)} %pad_add_fusion.2.pos_ref) | copy-start | bytes 52
  37.1 25.5 %copy-start.4 = (bf16[128,512]{1,0:T(8,128)(2,1)S(1)}, bf16[128,512]{1,0:T(8,128)(2,1)}, u32[]{:S(2)}) copy-start(bf16[128,512]{1,0:T(8,128)(2,1)} %param.10) | copy-start | bytes 393220
  37.1 7.8 %copy-start.6 = (s16[4,272,128]{2,1,0:T(8,128)(2,1)}, s16[4,272,128]{2,1,0:T(8,128)(2,1)S(1)}, u32[]{:S(2)}) copy-start(s16[4,272,128]{2,1,0:T(8,128)(2,1)S(1)} %collective-permute-done.4.rest_1_) | copy-start | bytes 835588
  44.9 26.8 %copy-start.2 = (bf16[128,1024]{1,0:T(8,128)(2,1)S(1)}, bf16[128,1024]{1,0:T(8,128)(2,1)}, u32[]{:S(2)}) copy-start(bf16[128,1024]{1,0:T(8,128)(2,1)} %og0_ref) | copy-start | bytes 786436
  48.0 16.2 %copy-start = (bf16[512,1024]{1,0:T(8,128)(2,1)S(1)}, bf16[512,1024]{1,0:T(8,128)(2,1)}, u32[]{:S(2)}) copy-start(bf16[512,1024]{1,0:T(8,128)(2,1)} %w_ref.1) | copy-start | bytes 3145732
  48.0 12.6 %collective-permute-start.9 = (s16[2,272,128]{2,1,0:T(8,128)(2,1)}, s16[2,272,128]{2,1,0:T(8,128)(2,1)S(1)}, u32[]{:S(2)}, u32[]{:S(2)}) collective-permute-start(s16[2,272,128]{2,1,0:T(8,128)(2,1)} %get-tuple-element.53), channel_id=1, source_target_pairs={{0,4},{1,5},{2,6},{3,7},{4,0},{5,1},{6,2},{7,3},{8,12},{9,13},{10,... | collective-permute-start | bytes 417800 | tf_op jit(solution)/shard_map/ppermute | solution.py:373
  50.7 9.8 %collective-permute-start.10 = (s16[2,272,128]{2,1,0:T(8,128)(2,1)}, s16[2,272,128]{2,1,0:T(8,128)(2,1)S(1)}, u32[]{:S(2)}, u32[]{:S(2)}) collective-permute-start(s16[2,272,128]{2,1,0:T(8,128)(2,1)} %get-tuple-element.54), channel_id=1, source_target_pairs={{0,2},{1,3},{2,4},{3,5},{4,6},{5,7},{6,0},{7,1},{8,10},{9,11},{10,... | collective-permute-start | bytes 417800 | tf_op jit(solution)/shard_map/ppermute | solution.py:373
  52.7 8.2 %collective-permute-start.11 = (s16[2,272,128]{2,1,0:T(8,128)(2,1)}, s16[2,272,128]{2,1,0:T(8,128)(2,1)S(1)}, u32[]{:S(2)}, u32[]{:S(2)}) collective-permute-start(s16[2,272,128]{2,1,0:T(8,128)(2,1)} %get-tuple-element.55), channel_id=1, source_target_pairs={{0,6},{1,7},{2,0},{3,1},{4,2},{5,3},{6,4},{7,5},{8,14},{9,15},{10,... | collective-permute-start | bytes 417800 | tf_op jit(solution)/shard_map/ppermute | solution.py:373
  60.8 1.0 copy-start.1
  62.5 1.7 %collective-permute-start.12 = (bf16[384,128]{1,0:T(8,128)(2,1)S(1)}, bf16[384,128]{1,0:T(8,128)(2,1)S(1)}, u32[]{:S(2)}, u32[]{:S(2)}) collective-permute-start(bf16[384,128]{1,0:T(8,128)(2,1)S(1)} %get-tuple-element.58), channel_id=1, source_target_pairs={{0,1},{1,0},{2,3},{3,2},{4,5},{5,4},{6,7},{7,6},{8,9},{9,8},{10,11... | collective-permute-start | bytes 294920 | tf_op jit(solution)/shard_map/ppermute | solution.py:346
  65.3 6.5 %collective-permute-start.13 = (s16[272,128]{1,0:T(8,128)(2,1)S(1)}, s16[272,128]{1,0:T(8,128)(2,1)S(1)}, u32[]{:S(2)}, u32[]{:S(2)}) collective-permute-start(s16[272,128]{1,0:T(8,128)(2,1)S(1)} %get-tuple-element.63), channel_id=1, source_target_pairs={{0,64},{32,96},{64,0},{96,32},{128,192},{160,224},{192,128},{224,1... | collective-permute-start | bytes 208904 | tf_op jit(solution)/shard_map/ppermute | solution.py:383
  68.4 5.5 %collective-permute-start.14 = (s16[272,128]{1,0:T(8,128)(2,1)S(1)}, s16[272,128]{1,0:T(8,128)(2,1)S(1)}, u32[]{:S(2)}, u32[]{:S(2)}) collective-permute-start(s16[272,128]{1,0:T(8,128)(2,1)S(1)} %get-tuple-element.64), channel_id=1, source_target_pairs={{0,32},{32,64},{64,96},{96,0},{128,160},{160,192},{192,224},{224,1... | collective-permute-start | bytes 208904 | tf_op jit(solution)/shard_map/ppermute | solution.py:383
  69.1 4.8 %collective-permute-start.15 = (s16[272,128]{1,0:T(8,128)(2,1)S(1)}, s16[272,128]{1,0:T(8,128)(2,1)S(1)}, u32[]{:S(2)}, u32[]{:S(2)}) collective-permute-start(s16[272,128]{1,0:T(8,128)(2,1)S(1)} %get-tuple-element.65), channel_id=1, source_target_pairs={{0,96},{32,0},{64,32},{96,64},{128,224},{160,128},{192,160},{224,1... | collective-permute-start | bytes 208904 | tf_op jit(solution)/shard_map/ppermute | solution.py:383
  71.7 21.2 %collective-permute-start.24 = (bf16[128,1024]{1,0:T(8,128)(2,1)S(1)}, bf16[128,1024]{1,0:T(8,128)(2,1)S(1)}, u32[]{:S(2)}, u32[]{:S(2)}) collective-permute-start(bf16[128,1024]{1,0:T(8,128)(2,1)S(1)} %copy-done.2), channel_id=1, source_target_pairs={{0,1},{1,0},{2,3},{3,2},{4,5},{5,4},{6,7},{7,6},{8,9},{9,8},{10,11... | collective-permute-start | bytes 786440 | tf_op jit(solution)/shard_map/ppermute | solution.py:346
  74.6 8.4 %collective-permute-start.16 = (s16[272,128]{1,0:T(8,128)(2,1)S(1)}, s16[272,128]{1,0:T(8,128)(2,1)S(1)}, u32[]{:S(2)}, u32[]{:S(2)}) collective-permute-start(s16[272,128]{1,0:T(8,128)(2,1)S(1)} %merge_y.1.own_ref), channel_id=1, source_target_pairs={{0,128},{32,160},{64,192},{96,224},{128,0},{160,32},{192,64},{224,... | collective-permute-start | bytes 208904 | tf_op jit(solution)/shard_map/ppermute | solution.py:385
  80.4 8.2 %collective-permute-start.25 = (bf16[256,128]{1,0:T(8,128)(2,1)S(1)}, bf16[256,128]{1,0:T(8,128)(2,1)S(1)}, u32[]{:S(2)}, u32[]{:S(2)}) collective-permute-start(bf16[256,128]{1,0:T(8,128)(2,1)S(1)} %bitcast.16), channel_id=1, source_target_pairs={{0,1},{1,0},{2,3},{3,2},{4,5},{5,4},{6,7},{7,6},{8,9},{9,8},{10,11... | collective-permute-start | bytes 196616 | tf_op jit(solution)/shard_map/ppermute | solution.py:346
  83.6 5.8 %collective-permute-start.17 = (bf16[256,128]{1,0:T(8,128)(2,1)S(1)}, bf16[256,128]{1,0:T(8,128)(2,1)S(1)}, u32[]{:S(2)}, u32[]{:S(2)}) collective-permute-start(bf16[256,128]{1,0:T(8,128)(2,1)S(1)} %hidden.1.a0_ref), channel_id=1, source_target_pairs={{0,32},{32,64},{64,96},{96,0},{128,160},{160,192},{192,224},{224,1... | collective-permute-start | bytes 196616 | tf_op jit(solution)/shard_map/ppermute | solution.py:387
  84.5 7.1 %collective-permute-start.18 = (bf16[256,128]{1,0:T(8,128)(2,1)S(1)}, bf16[256,128]{1,0:T(8,128)(2,1)S(1)}, u32[]{:S(2)}, u32[]{:S(2)}) collective-permute-start(bf16[256,128]{1,0:T(8,128)(2,1)S(1)} %hidden.1.a0_ref), channel_id=1, source_target_pairs={{0,64},{32,96},{64,0},{96,32},{128,192},{160,224},{192,128},{224,1... | collective-permute-start | bytes 196616 | tf_op jit(solution)/shard_map/ppermute | solution.py:387
  88.6 4.3 %collective-permute-start.19 = (bf16[256,128]{1,0:T(8,128)(2,1)S(1)}, bf16[256,128]{1,0:T(8,128)(2,1)S(1)}, u32[]{:S(2)}, u32[]{:S(2)}) collective-permute-start(bf16[256,128]{1,0:T(8,128)(2,1)S(1)} %hidden.1.a0_ref), channel_id=1, source_target_pairs={{0,96},{32,0},{64,32},{96,64},{128,224},{160,128},{192,160},{224,1... | collective-permute-start | bytes 196616 | tf_op jit(solution)/shard_map/ppermute | solution.py:387
  88.6 4.3 %collective-permute-start.20 = (bf16[256,128]{1,0:T(8,128)(2,1)S(1)}, bf16[256,128]{1,0:T(8,128)(2,1)S(1)}, u32[]{:S(2)}, u32[]{:S(2)}) collective-permute-start(bf16[256,128]{1,0:T(8,128)(2,1)S(1)} %hidden.1.a0_ref), channel_id=1, source_target_pairs={{0,1},{1,0},{2,3},{3,2},{4,5},{5,4},{6,7},{7,6},{8,9},{9,8},{10,11... | collective-permute-start | bytes 196616 | tf_op jit(solution)/shard_map/ppermute | solution.py:346
  89.4 3.5 %collective-permute-start.21 = (bf16[256,128]{1,0:T(8,128)(2,1)S(1)}, bf16[256,128]{1,0:T(8,128)(2,1)S(1)}, u32[]{:S(2)}, u32[]{:S(2)}) collective-permute-start(bf16[256,128]{1,0:T(8,128)(2,1)S(1)} %collective-permute-done.17.a1_ref), channel_id=1, source_target_pairs={{0,1},{1,0},{2,3},{3,2},{4,5},{5,4},{6,7},{7,6},{8,9},{9,8},{10,11... | collective-permute-start | bytes 196616 | tf_op jit(solution)/shard_map/ppermute | solution.py:346
  91.6 1.4 %collective-permute-start.22 = (bf16[256,128]{1,0:T(8,128)(2,1)S(1)}, bf16[256,128]{1,0:T(8,128)(2,1)S(1)}, u32[]{:S(2)}, u32[]{:S(2)}) collective-permute-start(bf16[256,128]{1,0:T(8,128)(2,1)S(1)} %collective-permute-done.18.a2_ref), channel_id=1, source_target_pairs={{0,1},{1,0},{2,3},{3,2},{4,5},{5,4},{6,7},{7,6},{8,9},{9,8},{10,11... | collective-permute-start | bytes 196616 | tf_op jit(solution)/shard_map/ppermute | solution.py:346
  92.9 1.3 %collective-permute-start.23 = (bf16[256,128]{1,0:T(8,128)(2,1)S(1)}, bf16[256,128]{1,0:T(8,128)(2,1)S(1)}, u32[]{:S(2)}, u32[]{:S(2)}) collective-permute-start(bf16[256,128]{1,0:T(8,128)(2,1)S(1)} %collective-permute-done.19.a3_ref), channel_id=1, source_target_pairs={{0,1},{1,0},{2,3},{3,2},{4,5},{5,4},{6,7},{7,6},{8,9},{9,8},{10,11... | collective-permute-start | bytes 196616 | tf_op jit(solution)/shard_map/ppermute | solution.py:346
  95.7 11.4 %collective-permute-start.26 = (bf16[128,1152]{1,0:T(8,128)(2,1)S(1)}, bf16[128,1152]{1,0:T(8,128)(2,1)S(1)}, u32[]{:S(2)}, u32[]{:S(2)}) collective-permute-start(bf16[128,1152]{1,0:T(8,128)(2,1)S(1)} %get-tuple-element.71), channel_id=1, source_target_pairs={{0,16},{1,17},{2,18},{3,19},{4,20},{5,21},{6,22},{7,23},{8,24},{9,... | collective-permute-start | bytes 884744 | tf_op jit(solution)/shard_map/ppermute | solution.py:401
  96.6 13.6 %collective-permute-start.27 = (bf16[128,1152]{1,0:T(8,128)(2,1)S(1)}, bf16[128,1152]{1,0:T(8,128)(2,1)S(1)}, u32[]{:S(2)}, u32[]{:S(2)}) collective-permute-start(bf16[128,1152]{1,0:T(8,128)(2,1)S(1)} %get-tuple-element.72), channel_id=1, source_target_pairs={{0,8},{1,9},{2,10},{3,11},{4,12},{5,13},{6,14},{7,15},{8,16},{9,17... | collective-permute-start | bytes 884744 | tf_op jit(solution)/shard_map/ppermute | solution.py:401
  97.7 14.9 %collective-permute-start.28 = (bf16[128,1152]{1,0:T(8,128)(2,1)S(1)}, bf16[128,1152]{1,0:T(8,128)(2,1)S(1)}, u32[]{:S(2)}, u32[]{:S(2)}) collective-permute-start(bf16[128,1152]{1,0:T(8,128)(2,1)S(1)} %get-tuple-element.73), channel_id=1, source_target_pairs={{0,24},{1,25},{2,26},{3,27},{4,28},{5,29},{6,30},{7,31},{8,0},{9,1... | collective-permute-start | bytes 884744 | tf_op jit(solution)/shard_map/ppermute | solution.py:401
  113.4 9.4 %collective-permute-start.29 = (bf16[32,1152]{1,0:T(8,128)(2,1)S(1)}, bf16[32,1152]{1,0:T(8,128)(2,1)S(1)}, u32[]{:S(2)}, u32[]{:S(2)}) collective-permute-start(bf16[32,1152]{1,0:T(8,128)(2,1)S(1)} %get-tuple-element.75), channel_id=1, source_target_pairs={{0,4},{1,5},{2,6},{3,7},{4,0},{5,1},{6,2},{7,3},{8,12},{9,13},{10,... | collective-permute-start | bytes 221192 | tf_op jit(solution)/shard_map/ppermute | solution.py:406
  117.4 6.5 %collective-permute-start.30 = (bf16[32,1152]{1,0:T(8,128)(2,1)S(1)}, bf16[32,1152]{1,0:T(8,128)(2,1)S(1)}, u32[]{:S(2)}, u32[]{:S(2)}) collective-permute-start(bf16[32,1152]{1,0:T(8,128)(2,1)S(1)} %get-tuple-element.76), channel_id=1, source_target_pairs={{0,2},{1,3},{2,4},{3,5},{4,6},{5,7},{6,0},{7,1},{8,10},{9,11},{10,... | collective-permute-start | bytes 221192 | tf_op jit(solution)/shard_map/ppermute | solution.py:406
  117.4 6.5 %collective-permute-start.31 = (bf16[32,1152]{1,0:T(8,128)(2,1)S(1)}, bf16[32,1152]{1,0:T(8,128)(2,1)S(1)}, u32[]{:S(2)}, u32[]{:S(2)}) collective-permute-start(bf16[32,1152]{1,0:T(8,128)(2,1)S(1)} %get-tuple-element.77), channel_id=1, source_target_pairs={{0,6},{1,7},{2,0},{3,1},{4,2},{5,3},{6,4},{7,5},{8,14},{9,15},{10,... | collective-permute-start | bytes 221192 | tf_op jit(solution)/shard_map/ppermute | solution.py:406

commit v3 on v2

--- a/solution.py
+++ b/solution.py
@@ -116,7 +116,13 @@
     )(side, features)
 
 
-def sums_kernel(d, pos_ref, table_ref, pat0_ref, pat1_ref, feat0_ref, feat1_ref, even_ref, odd_ref, *scratch):
+def sums_kernel(d, pos_ref, table_ref, pat0_ref, pat1_ref, feat0_ref, feat1_ref, *rest):
+    if not d:
+        seed_ref, w_ref, bias_ref, even_ref, odd_ref, self_ref, *scratch = rest
+        bias = jnp.where(pos_ref[4] == 0, bias_ref[...], 0.0)
+        self_ref[...] = F32(seed_ref[...], w_ref[...], (((1,), (0,)), ((), ()))) + bias
+    else:
+        even_ref, odd_ref, *scratch = rest
     tiles, accs, pops, pats, feats, done = scratch[0:2], scratch[2:4], scratch[4:7], scratch[7:9], scratch[9:11], scratch[11]
     blocks = pats[0].shape[0]
     first = lax.rem(pos_ref[0] + d, NX) * blocks
@@ -169,15 +175,16 @@
             finish(step - 2, accs[(step - 2) % 2], pops[(step - 2) % 3])
 
 
-def sums(d, pos, table, pat0, pat1, feat0, feat1):
+def sums(d, pos, table, pat0, pat1, feat0, feat1, *more):
     blocks = 2 * NZ
     rows, kind = (HALF + 16, jnp.int16) if d else (HALF + 8, jnp.float32)
     nodes = feat0.shape[0]
     return pl.pallas_call(
         functools.partial(sums_kernel, d),
-        out_shape=[jax.ShapeDtypeStruct((NZ, rows, BLK), kind)] * 2,
-        in_specs=[SMEM] * 2 + [pl.BlockSpec(memory_space=pl.ANY)] * 4,
-        out_specs=[VMEM] * 2,
+        out_shape=[jax.ShapeDtypeStruct((NZ, rows, BLK), kind)] * 2
+        + [jax.ShapeDtypeStruct((BLK, weights.shape[1]), jnp.float32) for weights in more[1:2]],
+        in_specs=[SMEM] * 2 + [pl.BlockSpec(memory_space=pl.ANY)] * 4 + [VMEM] * len(more),
+        out_specs=[VMEM] * (3 if more else 2),
         scratch_shapes=[pltpu.VMEM((2 * FAN * BLK, BLK), jnp.bfloat16)] * 2
         + [pltpu.VMEM((HALF, BLK), jnp.float32)] * 2
         + [pltpu.VMEM((8, BLK), jnp.int32)] * 3
@@ -187,7 +194,7 @@
         compiler_params=ALONE,
         cost_estimate=pl.CostEstimate(flops=2_000_000_000, bytes_accessed=3_000_000, transcendentals=0),
         name="sums",
-    )(pos, table, pat0, pat1, feat0, feat1)
+    )(pos, table, pat0, pat1, feat0, feat1, *more)
 
 
 def call(kernel, name, outs, count, scratch=(), waits=0, params=PARAMS):
@@ -341,7 +348,7 @@
     feat = lax.axis_index("feat")
     x, z, core = node // (NZ * 2), (node // 2) % NZ, node % 2
     y = feat % NY
-    pos = jnp.stack([x, z, core, y]).astype(jnp.int32)
+    pos = jnp.stack([x, z, core, y, feat]).astype(jnp.int32)
     hid = w_self.shape[1]
     swap = lambda value: lax.ppermute(value, "node", SWAP_CORE)
 
@@ -354,30 +361,28 @@
 
     made = {}
     for d in (2, 1, 3, 0):
-        made[d] = sums(d, pos, table, packed, packed_other, features, other)
+        more = () if d else (seed_feats, w_self, bias_term[None])
+        made[d] = sums(d, pos, table, packed, packed_other, features, other, *more)
     far = [lax.ppermute(part, "node", shift_x(d)) for d in (2, 1, 3) for part in made[d]]
 
-    seed_feats, w_self, bias_term, out_grad, own = lax.optimization_barrier(
-        (seed_feats, w_self, bias_term, out_grad, made[0])
-    )
+    *own, self_term = made[0]
+    seed_feats, out_grad, own = lax.optimization_barrier((seed_feats, out_grad, own))
     turned = seed_feats.T.reshape(WIDE // 32, 2, 16, BLK)
     pick = lambda c: lax.dynamic_index_in_dim(turned, c, 1, keepdims=False).reshape(HALF, BLK)
     seed_mine, seed_other = pick(core), swap(pick(1 - core))
     og_other = swap(out_grad)
-    self_term = jnp.dot(seed_feats, w_self, preferred_element_type=jnp.float32)
-    self_term = self_term + jnp.where(feat == 0, bias_term, 0.0)
 
     own, *coded = call(merge_x_kernel, "merge_x", [SUM_PLAIN] + [SUM_CODED] * 3, 8, params=ALONE)(
         pos, *far, *own
     )
     arrived = [lax.ppermute(coded[d - 1], "node", shift_z(d)) for d in (2, 1, 3)]
     mine, give, rest = call(
-        merge_z_kernel, "merge_z", [HALF16, shaped(HALF + BLK, BLK, jnp.bfloat16), shaped(BLK, BLK, jnp.bfloat16)], 4
+        merge_z_kernel, "merge_z", [HALF16, shaped(HALF + BLK, BLK, jnp.bfloat16), shaped(BLK, BLK, jnp.bfloat16)], 4, params=ALONE
     )(pos, *arrived, own)
 
     *coded, agg_mine, agg_other = call(
         pre_kernel, "pre_terms", [PLAIN] + [CODED] * 3 + [HALF16] * 2, 5,
-        [pltpu.VMEM((WIDE, BLK), jnp.bfloat16), pltpu.VMEM((hid, BLK), jnp.float32)],
+        [pltpu.VMEM((WIDE, BLK), jnp.bfloat16), pltpu.VMEM((hid, BLK), jnp.float32)], params=ALONE,
     )(pos, mine, swap(give), rest, w_neigh, self_term)
     own, *coded = coded
     received = [lax.ppermute(coded[d - 1], "feat", shift_y(d)) for d in (2, 1, 3)]

time: 126 us -> 131 us (1.040)
  Pallas kernels: 34.1 us -> 37.7 us
  local copies, waits for them, and re-layouts: 1.36 us -> 4.88 us
  matrix products: 1.54 us -> 0 us
    unnamed x21 -> x29, local copies, waits for them, and re-layouts: 1.07 us -> 3.98 us
    pallas_call x1, Pallas kernels: 1.13 us -> 2.73 us  [body(): call(pre_kernel, 'pre_terms', [PLAIN] + [CODED] * 3 + [HALF16] * 2, 5, [p...]
    ppermute x10, waiting for transfers between devices: 2.54 us -> 4.08 us  [body(): swap = lambda value: lax.ppermute(value, 'node', SWAP_CORE)]
    dot_general x1 -> x0, matrix products: 1.54 us -> none  [body(): self_term = jnp.dot(seed_feats, w_self, preferred_element_type=jnp.float32)]
  transfers between devices with their start and end apart: 32 -> 32, of which waited for: 17 -> 18; matrix products, arithmetic and copies ran while one was open for 3% -> 1% of each run, Pallas kernels for 16% -> 16%
where the time goes in v3:
time: 131 us
  starting transfers between devices  43.6 us (33%)
  waiting for transfers between devices  43.1 us (33%)
  Pallas kernels  37.7 us (29%)
  local copies, waits for them, and re-layouts  4.88 us (4%)
    pallas_call x4, Pallas kernels, sums(): pl.pallas_call(functools.partial(sums_kernel, d), out_shape=[jax.ShapeDty...  23 us
    ppermute x3, waiting for transfers between devices, body(): lax.ppermute(parts[d - 1], 'node', shift_x(d))  14 us
    ppermute x6, starting transfers between devices, body(): lax.ppermute(part, 'node', shift_x(d))  8.31 us
    ppermute x3, starting transfers between devices, body(): lax.ppermute(parts[d - 1], 'node', shift_z(d))  7.98 us
    ppermute x6, waiting for transfers between devices, body(): lax.ppermute(part, 'node', shift_x(d))  7.07 us
    ppermute x3, starting transfers between devices, body(): lax.ppermute(coded[d - 1], 'node', shift_z(d))  6.49 us
    ppermute x3, starting transfers between devices, body(): lax.ppermute(coded[d - 1], 'feat', shift_y(d))  6.28 us
    ppermute x3, waiting for transfers between devices, body(): lax.ppermute(coded[d - 1], 'node', shift_z(d))  6.25 us
  transfers between devices with their start and end apart: 32, of which 18 were waited for; matrix products, arithmetic and copies ran while one was open for 1% of the time, Pallas kernels for 16%

profile of v3, /device:TPU:6, one launch (start us, length us, event | category | flops | bytes accessed | tf_op | source)
XLA Modules:
  0.0 130.9 jit_solution(12237831711907542806)
XLA Ops:
  0.7 0.1 collective-permute-start.1
  0.8 2.1 %half_columns.1 = bf16[2048,256]{1,0:T(8,128)(2,1)} custom-call(s32[1]{0:T(128)} %bitcast.6.side_ref, bf16[2048,512]{1,0:T(8,128)(2,1)} %feat0_ref.7), custom_call_target="tpu_custom_call" | custom-call | tf_op jit(solution)/shard_map/half_columns/pallas_call | solution.py:108
  2.9 0.6 collective-permute-start.2
  3.5 0.1 reshape.22
  3.8 0.6 stack.23.pos_ref
  4.4 1.3 %collective-permute-done = s32[288]{0:T(512)S(1)} collective-permute-done((s32[288]{0:T(512)S(1)}, s32[288]{0:T(512)S(1)}, u32[]{:S(2)}, u32[]{:S(2)}) %collective-permute-start) | collective-permute-done | bytes 1184 | tf_op jit(solution)/shard_map/ppermute | solution.py:353
  5.8 0.7 pad_add_fusion.table_ref
  6.5 5.5 %sums.4 = (s16[4,272,128]{2,1,0:T(8,128)(2,1)}, s16[4,272,128]{2,1,0:T(8,128)(2,1)}) custom-call(s32[5]{0:T(128)} %stack.23.pos_ref, s32[576]{0:T(1024)} %pad_add_fusion.table_ref, s32[32,8,8,128]{3,2,1,0:T(8,128)} %bitcast.18, s32[32,8,8,128]{3,2,1,0:T(8,128)} %collective-permute-done.1.pat1_ref, bf16[2048,512]{1,0:T(8,128)(2,1)} %feat0_ref.7, ...), custom_call_target="tpu_custom_call" | custom-call | flops 2000000000 | bytes 3000000 | tf_op jit(solution)/shard_map/sums/pallas_call | solution.py:182
  12.0 1.5 %collective-permute-start.3 = (s16[4,272,128]{2,1,0:T(8,128)(2,1)}, s16[4,272,128]{2,1,0:T(8,128)(2,1)S(1)}, u32[]{:S(2)}, u32[]{:S(2)}) collective-permute-start(s16[4,272,128]{2,1,0:T(8,128)(2,1)} %get-tuple-element.42), channel_id=1, source_target_pairs={{0,16},{1,17},{2,18},{3,19},{4,20},{5,21},{6,22},{7,23},{8,24},{9,... | collective-permute-start | bytes 835592 | tf_op jit(solution)/shard_map/ppermute | solution.py:366
  13.5 2.1 %collective-permute-start.4 = (s16[4,272,128]{2,1,0:T(8,128)(2,1)}, s16[4,272,128]{2,1,0:T(8,128)(2,1)S(1)}, u32[]{:S(2)}, u32[]{:S(2)}) collective-permute-start(s16[4,272,128]{2,1,0:T(8,128)(2,1)} %get-tuple-element.43), channel_id=1, source_target_pairs={{0,16},{1,17},{2,18},{3,19},{4,20},{5,21},{6,22},{7,23},{8,24},{9,... | collective-permute-start | bytes 835592 | tf_op jit(solution)/shard_map/ppermute | solution.py:366
  15.7 5.5 %sums.5 = (s16[4,272,128]{2,1,0:T(8,128)(2,1)}, s16[4,272,128]{2,1,0:T(8,128)(2,1)}) custom-call(s32[5]{0:T(128)} %stack.23.pos_ref, s32[576]{0:T(1024)} %pad_add_fusion.table_ref, s32[32,8,8,128]{3,2,1,0:T(8,128)} %bitcast.19, s32[32,8,8,128]{3,2,1,0:T(8,128)} %collective-permute-done.1.pat1_ref, bf16[2048,512]{1,0:T(8,128)(2,1)} %feat0_ref.7, ...), custom_call_target="tpu_custom_call" | custom-call | flops 2000000000 | bytes 3000000 | tf_op jit(solution)/shard_map/sums/pallas_call | solution.py:182
  21.2 2.3 %collective-permute-start.5 = (s16[4,272,128]{2,1,0:T(8,128)(2,1)}, s16[4,272,128]{2,1,0:T(8,128)(2,1)}, u32[]{:S(2)}, u32[]{:S(2)}) collective-permute-start(s16[4,272,128]{2,1,0:T(8,128)(2,1)} %get-tuple-element.44), channel_id=1, source_target_pairs={{0,8},{1,9},{2,10},{3,11},{4,12},{5,13},{6,14},{7,15},{8,16},{9,17... | collective-permute-start | bytes 835592 | tf_op jit(solution)/shard_map/ppermute | solution.py:366
  23.5 0.1 collective-permute-start.6
  23.6 5.5 %sums.6 = (s16[4,272,128]{2,1,0:T(8,128)(2,1)}, s16[4,272,128]{2,1,0:T(8,128)(2,1)}) custom-call(s32[5]{0:T(128)} %stack.23.pos_ref, s32[576]{0:T(1024)} %pad_add_fusion.table_ref, s32[32,8,8,128]{3,2,1,0:T(8,128)} %bitcast.20, s32[32,8,8,128]{3,2,1,0:T(8,128)} %collective-permute-done.1.pat1_ref, bf16[2048,512]{1,0:T(8,128)(2,1)} %feat0_ref.7, ...), custom_call_target="tpu_custom_call" | custom-call | flops 2000000000 | bytes 3000000 | tf_op jit(solution)/shard_map/sums/pallas_call | solution.py:182
  29.1 2.2 %collective-permute-start.7 = (s16[4,272,128]{2,1,0:T(8,128)(2,1)}, s16[4,272,128]{2,1,0:T(8,128)(2,1)}, u32[]{:S(2)}, u32[]{:S(2)}) collective-permute-start(s16[4,272,128]{2,1,0:T(8,128)(2,1)} %get-tuple-element.46), channel_id=1, source_target_pairs={{0,24},{1,25},{2,26},{3,27},{4,28},{5,29},{6,30},{7,31},{8,0},{9,1... | collective-permute-start | bytes 835592 | tf_op jit(solution)/shard_map/ppermute | solution.py:366
  31.3 0.1 collective-permute-start.8
  31.4 6.4 %sums.7 = (f32[4,264,128]{2,1,0:T(8,128)}, f32[4,264,128]{2,1,0:T(8,128)}, f32[128,1024]{1,0:T(8,128)}) custom-call(s32[5]{0:T(128)} %stack.23.pos_ref, s32[576]{0:T(1024)} %pad_add_fusion.table_ref, s32[32,8,8,128]{3,2,1,0:T(8,128)} %bitcast.21, s32[32,8,8,128]{3,2,1,0:T(8,128)} %collective-permute-done.1.pat1_ref, bf16[2048,512]{1,0:T(8,128)(2,1)} %feat0_ref.7, ...), custom_call_target="tpu_custom_call" | custom-call | flops 2000000000 | bytes 3000000 | tf_op jit(solution)/shard_map/sums/pallas_call | solution.py:182
  37.9 2.5 %collective-permute-done.6.rest_3_ = s16[4,272,128]{2,1,0:T(8,128)(2,1)} collective-permute-done((s16[4,272,128]{2,1,0:T(8,128)(2,1)}, s16[4,272,128]{2,1,0:T(8,128)(2,1)}, u32[]{:S(2)}, u32[]{:S(2)}) %collective-permute-start.6) | collective-permute-done | bytes 278560 | tf_op jit(solution)/shard_map/ppermute | solution.py:366
  40.4 0.1 collective-permute-done.7.rest_4_
  40.5 4.5 %collective-permute-done.8.rest_5_ = s16[4,272,128]{2,1,0:T(8,128)(2,1)} collective-permute-done((s16[4,272,128]{2,1,0:T(8,128)(2,1)}, s16[4,272,128]{2,1,0:T(8,128)(2,1)}, u32[]{:S(2)}, u32[]{:S(2)}) %collective-permute-start.8) | collective-permute-done | bytes 278560 | tf_op jit(solution)/shard_map/ppermute | solution.py:366
  44.9 3.0 %merge_x.1 = (f32[2,264,128]{2,1,0:T(8,128)}, s16[2,272,128]{2,1,0:T(8,128)(2,1)}, s16[2,272,128]{2,1,0:T(8,128)(2,1)}, s16[2,272,128]{2,1,0:T(8,128)(2,1)}) custom-call(s32[5]{0:T(128)} %stack.23.pos_ref, s16[4,272,128]{2,1,0:T(8,128)(2,1)} %copy-done.5, s16[4,272,128]{2,1,0:T(8,128)(2,1)} %copy-done.6, s16[4,272,128]{2,1,0:T(8,128)(2,1)} %collective-permute-done.5.rest_2_, ...), custom_call_target="tpu_custom_call" | custom-call | tf_op jit(solution)/shard_map/merge_x/pallas_call | solution.py:375
  48.0 2.7 %collective-permute-start.9 = (s16[2,272,128]{2,1,0:T(8,128)(2,1)}, s16[2,272,128]{2,1,0:T(8,128)(2,1)S(1)}, u32[]{:S(2)}, u32[]{:S(2)}) collective-permute-start(s16[2,272,128]{2,1,0:T(8,128)(2,1)} %get-tuple-element.52), channel_id=1, source_target_pairs={{0,4},{1,5},{2,6},{3,7},{4,0},{5,1},{6,2},{7,3},{8,12},{9,13},{10,... | collective-permute-start | bytes 417800 | tf_op jit(solution)/shard_map/ppermute | solution.py:378
  50.6 1.9 %collective-permute-start.10 = (s16[2,272,128]{2,1,0:T(8,128)(2,1)}, s16[2,272,128]{2,1,0:T(8,128)(2,1)S(1)}, u32[]{:S(2)}, u32[]{:S(2)}) collective-permute-start(s16[2,272,128]{2,1,0:T(8,128)(2,1)} %get-tuple-element.53), channel_id=1, source_target_pairs={{0,2},{1,3},{2,4},{3,5},{4,6},{5,7},{6,0},{7,1},{8,10},{9,11},{10,... | collective-permute-start | bytes 417800 | tf_op jit(solution)/shard_map/ppermute | solution.py:378
  52.6 1.9 %collective-permute-start.11 = (s16[2,272,128]{2,1,0:T(8,128)(2,1)}, s16[2,272,128]{2,1,0:T(8,128)(2,1)S(1)}, u32[]{:S(2)}, u32[]{:S(2)}) collective-permute-start(s16[2,272,128]{2,1,0:T(8,128)(2,1)} %get-tuple-element.54), channel_id=1, source_target_pairs={{0,6},{1,7},{2,0},{3,1},{4,2},{5,3},{6,4},{7,5},{8,14},{9,15},{10,... | collective-permute-start | bytes 417800 | tf_op jit(solution)/shard_map/ppermute | solution.py:378
  54.5 6.0 %collective-permute-done.9.r1_ref = s16[2,272,128]{2,1,0:T(8,128)(2,1)S(1)} collective-permute-done((s16[2,272,128]{2,1,0:T(8,128)(2,1)}, s16[2,272,128]{2,1,0:T(8,128)(2,1)S(1)}, u32[]{:S(2)}, u32[]{:S(2)}) %collective-permute-start.9) | collective-permute-done | bytes 139296 | tf_op jit(solution)/shard_map/ppermute | solution.py:378
  60.5 0.2 collective-permute-done.11.r3_ref
  60.7 0.4 copy-done.7
  61.2 0.2 copy-done.9
  61.4 2.0 %merge_z.1 = (bf16[256,128]{1,0:T(8,128)(2,1)}, bf16[384,128]{1,0:T(8,128)(2,1)}, bf16[128,128]{1,0:T(8,128)(2,1)}) custom-call(s32[5]{0:T(128)} %stack.23.pos_ref, s16[2,272,128]{2,1,0:T(8,128)(2,1)} %copy-done.7, s16[2,272,128]{2,1,0:T(8,128)(2,1)} %copy-done.8, s16[2,272,128]{2,1,0:T(8,128)(2,1)} %copy-done.9, f32[2,264,128]{2,1,0:T(8,128)} %get-tuple-element.55.own_ref), custom_call_target="tpu_custom_call" | custom-call | tf_op jit(solution)/shard_map/merge_z/pallas_call | solution.py:379
  63.3 1.5 %collective-permute-done.12.got_ref = bf16[384,128]{1,0:T(8,128)(2,1)S(1)} collective-permute-done((bf16[384,128]{1,0:T(8,128)(2,1)}, bf16[384,128]{1,0:T(8,128)(2,1)S(1)}, u32[]{:S(2)}, u32[]{:S(2)}) %collective-permute-start.12) | collective-permute-done | bytes 98336 | tf_op jit(solution)/shard_map/ppermute | solution.py:353
  64.9 0.6 copy-done.11
  65.5 2.7 %pre_terms.1 = (f32[264,128]{1,0:T(8,128)}, s16[272,128]{1,0:T(8,128)(2,1)}, s16[272,128]{1,0:T(8,128)(2,1)}, s16[272,128]{1,0:T(8,128)(2,1)}, bf16[256,128]{1,0:T(8,128)(2,1)}, /*index=5*/bf16[256,128]{1,0:T(8,128)(2,1)}) custom-call(s32[5]{0:T(128)} %stack.23.pos_ref, bf16[256,128]{1,0:T(8,128)(2,1)} %get-tuple-element.56.mine_ref, ...), custom_call_target="tpu_custom_call" | custom-call | tf_op jit(solution)/shard_map/pre_terms/pallas_call | solution.py:383
  68.2 3.0 %collective-permute-start.13 = (s16[272,128]{1,0:T(8,128)(2,1)}, s16[272,128]{1,0:T(8,128)(2,1)S(1)}, u32[]{:S(2)}, u32[]{:S(2)}) collective-permute-start(s16[272,128]{1,0:T(8,128)(2,1)} %get-tuple-element.60), channel_id=1, source_target_pairs={{0,64},{32,96},{64,0},{96,32},{128,192},{160,224},{192,128},{224,1... | collective-permute-start | bytes 208904 | tf_op jit(solution)/shard_map/ppermute | solution.py:388
  71.3 0.7 collective-permute-start.14
  72.0 2.5 %collective-permute-start.15 = (s16[272,128]{1,0:T(8,128)(2,1)}, s16[272,128]{1,0:T(8,128)(2,1)S(1)}, u32[]{:S(2)}, u32[]{:S(2)}) collective-permute-start(s16[272,128]{1,0:T(8,128)(2,1)} %get-tuple-element.62), channel_id=1, source_target_pairs={{0,96},{32,0},{64,32},{96,64},{128,224},{160,128},{192,160},{224,1... | collective-permute-start | bytes 208904 | tf_op jit(solution)/shard_map/ppermute | solution.py:388
  74.5 0.1 copy.16
  74.7 2.3 %collective-permute-done.14.r2_ref = s16[272,128]{1,0:T(8,128)(2,1)S(1)} collective-permute-done((s16[272,128]{1,0:T(8,128)(2,1)}, s16[272,128]{1,0:T(8,128)(2,1)S(1)}, u32[]{:S(2)}, u32[]{:S(2)}) %collective-permute-start.14) | collective-permute-done | bytes 69664 | tf_op jit(solution)/shard_map/ppermute | solution.py:388
  77.0 0.9 copy-done.1
  77.9 0.6 merge_y.1.own_ref
  78.6 5.8 %collective-permute-start.16 = (s16[272,128]{1,0:T(8,128)(2,1)S(1)}, s16[272,128]{1,0:T(8,128)(2,1)S(1)}, u32[]{:S(2)}, u32[]{:S(2)}) collective-permute-start(s16[272,128]{1,0:T(8,128)(2,1)S(1)} %merge_y.1.own_ref), channel_id=1, source_target_pairs={{0,128},{32,160},{64,192},{96,224},{128,0},{160,32},{192,64},{224,... | collective-permute-start | bytes 208904 | tf_op jit(solution)/shard_map/ppermute | solution.py:390
  84.4 0.1 collective-permute-start.25
  84.5 2.4 %collective-permute-done.16.far_ref = s16[272,128]{1,0:T(8,128)(2,1)S(1)} collective-permute-done((s16[272,128]{1,0:T(8,128)(2,1)S(1)}, s16[272,128]{1,0:T(8,128)(2,1)S(1)}, u32[]{:S(2)}, u32[]{:S(2)}) %collective-permute-start.16) | collective-permute-done | bytes 69664 | tf_op jit(solution)/shard_map/ppermute | solution.py:390
  87.0 0.6 hidden.1.a0_ref
  87.6 0.6 collective-permute-start.17
  88.1 4.3 %collective-permute-start.18 = (bf16[256,128]{1,0:T(8,128)(2,1)S(1)}, bf16[256,128]{1,0:T(8,128)(2,1)S(1)}, u32[]{:S(2)}, u32[]{:S(2)}) collective-permute-start(bf16[256,128]{1,0:T(8,128)(2,1)S(1)} %hidden.1.a0_ref), channel_id=1, source_target_pairs={{0,64},{32,96},{64,0},{96,32},{128,192},{160,224},{192,128},{224,1... | collective-permute-start | bytes 196616 | tf_op jit(solution)/shard_map/ppermute | solution.py:392
  92.5 0.9 collective-permute-done.17.a1_ref
  93.4 2.1 %collective-permute-done.18.a2_ref = bf16[256,128]{1,0:T(8,128)(2,1)S(1)} collective-permute-done((bf16[256,128]{1,0:T(8,128)(2,1)S(1)}, bf16[256,128]{1,0:T(8,128)(2,1)S(1)}, u32[]{:S(2)}, u32[]{:S(2)}) %collective-permute-start.18) | collective-permute-done | bytes 65568 | tf_op jit(solution)/shard_map/ppermute | solution.py:392
  95.4 1.3 %collective-permute-done.19.a3_ref = bf16[256,128]{1,0:T(8,128)(2,1)S(1)} collective-permute-done((bf16[256,128]{1,0:T(8,128)(2,1)S(1)}, bf16[256,128]{1,0:T(8,128)(2,1)S(1)}, u32[]{:S(2)}, u32[]{:S(2)}) %collective-permute-start.19) | collective-permute-done | bytes 65568 | tf_op jit(solution)/shard_map/ppermute | solution.py:392
  96.8 1.2 collective-permute-done.23.b3_ref
  98.0 0.8 copy-done.2
  98.8 0.8 copy-done.3
  99.7 1.6 %grads.1 = (bf16[128,1024]{1,0:T(8,128)(2,1)}, f32[128,1152]{1,0:T(8,128)S(1)}, bf16[128,1152]{1,0:T(8,128)(2,1)S(1)}, bf16[128,1152]{1,0:T(8,128)(2,1)S(1)}, bf16[128,1152]{1,0:T(8,128)(2,1)S(1)}) custom-call(s32[5]{0:T(128)S(1)} %copy-done.4, bf16[256,128]{1,0:T(8,128)(2,1)S(1)} %hidden.1.a0_ref, bf16[256,128]{1,0:T(8,128)(2,1)S(1)} %collective-permute-done.17.a1_ref, ...), custom_call_target="tpu_custom_call" | custom-call | tf_op jit(solution)/shard_map/grads/pallas_call | solution.py:403
  101.2 0.9 collective-permute-start.26
  102.2 1.1 collective-permute-start.27
  103.2 0.9 collective-permute-start.28
  104.2 8.5 %collective-permute-done.26.r1_ref = bf16[128,1152]{1,0:T(8,128)(2,1)S(1)} collective-permute-done((bf16[128,1152]{1,0:T(8,128)(2,1)S(1)}, bf16[128,1152]{1,0:T(8,128)(2,1)S(1)}, u32[]{:S(2)}, u32[]{:S(2)}) %collective-permute-start.26) | collective-permute-done | bytes 294944 | tf_op jit(solution)/shard_map/ppermute | solution.py:406
  112.7 3.1 %collective-permute-done.27.r2_ref = bf16[128,1152]{1,0:T(8,128)(2,1)S(1)} collective-permute-done((bf16[128,1152]{1,0:T(8,128)(2,1)S(1)}, bf16[128,1152]{1,0:T(8,128)(2,1)S(1)}, u32[]{:S(2)}, u32[]{:S(2)}) %collective-permute-start.27) | collective-permute-done | bytes 294944 | tf_op jit(solution)/shard_map/ppermute | solution.py:406
  115.8 2.3 %collective-permute-done.28.r3_ref = bf16[128,1152]{1,0:T(8,128)(2,1)S(1)} collective-permute-done((bf16[128,1152]{1,0:T(8,128)(2,1)S(1)}, bf16[128,1152]{1,0:T(8,128)(2,1)S(1)}, u32[]{:S(2)}, u32[]{:S(2)}) %collective-permute-start.28) | collective-permute-done | bytes 294944 | tf_op jit(solution)/shard_map/ppermute | solution.py:406
  118.1 0.8 fold_x.1
  118.9 4.2 %collective-permute-start.29 = (bf16[32,1152]{1,0:T(8,128)(2,1)S(1)}, bf16[32,1152]{1,0:T(8,128)(2,1)S(1)}, u32[]{:S(2)}, u32[]{:S(2)}) collective-permute-start(bf16[32,1152]{1,0:T(8,128)(2,1)S(1)} %get-tuple-element.73), channel_id=1, source_target_pairs={{0,4},{1,5},{2,6},{3,7},{4,0},{5,1},{6,2},{7,3},{8,12},{9,13},{10,... | collective-permute-start | bytes 221192 | tf_op jit(solution)/shard_map/ppermute | solution.py:411
  123.1 3.8 %collective-permute-start.31 = (bf16[32,1152]{1,0:T(8,128)(2,1)S(1)}, bf16[32,1152]{1,0:T(8,128)(2,1)S(1)}, u32[]{:S(2)}, u32[]{:S(2)}) collective-permute-start(bf16[32,1152]{1,0:T(8,128)(2,1)S(1)} %get-tuple-element.75), channel_id=1, source_target_pairs={{0,6},{1,7},{2,0},{3,1},{4,2},{5,3},{6,4},{7,5},{8,14},{9,15},{10,... | collective-permute-start | bytes 221192 | tf_op jit(solution)/shard_map/ppermute | solution.py:411
  126.9 1.6 %collective-permute-done.29.r1_ref = bf16[32,1152]{1,0:T(8,128)(2,1)S(1)} collective-permute-done((bf16[32,1152]{1,0:T(8,128)(2,1)S(1)}, bf16[32,1152]{1,0:T(8,128)(2,1)S(1)}, u32[]{:S(2)}, u32[]{:S(2)}) %collective-permute-start.29) | collective-permute-done | bytes 73760 | tf_op jit(solution)/shard_map/ppermute | solution.py:411
  128.5 1.2 collective-permute-done.30.r2_ref
  129.6 1.3 last.1
  (50 shorter events, 0.4 us)
Async XLA Ops:
  0.6 2.8 %copy-start.12 = (s32[32,8]{0,1:T(8,128)S(1)}, s32[32,8]{0,1:T(8,128)}, u32[]{:S(2)}) copy-start(s32[32,8]{0,1:T(8,128)} %param.12) | copy-start | bytes 3076
  0.6 3.0 %copy-start.13 = (s32[32]{0:T(128)S(1)}, s32[32]{0:T(128)}, u32[]{:S(2)}) copy-start(s32[32]{0:T(128)} %param.13) | copy-start | bytes 388
  0.7 5.8 %collective-permute-start.1 = (s32[32,8,8,128]{3,2,1,0:T(8,128)}, s32[32,8,8,128]{3,2,1,0:T(8,128)}, u32[]{:S(2)}, u32[]{:S(2)}) collective-permute-start(s32[32,8,8,128]{3,2,1,0:T(8,128)} %bitcast.17), channel_id=1, source_target_pairs={{0,1},{1,0},{2,3},{3,2},{4,5},{5,4},{6,7},{7,6},{8,9},{9,8},{10,11... | collective-permute-start | bytes 3145736 | tf_op jit(solution)/shard_map/ppermute | solution.py:353
  2.9 3.6 %collective-permute-start.2 = (bf16[2048,256]{1,0:T(8,128)(2,1)}, bf16[2048,256]{1,0:T(8,128)(2,1)}, u32[]{:S(2)}, u32[]{:S(2)}) collective-permute-start(bf16[2048,256]{1,0:T(8,128)(2,1)} %half_columns.1), channel_id=1, source_target_pairs={{0,1},{1,0},{2,3},{3,2},{4,5},{5,4},{6,7},{7,6},{8,9},{9,8},{10,11... | collective-permute-start | bytes 3145736 | tf_op jit(solution)/shard_map/ppermute | solution.py:353
  3.7 2.0 %collective-permute-start = (s32[288]{0:T(512)S(1)}, s32[288]{0:T(512)S(1)}, u32[]{:S(2)}, u32[]{:S(2)}) collective-permute-start(s32[288]{0:T(512)S(1)} %pad_add_fusion.1), channel_id=1, source_target_pairs={{0,1},{1,0},{2,3},{3,2},{4,5},{5,4},{6,7},{7,6},{8,9},{9,8},{10,11... | collective-permute-start | bytes 3464 | tf_op jit(solution)/shard_map/ppermute | solution.py:353
  12.0 19.3 %collective-permute-start.3 = (s16[4,272,128]{2,1,0:T(8,128)(2,1)}, s16[4,272,128]{2,1,0:T(8,128)(2,1)S(1)}, u32[]{:S(2)}, u32[]{:S(2)}) collective-permute-start(s16[4,272,128]{2,1,0:T(8,128)(2,1)} %get-tuple-element.42), channel_id=1, source_target_pairs={{0,16},{1,17},{2,18},{3,19},{4,20},{5,21},{6,22},{7,23},{8,24},{9,... | collective-permute-start | bytes 835592 | tf_op jit(solution)/shard_map/ppermute | solution.py:366
  13.5 24.3 %collective-permute-start.4 = (s16[4,272,128]{2,1,0:T(8,128)(2,1)}, s16[4,272,128]{2,1,0:T(8,128)(2,1)S(1)}, u32[]{:S(2)}, u32[]{:S(2)}) collective-permute-start(s16[4,272,128]{2,1,0:T(8,128)(2,1)} %get-tuple-element.43), channel_id=1, source_target_pairs={{0,16},{1,17},{2,18},{3,19},{4,20},{5,21},{6,22},{7,23},{8,24},{9,... | collective-permute-start | bytes 835592 | tf_op jit(solution)/shard_map/ppermute | solution.py:366
  21.2 16.7 %collective-permute-start.5 = (s16[4,272,128]{2,1,0:T(8,128)(2,1)}, s16[4,272,128]{2,1,0:T(8,128)(2,1)}, u32[]{:S(2)}, u32[]{:S(2)}) collective-permute-start(s16[4,272,128]{2,1,0:T(8,128)(2,1)} %get-tuple-element.44), channel_id=1, source_target_pairs={{0,8},{1,9},{2,10},{3,11},{4,12},{5,13},{6,14},{7,15},{8,16},{9,17... | collective-permute-start | bytes 835592 | tf_op jit(solution)/shard_map/ppermute | solution.py:366
  23.5 16.9 %collective-permute-start.6 = (s16[4,272,128]{2,1,0:T(8,128)(2,1)}, s16[4,272,128]{2,1,0:T(8,128)(2,1)}, u32[]{:S(2)}, u32[]{:S(2)}) collective-permute-start(s16[4,272,128]{2,1,0:T(8,128)(2,1)} %get-tuple-element.45), channel_id=1, source_target_pairs={{0,8},{1,9},{2,10},{3,11},{4,12},{5,13},{6,14},{7,15},{8,16},{9,17... | collective-permute-start | bytes 835592 | tf_op jit(solution)/shard_map/ppermute | solution.py:366
  29.1 11.4 %collective-permute-start.7 = (s16[4,272,128]{2,1,0:T(8,128)(2,1)}, s16[4,272,128]{2,1,0:T(8,128)(2,1)}, u32[]{:S(2)}, u32[]{:S(2)}) collective-permute-start(s16[4,272,128]{2,1,0:T(8,128)(2,1)} %get-tuple-element.46), channel_id=1, source_target_pairs={{0,24},{1,25},{2,26},{3,27},{4,28},{5,29},{6,30},{7,31},{8,0},{9,1... | collective-permute-start | bytes 835592 | tf_op jit(solution)/shard_map/ppermute | solution.py:366
  31.3 6.5 %copy-start.5 = (s16[4,272,128]{2,1,0:T(8,128)(2,1)}, s16[4,272,128]{2,1,0:T(8,128)(2,1)S(1)}, u32[]{:S(2)}) copy-start(s16[4,272,128]{2,1,0:T(8,128)(2,1)S(1)} %collective-permute-done.3.rest_0_) | copy-start | bytes 835588
  31.3 13.6 %collective-permute-start.8 = (s16[4,272,128]{2,1,0:T(8,128)(2,1)}, s16[4,272,128]{2,1,0:T(8,128)(2,1)}, u32[]{:S(2)}, u32[]{:S(2)}) collective-permute-start(s16[4,272,128]{2,1,0:T(8,128)(2,1)} %get-tuple-element.47), channel_id=1, source_target_pairs={{0,24},{1,25},{2,26},{3,27},{4,28},{5,29},{6,30},{7,31},{8,0},{9,1... | collective-permute-start | bytes 835592 | tf_op jit(solution)/shard_map/ppermute | solution.py:366
  37.8 36.7 %copy-start = (bf16[128,1024]{1,0:T(8,128)(2,1)S(1)}, bf16[128,1024]{1,0:T(8,128)(2,1)}, u32[]{:S(2)}) copy-start(bf16[128,1024]{1,0:T(8,128)(2,1)} %og0_ref) | copy-start | bytes 786436
  37.8 36.7 %copy-start.10 = (bf16[128,512]{1,0:T(8,128)(2,1)S(1)}, bf16[128,512]{1,0:T(8,128)(2,1)}, u32[]{:S(2)}) copy-start(bf16[128,512]{1,0:T(8,128)(2,1)} %rest_0_.1) | copy-start | bytes 393220
  37.8 39.2 %copy-start.4 = (s32[5]{0:T(128)S(1)}, s32[5]{0:T(128)}, u32[]{:S(2)}) copy-start(s32[5]{0:T(128)} %stack.23.pos_ref) | copy-start | bytes 64
  37.8 7.1 %copy-start.6 = (s16[4,272,128]{2,1,0:T(8,128)(2,1)}, s16[4,272,128]{2,1,0:T(8,128)(2,1)S(1)}, u32[]{:S(2)}) copy-start(s16[4,272,128]{2,1,0:T(8,128)(2,1)S(1)} %collective-permute-done.4.rest_1_) | copy-start | bytes 835588
  48.0 12.5 %collective-permute-start.9 = (s16[2,272,128]{2,1,0:T(8,128)(2,1)}, s16[2,272,128]{2,1,0:T(8,128)(2,1)S(1)}, u32[]{:S(2)}, u32[]{:S(2)}) collective-permute-start(s16[2,272,128]{2,1,0:T(8,128)(2,1)} %get-tuple-element.52), channel_id=1, source_target_pairs={{0,4},{1,5},{2,6},{3,7},{4,0},{5,1},{6,2},{7,3},{8,12},{9,13},{10,... | collective-permute-start | bytes 417800 | tf_op jit(solution)/shard_map/ppermute | solution.py:378
  50.6 9.8 %collective-permute-start.10 = (s16[2,272,128]{2,1,0:T(8,128)(2,1)}, s16[2,272,128]{2,1,0:T(8,128)(2,1)S(1)}, u32[]{:S(2)}, u32[]{:S(2)}) collective-permute-start(s16[2,272,128]{2,1,0:T(8,128)(2,1)} %get-tuple-element.53), channel_id=1, source_target_pairs={{0,2},{1,3},{2,4},{3,5},{4,6},{5,7},{6,0},{7,1},{8,10},{9,11},{10,... | collective-permute-start | bytes 417800 | tf_op jit(solution)/shard_map/ppermute | solution.py:378
  52.6 8.2 %collective-permute-start.11 = (s16[2,272,128]{2,1,0:T(8,128)(2,1)}, s16[2,272,128]{2,1,0:T(8,128)(2,1)S(1)}, u32[]{:S(2)}, u32[]{:S(2)}) collective-permute-start(s16[2,272,128]{2,1,0:T(8,128)(2,1)} %get-tuple-element.54), channel_id=1, source_target_pairs={{0,6},{1,7},{2,0},{3,1},{4,2},{5,3},{6,4},{7,5},{8,14},{9,15},{10,... | collective-permute-start | bytes 417800 | tf_op jit(solution)/shard_map/ppermute | solution.py:378
  60.5 0.7 copy-start.7
  60.5 0.7 copy-start.8
  60.7 0.6 copy-start.9
  63.3 1.5 %collective-permute-start.12 = (bf16[384,128]{1,0:T(8,128)(2,1)}, bf16[384,128]{1,0:T(8,128)(2,1)S(1)}, u32[]{:S(2)}, u32[]{:S(2)}) collective-permute-start(bf16[384,128]{1,0:T(8,128)(2,1)} %get-tuple-element.57), channel_id=1, source_target_pairs={{0,1},{1,0},{2,3},{3,2},{4,5},{5,4},{6,7},{7,6},{8,9},{9,8},{10,11... | collective-permute-start | bytes 294920 | tf_op jit(solution)/shard_map/ppermute | solution.py:353
  64.9 0.6 copy-start.11
  68.2 6.4 %collective-permute-start.13 = (s16[272,128]{1,0:T(8,128)(2,1)}, s16[272,128]{1,0:T(8,128)(2,1)S(1)}, u32[]{:S(2)}, u32[]{:S(2)}) collective-permute-start(s16[272,128]{1,0:T(8,128)(2,1)} %get-tuple-element.60), channel_id=1, source_target_pairs={{0,64},{32,96},{64,0},{96,32},{128,192},{160,224},{192,128},{224,1... | collective-permute-start | bytes 208904 | tf_op jit(solution)/shard_map/ppermute | solution.py:388
  71.3 5.7 %collective-permute-start.14 = (s16[272,128]{1,0:T(8,128)(2,1)}, s16[272,128]{1,0:T(8,128)(2,1)S(1)}, u32[]{:S(2)}, u32[]{:S(2)}) collective-permute-start(s16[272,128]{1,0:T(8,128)(2,1)} %get-tuple-element.61), channel_id=1, source_target_pairs={{0,32},{32,64},{64,96},{96,0},{128,160},{160,192},{192,224},{224,1... | collective-permute-start | bytes 208904 | tf_op jit(solution)/shard_map/ppermute | solution.py:388
  72.0 5.0 %collective-permute-start.15 = (s16[272,128]{1,0:T(8,128)(2,1)}, s16[272,128]{1,0:T(8,128)(2,1)S(1)}, u32[]{:S(2)}, u32[]{:S(2)}) collective-permute-start(s16[272,128]{1,0:T(8,128)(2,1)} %get-tuple-element.62), channel_id=1, source_target_pairs={{0,96},{32,0},{64,32},{96,64},{128,224},{160,128},{192,160},{224,1... | collective-permute-start | bytes 208904 | tf_op jit(solution)/shard_map/ppermute | solution.py:388
  74.5 22.2 %collective-permute-start.24 = (bf16[128,1024]{1,0:T(8,128)(2,1)S(1)}, bf16[128,1024]{1,0:T(8,128)(2,1)S(1)}, u32[]{:S(2)}, u32[]{:S(2)}) collective-permute-start(bf16[128,1024]{1,0:T(8,128)(2,1)S(1)} %copy-done), channel_id=1, source_target_pairs={{0,1},{1,0},{2,3},{3,2},{4,5},{5,4},{6,7},{7,6},{8,9},{9,8},{10,11... | collective-permute-start | bytes 786440 | tf_op jit(solution)/shard_map/ppermute | solution.py:353
  77.0 0.9 copy-start.1
  78.6 8.4 %collective-permute-start.16 = (s16[272,128]{1,0:T(8,128)(2,1)S(1)}, s16[272,128]{1,0:T(8,128)(2,1)S(1)}, u32[]{:S(2)}, u32[]{:S(2)}) collective-permute-start(s16[272,128]{1,0:T(8,128)(2,1)S(1)} %merge_y.1.own_ref), channel_id=1, source_target_pairs={{0,128},{32,160},{64,192},{96,224},{128,0},{160,32},{192,64},{224,... | collective-permute-start | bytes 208904 | tf_op jit(solution)/shard_map/ppermute | solution.py:390
  84.4 8.0 %collective-permute-start.25 = (bf16[256,128]{1,0:T(8,128)(2,1)S(1)}, bf16[256,128]{1,0:T(8,128)(2,1)S(1)}, u32[]{:S(2)}, u32[]{:S(2)}) collective-permute-start(bf16[256,128]{1,0:T(8,128)(2,1)S(1)} %bitcast.16), channel_id=1, source_target_pairs={{0,1},{1,0},{2,3},{3,2},{4,5},{5,4},{6,7},{7,6},{8,9},{9,8},{10,11... | collective-permute-start | bytes 196616 | tf_op jit(solution)/shard_map/ppermute | solution.py:353
  87.6 5.8 %collective-permute-start.17 = (bf16[256,128]{1,0:T(8,128)(2,1)S(1)}, bf16[256,128]{1,0:T(8,128)(2,1)S(1)}, u32[]{:S(2)}, u32[]{:S(2)}) collective-permute-start(bf16[256,128]{1,0:T(8,128)(2,1)S(1)} %hidden.1.a0_ref), channel_id=1, source_target_pairs={{0,32},{32,64},{64,96},{96,0},{128,160},{160,192},{192,224},{224,1... | collective-permute-start | bytes 196616 | tf_op jit(solution)/shard_map/ppermute | solution.py:392
  88.1 7.3 %collective-permute-start.18 = (bf16[256,128]{1,0:T(8,128)(2,1)S(1)}, bf16[256,128]{1,0:T(8,128)(2,1)S(1)}, u32[]{:S(2)}, u32[]{:S(2)}) collective-permute-start(bf16[256,128]{1,0:T(8,128)(2,1)S(1)} %hidden.1.a0_ref), channel_id=1, source_target_pairs={{0,64},{32,96},{64,0},{96,32},{128,192},{160,224},{192,128},{224,1... | collective-permute-start | bytes 196616 | tf_op jit(solution)/shard_map/ppermute | solution.py:392
  92.5 4.3 %collective-permute-start.19 = (bf16[256,128]{1,0:T(8,128)(2,1)S(1)}, bf16[256,128]{1,0:T(8,128)(2,1)S(1)}, u32[]{:S(2)}, u32[]{:S(2)}) collective-permute-start(bf16[256,128]{1,0:T(8,128)(2,1)S(1)} %hidden.1.a0_ref), channel_id=1, source_target_pairs={{0,96},{32,0},{64,32},{96,64},{128,224},{160,128},{192,160},{224,1... | collective-permute-start | bytes 196616 | tf_op jit(solution)/shard_map/ppermute | solution.py:392
  92.5 4.3 %collective-permute-start.20 = (bf16[256,128]{1,0:T(8,128)(2,1)S(1)}, bf16[256,128]{1,0:T(8,128)(2,1)S(1)}, u32[]{:S(2)}, u32[]{:S(2)}) collective-permute-start(bf16[256,128]{1,0:T(8,128)(2,1)S(1)} %hidden.1.a0_ref), channel_id=1, source_target_pairs={{0,1},{1,0},{2,3},{3,2},{4,5},{5,4},{6,7},{7,6},{8,9},{9,8},{10,11... | collective-permute-start | bytes 196616 | tf_op jit(solution)/shard_map/ppermute | solution.py:353
  93.4 3.4 %collective-permute-start.21 = (bf16[256,128]{1,0:T(8,128)(2,1)S(1)}, bf16[256,128]{1,0:T(8,128)(2,1)S(1)}, u32[]{:S(2)}, u32[]{:S(2)}) collective-permute-start(bf16[256,128]{1,0:T(8,128)(2,1)S(1)} %collective-permute-done.17.a1_ref), channel_id=1, source_target_pairs={{0,1},{1,0},{2,3},{3,2},{4,5},{5,4},{6,7},{7,6},{8,9},{9,8},{10,11... | collective-permute-start | bytes 196616 | tf_op jit(solution)/shard_map/ppermute | solution.py:353
  95.4 1.4 %collective-permute-start.22 = (bf16[256,128]{1,0:T(8,128)(2,1)S(1)}, bf16[256,128]{1,0:T(8,128)(2,1)S(1)}, u32[]{:S(2)}, u32[]{:S(2)}) collective-permute-start(bf16[256,128]{1,0:T(8,128)(2,1)S(1)} %collective-permute-done.18.a2_ref), channel_id=1, source_target_pairs={{0,1},{1,0},{2,3},{3,2},{4,5},{5,4},{6,7},{7,6},{8,9},{9,8},{10,11... | collective-permute-start | bytes 196616 | tf_op jit(solution)/shard_map/ppermute | solution.py:353
  96.7 1.3 collective-permute-start.23
  98.0 0.8 copy-start.2
  98.8 0.8 copy-start.3
  101.2 11.4 %collective-permute-start.26 = (bf16[128,1152]{1,0:T(8,128)(2,1)S(1)}, bf16[128,1152]{1,0:T(8,128)(2,1)S(1)}, u32[]{:S(2)}, u32[]{:S(2)}) collective-permute-start(bf16[128,1152]{1,0:T(8,128)(2,1)S(1)} %get-tuple-element.69), channel_id=1, source_target_pairs={{0,16},{1,17},{2,18},{3,19},{4,20},{5,21},{6,22},{7,23},{8,24},{9,... | collective-permute-start | bytes 884744 | tf_op jit(solution)/shard_map/ppermute | solution.py:406
  102.2 13.6 %collective-permute-start.27 = (bf16[128,1152]{1,0:T(8,128)(2,1)S(1)}, bf16[128,1152]{1,0:T(8,128)(2,1)S(1)}, u32[]{:S(2)}, u32[]{:S(2)}) collective-permute-start(bf16[128,1152]{1,0:T(8,128)(2,1)S(1)} %get-tuple-element.70), channel_id=1, source_target_pairs={{0,8},{1,9},{2,10},{3,11},{4,12},{5,13},{6,14},{7,15},{8,16},{9,17... | collective-permute-start | bytes 884744 | tf_op jit(solution)/shard_map/ppermute | solution.py:406
  103.2 14.9 %collective-permute-start.28 = (bf16[128,1152]{1,0:T(8,128)(2,1)S(1)}, bf16[128,1152]{1,0:T(8,128)(2,1)S(1)}, u32[]{:S(2)}, u32[]{:S(2)}) collective-permute-start(bf16[128,1152]{1,0:T(8,128)(2,1)S(1)} %get-tuple-element.71), channel_id=1, source_target_pairs={{0,24},{1,25},{2,26},{3,27},{4,28},{5,29},{6,30},{7,31},{8,0},{9,1... | collective-permute-start | bytes 884744 | tf_op jit(solution)/shard_map/ppermute | solution.py:406
  118.9 9.5 %collective-permute-start.29 = (bf16[32,1152]{1,0:T(8,128)(2,1)S(1)}, bf16[32,1152]{1,0:T(8,128)(2,1)S(1)}, u32[]{:S(2)}, u32[]{:S(2)}) collective-permute-start(bf16[32,1152]{1,0:T(8,128)(2,1)S(1)} %get-tuple-element.73), channel_id=1, source_target_pairs={{0,4},{1,5},{2,6},{3,7},{4,0},{5,1},{6,2},{7,3},{8,12},{9,13},{10,... | collective-permute-start | bytes 221192 | tf_op jit(solution)/shard_map/ppermute | solution.py:411
  123.1 6.5 %collective-permute-start.30 = (bf16[32,1152]{1,0:T(8,128)(2,1)S(1)}, bf16[32,1152]{1,0:T(8,128)(2,1)S(1)}, u32[]{:S(2)}, u32[]{:S(2)}) collective-permute-start(bf16[32,1152]{1,0:T(8,128)(2,1)S(1)} %get-tuple-element.74), channel_id=1, source_target_pairs={{0,2},{1,3},{2,4},{3,5},{4,6},{5,7},{6,0},{7,1},{8,10},{9,11},{10,... | collective-permute-start | bytes 221192 | tf_op jit(solution)/shard_map/ppermute | solution.py:411
  123.1 6.5 %collective-permute-start.31 = (bf16[32,1152]{1,0:T(8,128)(2,1)S(1)}, bf16[32,1152]{1,0:T(8,128)(2,1)S(1)}, u32[]{:S(2)}, u32[]{:S(2)}) collective-permute-start(bf16[32,1152]{1,0:T(8,128)(2,1)S(1)} %get-tuple-element.75), channel_id=1, source_target_pairs={{0,6},{1,7},{2,0},{3,1},{4,2},{5,3},{6,4},{7,5},{8,14},{9,15},{10,... | collective-permute-start | bytes 221192 | tf_op jit(solution)/shard_map/ppermute | solution.py:411

commit v4 on v2

--- a/solution.py
+++ b/solution.py
@@ -214,11 +214,29 @@
 
 
 def merge_x_kernel(pos_ref, *rest):
-    for d, out_ref in enumerate(rest[-4:]):
-        for c in range(2):
-            index = lax.rem(pos_ref[1] + d, NZ)
-            total, count = gathered((rest[6 + c].at[index],), [ref.at[index] for ref in rest[c:6:2]])
-            (put_coded if d else put_plain)(out_ref.at[c], total, count)
+    for step, out_ref in enumerate(rest[-4:]):
+        @pl.when(pl.program_id(0) == step)
+        def _():
+            for c in range(2):
+                total, count = gathered((rest[6 + c].at[0],), [ref.at[0] for ref in rest[c:6:2]])
+                (put_coded if step else put_plain)(out_ref.at[c], total, count)
+
+
+def merge_x(pos, *parts):
+    block = lambda rows: pl.BlockSpec((1, rows, BLK), lambda d, p: (lax.rem(p[1] + d, NZ), 0, 0))
+    outs = [SUM_PLAIN] + [SUM_CODED] * 3
+    return pl.pallas_call(
+        merge_x_kernel,
+        out_shape=outs,
+        grid_spec=pltpu.PrefetchScalarGridSpec(
+            num_scalar_prefetch=1,
+            grid=(NZ,),
+            in_specs=[block(part.shape[1]) for part in parts],
+            out_specs=[pl.BlockSpec(out.shape, lambda d, p: (0, 0, 0)) for out in outs],
+        ),
+        compiler_params=ALONE,
+        name="merge_x",
+    )(pos, *parts)
 
 
 def merge_z_kernel(pos_ref, r1_ref, r2_ref, r3_ref, own_ref, *rest):
@@ -367,9 +385,7 @@
     self_term = jnp.dot(seed_feats, w_self, preferred_element_type=jnp.float32)
     self_term = self_term + jnp.where(feat == 0, bias_term, 0.0)
 
-    own, *coded = call(merge_x_kernel, "merge_x", [SUM_PLAIN] + [SUM_CODED] * 3, 8, params=ALONE)(
-        pos, *far, *own
-    )
+    own, *coded = merge_x(pos, *far, *own)
     arrived = [lax.ppermute(coded[d - 1], "node", shift_z(d)) for d in (2, 1, 3)]
     mine, give, rest = call(
         merge_z_kernel, "merge_z", [HALF16, shaped(HALF + BLK, BLK, jnp.bfloat16), shaped(BLK, BLK, jnp.bfloat16)], 4

time: 126 us -> 127 us (level)
  Pallas kernels: 34.1 us -> 35.7 us
    pallas_call x1, Pallas kernels: 3.1 us -> 4.7 us  [merge_x(): pl.pallas_call(merge_x_kernel, out_shape=outs, grid_spec=pltpu.PrefetchSc...]
where the time goes in v4:
time: 127 us
  starting transfers between devices  43.7 us (34%)
  waiting for transfers between devices  42.2 us (33%)
  Pallas kernels  35.7 us (28%)
  matrix products  1.54 us (1%)
  other arithmetic  1.4 us (1%)
  local copies, waits for them, and re-layouts  1.36 us (1%)
    pallas_call x4, Pallas kernels, sums(): pl.pallas_call(functools.partial(sums_kernel, d), out_shape=[jax.ShapeDty...  22.2 us
    ppermute x3, waiting for transfers between devices, body(): lax.ppermute(parts[d - 1], 'node', shift_x(d))  14 us
    ppermute x6, starting transfers between devices, body(): lax.ppermute(part, 'node', shift_x(d))  8.31 us
    ppermute x3, starting transfers between devices, body(): lax.ppermute(parts[d - 1], 'node', shift_z(d))  7.83 us
    ppermute x6, waiting for transfers between devices, body(): lax.ppermute(part, 'node', shift_x(d))  7.77 us
    ppermute x3, starting transfers between devices, body(): lax.ppermute(coded[d - 1], 'node', shift_z(d))  6.57 us
    ppermute x3, starting transfers between devices, body(): lax.ppermute(coded[d - 1], 'feat', shift_y(d))  6.36 us
    ppermute x3, waiting for transfers between devices, body(): lax.ppermute(coded[d - 1], 'node', shift_z(d))  6.26 us
  transfers between devices with their start and end apart: 32, of which 17 were waited for; matrix products, arithmetic and copies ran while one was open for 3% of the time, Pallas kernels for 16%

profile of v4, /device:TPU:6, one launch (start us, length us, event | category | flops | bytes accessed | tf_op | source)
XLA Modules:
  0.0 126.8 jit_solution(8200588496602545103)
XLA Ops:
  0.7 0.1 collective-permute-start.1
  0.8 2.1 %half_columns.1 = bf16[2048,256]{1,0:T(8,128)(2,1)} custom-call(s32[1]{0:T(128)} %bitcast.5.side_ref, bf16[2048,512]{1,0:T(8,128)(2,1)} %feat0_ref.7), custom_call_target="tpu_custom_call" | custom-call | tf_op jit(solution)/shard_map/half_columns/pallas_call | solution.py:108
  2.9 0.6 collective-permute-start.2
  3.4 0.1 copy.15
  3.5 0.1 reshape.23
  3.6 0.1 pad_add_fusion.1
  3.7 0.1 collective-permute-start
  3.8 0.7 pad_add_fusion.2.pos_ref
  4.4 1.3 %collective-permute-done = s32[288]{0:T(512)S(1)} collective-permute-done((s32[288]{0:T(512)S(1)}, s32[288]{0:T(512)S(1)}, u32[]{:S(2)}, u32[]{:S(2)}) %collective-permute-start) | collective-permute-done | bytes 1184 | tf_op jit(solution)/shard_map/ppermute | solution.py:364
  5.7 0.1 slice.7
  5.8 0.7 pad_add_fusion.table_ref
  6.5 5.5 %sums.4 = (s16[4,272,128]{2,1,0:T(8,128)(2,1)}, s16[4,272,128]{2,1,0:T(8,128)(2,1)}) custom-call(s32[4]{0:T(128)} %pad_add_fusion.2.pos_ref, s32[576]{0:T(1024)} %pad_add_fusion.table_ref, s32[32,8,8,128]{3,2,1,0:T(8,128)} %bitcast.18, s32[32,8,8,128]{3,2,1,0:T(8,128)} %collective-permute-done.1.pat1_ref, bf16[2048,512]{1,0:T(8,128)(2,1)} %feat0_ref.7, ...), custom_call_target="tpu_custom_call" | custom-call | flops 2000000000 | bytes 3000000 | tf_op jit(solution)/shard_map/sums/pallas_call | solution.py:176
  12.0 1.5 %collective-permute-start.3 = (s16[4,272,128]{2,1,0:T(8,128)(2,1)}, s16[4,272,128]{2,1,0:T(8,128)(2,1)S(1)}, u32[]{:S(2)}, u32[]{:S(2)}) collective-permute-start(s16[4,272,128]{2,1,0:T(8,128)(2,1)} %get-tuple-element.43), channel_id=1, source_target_pairs={{0,16},{1,17},{2,18},{3,19},{4,20},{5,21},{6,22},{7,23},{8,24},{9,... | collective-permute-start | bytes 835592 | tf_op jit(solution)/shard_map/ppermute | solution.py:376
  13.5 2.1 %collective-permute-start.4 = (s16[4,272,128]{2,1,0:T(8,128)(2,1)}, s16[4,272,128]{2,1,0:T(8,128)(2,1)S(1)}, u32[]{:S(2)}, u32[]{:S(2)}) collective-permute-start(s16[4,272,128]{2,1,0:T(8,128)(2,1)} %get-tuple-element.44), channel_id=1, source_target_pairs={{0,16},{1,17},{2,18},{3,19},{4,20},{5,21},{6,22},{7,23},{8,24},{9,... | collective-permute-start | bytes 835592 | tf_op jit(solution)/shard_map/ppermute | solution.py:376
  15.6 5.5 %sums.5 = (s16[4,272,128]{2,1,0:T(8,128)(2,1)}, s16[4,272,128]{2,1,0:T(8,128)(2,1)}) custom-call(s32[4]{0:T(128)} %pad_add_fusion.2.pos_ref, s32[576]{0:T(1024)} %pad_add_fusion.table_ref, s32[32,8,8,128]{3,2,1,0:T(8,128)} %bitcast.19, s32[32,8,8,128]{3,2,1,0:T(8,128)} %collective-permute-done.1.pat1_ref, bf16[2048,512]{1,0:T(8,128)(2,1)} %feat0_ref.7, ...), custom_call_target="tpu_custom_call" | custom-call | flops 2000000000 | bytes 3000000 | tf_op jit(solution)/shard_map/sums/pallas_call | solution.py:176
  21.2 2.3 %collective-permute-start.5 = (s16[4,272,128]{2,1,0:T(8,128)(2,1)}, s16[4,272,128]{2,1,0:T(8,128)(2,1)}, u32[]{:S(2)}, u32[]{:S(2)}) collective-permute-start(s16[4,272,128]{2,1,0:T(8,128)(2,1)} %get-tuple-element.45), channel_id=1, source_target_pairs={{0,8},{1,9},{2,10},{3,11},{4,12},{5,13},{6,14},{7,15},{8,16},{9,17... | collective-permute-start | bytes 835592 | tf_op jit(solution)/shard_map/ppermute | solution.py:376
  23.5 0.1 collective-permute-start.6
  23.6 5.5 %sums.6 = (s16[4,272,128]{2,1,0:T(8,128)(2,1)}, s16[4,272,128]{2,1,0:T(8,128)(2,1)}) custom-call(s32[4]{0:T(128)} %pad_add_fusion.2.pos_ref, s32[576]{0:T(1024)} %pad_add_fusion.table_ref, s32[32,8,8,128]{3,2,1,0:T(8,128)} %bitcast.20, s32[32,8,8,128]{3,2,1,0:T(8,128)} %collective-permute-done.1.pat1_ref, bf16[2048,512]{1,0:T(8,128)(2,1)} %feat0_ref.7, ...), custom_call_target="tpu_custom_call" | custom-call | flops 2000000000 | bytes 3000000 | tf_op jit(solution)/shard_map/sums/pallas_call | solution.py:176
  29.1 2.2 %collective-permute-start.7 = (s16[4,272,128]{2,1,0:T(8,128)(2,1)}, s16[4,272,128]{2,1,0:T(8,128)(2,1)}, u32[]{:S(2)}, u32[]{:S(2)}) collective-permute-start(s16[4,272,128]{2,1,0:T(8,128)(2,1)} %get-tuple-element.47), channel_id=1, source_target_pairs={{0,24},{1,25},{2,26},{3,27},{4,28},{5,29},{6,30},{7,31},{8,0},{9,1... | collective-permute-start | bytes 835592 | tf_op jit(solution)/shard_map/ppermute | solution.py:376
  31.3 0.1 collective-permute-start.8
  31.4 5.7 %sums.7 = (f32[4,264,128]{2,1,0:T(8,128)}, f32[4,264,128]{2,1,0:T(8,128)}) custom-call(s32[4]{0:T(128)} %pad_add_fusion.2.pos_ref, s32[576]{0:T(1024)} %pad_add_fusion.table_ref, s32[32,8,8,128]{3,2,1,0:T(8,128)} %bitcast.21, s32[32,8,8,128]{3,2,1,0:T(8,128)} %collective-permute-done.1.pat1_ref, bf16[2048,512]{1,0:T(8,128)(2,1)} %feat0_ref.7, ...), custom_call_target="tpu_custom_call" | custom-call | flops 2000000000 | bytes 3000000 | tf_op jit(solution)/shard_map/sums/pallas_call | solution.py:176
  37.1 3.2 %collective-permute-done.6.rest_3_ = s16[4,272,128]{2,1,0:T(8,128)(2,1)} collective-permute-done((s16[4,272,128]{2,1,0:T(8,128)(2,1)}, s16[4,272,128]{2,1,0:T(8,128)(2,1)}, u32[]{:S(2)}, u32[]{:S(2)}) %collective-permute-start.6) | collective-permute-done | bytes 278560 | tf_op jit(solution)/shard_map/ppermute | solution.py:376
  40.3 0.1 collective-permute-done.7.rest_4_
  40.5 4.5 %collective-permute-done.8.rest_5_ = s16[4,272,128]{2,1,0:T(8,128)(2,1)} collective-permute-done((s16[4,272,128]{2,1,0:T(8,128)(2,1)}, s16[4,272,128]{2,1,0:T(8,128)(2,1)}, u32[]{:S(2)}, u32[]{:S(2)}) %collective-permute-start.8) | collective-permute-done | bytes 278560 | tf_op jit(solution)/shard_map/ppermute | solution.py:376
  44.9 4.7 %merge_x.1 = (f32[2,264,128]{2,1,0:T(8,128)}, s16[2,272,128]{2,1,0:T(8,128)(2,1)}, s16[2,272,128]{2,1,0:T(8,128)(2,1)}, s16[2,272,128]{2,1,0:T(8,128)(2,1)}) custom-call(s32[4]{0:T(128)} %pad_add_fusion.2.pos_ref, s16[4,272,128]{2,1,0:T(8,128)(2,1)} %copy-done.5, s16[4,272,128]{2,1,0:T(8,128)(2,1)} %copy-done.6, ...), custom_call_target="tpu_custom_call" | custom-call | tf_op jit(solution)/shard_map/merge_x/pallas_call | solution.py:228
  49.6 2.7 %collective-permute-start.9 = (s16[2,272,128]{2,1,0:T(8,128)(2,1)}, s16[2,272,128]{2,1,0:T(8,128)(2,1)S(1)}, u32[]{:S(2)}, u32[]{:S(2)}) collective-permute-start(s16[2,272,128]{2,1,0:T(8,128)(2,1)} %get-tuple-element.53), channel_id=1, source_target_pairs={{0,4},{1,5},{2,6},{3,7},{4,0},{5,1},{6,2},{7,3},{8,12},{9,13},{10,... | collective-permute-start | bytes 417800 | tf_op jit(solution)/shard_map/ppermute | solution.py:389
  52.4 1.9 %collective-permute-start.10 = (s16[2,272,128]{2,1,0:T(8,128)(2,1)}, s16[2,272,128]{2,1,0:T(8,128)(2,1)S(1)}, u32[]{:S(2)}, u32[]{:S(2)}) collective-permute-start(s16[2,272,128]{2,1,0:T(8,128)(2,1)} %get-tuple-element.54), channel_id=1, source_target_pairs={{0,2},{1,3},{2,4},{3,5},{4,6},{5,7},{6,0},{7,1},{8,10},{9,11},{10,... | collective-permute-start | bytes 417800 | tf_op jit(solution)/shard_map/ppermute | solution.py:389
  54.3 1.9 %collective-permute-start.11 = (s16[2,272,128]{2,1,0:T(8,128)(2,1)}, s16[2,272,128]{2,1,0:T(8,128)(2,1)S(1)}, u32[]{:S(2)}, u32[]{:S(2)}) collective-permute-start(s16[2,272,128]{2,1,0:T(8,128)(2,1)} %get-tuple-element.55), channel_id=1, source_target_pairs={{0,6},{1,7},{2,0},{3,1},{4,2},{5,3},{6,4},{7,5},{8,14},{9,15},{10,... | collective-permute-start | bytes 417800 | tf_op jit(solution)/shard_map/ppermute | solution.py:389
  56.2 6.0 %collective-permute-done.9.r1_ref = s16[2,272,128]{2,1,0:T(8,128)(2,1)S(1)} collective-permute-done((s16[2,272,128]{2,1,0:T(8,128)(2,1)}, s16[2,272,128]{2,1,0:T(8,128)(2,1)S(1)}, u32[]{:S(2)}, u32[]{:S(2)}) %collective-permute-start.9) | collective-permute-done | bytes 139296 | tf_op jit(solution)/shard_map/ppermute | solution.py:389
  62.2 0.2 collective-permute-done.11.r3_ref
  62.5 1.0 copy-done.1
  63.4 0.7 merge_z.1
  64.1 0.1 collective-permute-start.12
  64.2 1.5 %convolution_add_fusion.self_ref = f32[128,1024]{1,0:T(8,128)S(1)} fusion(bf16[128,512]{1,0:T(8,128)(2,1)S(1)} %copy-done.4, bf16[512,1024]{1,0:T(8,128)(2,1)} %param.14, f32[1024]{0:T(1024)S(1)} %broadcast_select_fusion), kind=kOutput, calls=%fused_computation | convolution fusion | flops 134348800 | bytes 1708032 | tf_op jit(solution)/shard_map/dot_general | solution.py:385
  65.8 1.1 pre_terms.1
  66.9 3.1 %collective-permute-start.13 = (s16[272,128]{1,0:T(8,128)(2,1)S(1)}, s16[272,128]{1,0:T(8,128)(2,1)S(1)}, u32[]{:S(2)}, u32[]{:S(2)}) collective-permute-start(s16[272,128]{1,0:T(8,128)(2,1)S(1)} %get-tuple-element.63), channel_id=1, source_target_pairs={{0,64},{32,96},{64,0},{96,32},{128,192},{160,224},{192,128},{224,1... | collective-permute-start | bytes 208904 | tf_op jit(solution)/shard_map/ppermute | solution.py:399
  70.1 0.7 collective-permute-start.14
  70.8 2.5 %collective-permute-start.15 = (s16[272,128]{1,0:T(8,128)(2,1)S(1)}, s16[272,128]{1,0:T(8,128)(2,1)S(1)}, u32[]{:S(2)}, u32[]{:S(2)}) collective-permute-start(s16[272,128]{1,0:T(8,128)(2,1)S(1)} %get-tuple-element.65), channel_id=1, source_target_pairs={{0,96},{32,0},{64,32},{96,64},{128,224},{160,128},{192,160},{224,1... | collective-permute-start | bytes 208904 | tf_op jit(solution)/shard_map/ppermute | solution.py:399
  73.3 0.1 copy.16
  73.4 2.1 %collective-permute-done.14.r2_ref = s16[272,128]{1,0:T(8,128)(2,1)S(1)} collective-permute-done((s16[272,128]{1,0:T(8,128)(2,1)S(1)}, s16[272,128]{1,0:T(8,128)(2,1)S(1)}, u32[]{:S(2)}, u32[]{:S(2)}) %collective-permute-start.14) | collective-permute-done | bytes 69664 | tf_op jit(solution)/shard_map/ppermute | solution.py:399
  75.6 0.7 merge_y.1.own_ref
  76.2 5.8 %collective-permute-start.16 = (s16[272,128]{1,0:T(8,128)(2,1)S(1)}, s16[272,128]{1,0:T(8,128)(2,1)S(1)}, u32[]{:S(2)}, u32[]{:S(2)}) collective-permute-start(s16[272,128]{1,0:T(8,128)(2,1)S(1)} %merge_y.1.own_ref), channel_id=1, source_target_pairs={{0,128},{32,160},{64,192},{96,224},{128,0},{160,32},{192,64},{224,... | collective-permute-start | bytes 208904 | tf_op jit(solution)/shard_map/ppermute | solution.py:401
  82.0 0.1 collective-permute-start.25
  82.1 2.5 %collective-permute-done.16.far_ref = s16[272,128]{1,0:T(8,128)(2,1)S(1)} collective-permute-done((s16[272,128]{1,0:T(8,128)(2,1)S(1)}, s16[272,128]{1,0:T(8,128)(2,1)S(1)}, u32[]{:S(2)}, u32[]{:S(2)}) %collective-permute-start.16) | collective-permute-done | bytes 69664 | tf_op jit(solution)/shard_map/ppermute | solution.py:401
  84.7 0.6 hidden.1.a0_ref
  85.2 0.9 collective-permute-start.17
  86.1 4.1 %collective-permute-start.18 = (bf16[256,128]{1,0:T(8,128)(2,1)S(1)}, bf16[256,128]{1,0:T(8,128)(2,1)S(1)}, u32[]{:S(2)}, u32[]{:S(2)}) collective-permute-start(bf16[256,128]{1,0:T(8,128)(2,1)S(1)} %hidden.1.a0_ref), channel_id=1, source_target_pairs={{0,64},{32,96},{64,0},{96,32},{128,192},{160,224},{192,128},{224,1... | collective-permute-start | bytes 196616 | tf_op jit(solution)/shard_map/ppermute | solution.py:403
  90.2 0.8 collective-permute-done.17.a1_ref
  91.0 2.2 %collective-permute-done.18.a2_ref = bf16[256,128]{1,0:T(8,128)(2,1)S(1)} collective-permute-done((bf16[256,128]{1,0:T(8,128)(2,1)S(1)}, bf16[256,128]{1,0:T(8,128)(2,1)S(1)}, u32[]{:S(2)}, u32[]{:S(2)}) %collective-permute-start.18) | collective-permute-done | bytes 65568 | tf_op jit(solution)/shard_map/ppermute | solution.py:403
  93.2 1.3 %collective-permute-done.19.a3_ref = bf16[256,128]{1,0:T(8,128)(2,1)S(1)} collective-permute-done((bf16[256,128]{1,0:T(8,128)(2,1)S(1)}, bf16[256,128]{1,0:T(8,128)(2,1)S(1)}, u32[]{:S(2)}, u32[]{:S(2)}) %collective-permute-start.19) | collective-permute-done | bytes 65568 | tf_op jit(solution)/shard_map/ppermute | solution.py:403
  94.5 1.2 collective-permute-done.23.b3_ref
  95.8 1.6 %grads.1 = (bf16[128,1024]{1,0:T(8,128)(2,1)}, f32[128,1152]{1,0:T(8,128)S(1)}, bf16[128,1152]{1,0:T(8,128)(2,1)S(1)}, bf16[128,1152]{1,0:T(8,128)(2,1)S(1)}, bf16[128,1152]{1,0:T(8,128)(2,1)S(1)}) custom-call(s32[4]{0:T(128)S(1)} %copy-done.3, bf16[256,128]{1,0:T(8,128)(2,1)S(1)} %hidden.1.a0_ref, bf16[256,128]{1,0:T(8,128)(2,1)S(1)} %collective-permute-done.17.a1_ref, ...), custom_call_target="tpu_custom_call" | custom-call | tf_op jit(solution)/shard_map/grads/pallas_call | solution.py:414
  97.3 0.9 collective-permute-start.26
  98.2 1.1 collective-permute-start.27
  99.3 0.9 collective-permute-start.28
  100.3 8.5 %collective-permute-done.26.r1_ref = bf16[128,1152]{1,0:T(8,128)(2,1)S(1)} collective-permute-done((bf16[128,1152]{1,0:T(8,128)(2,1)S(1)}, bf16[128,1152]{1,0:T(8,128)(2,1)S(1)}, u32[]{:S(2)}, u32[]{:S(2)}) %collective-permute-start.26) | collective-permute-done | bytes 294944 | tf_op jit(solution)/shard_map/ppermute | solution.py:417
  108.7 3.1 %collective-permute-done.27.r2_ref = bf16[128,1152]{1,0:T(8,128)(2,1)S(1)} collective-permute-done((bf16[128,1152]{1,0:T(8,128)(2,1)S(1)}, bf16[128,1152]{1,0:T(8,128)(2,1)S(1)}, u32[]{:S(2)}, u32[]{:S(2)}) %collective-permute-start.27) | collective-permute-done | bytes 294944 | tf_op jit(solution)/shard_map/ppermute | solution.py:417
  111.9 2.3 %collective-permute-done.28.r3_ref = bf16[128,1152]{1,0:T(8,128)(2,1)S(1)} collective-permute-done((bf16[128,1152]{1,0:T(8,128)(2,1)S(1)}, bf16[128,1152]{1,0:T(8,128)(2,1)S(1)}, u32[]{:S(2)}, u32[]{:S(2)}) %collective-permute-start.28) | collective-permute-done | bytes 294944 | tf_op jit(solution)/shard_map/ppermute | solution.py:417
  114.2 0.8 fold_x.1
  115.0 4.0 %collective-permute-start.29 = (bf16[32,1152]{1,0:T(8,128)(2,1)S(1)}, bf16[32,1152]{1,0:T(8,128)(2,1)S(1)}, u32[]{:S(2)}, u32[]{:S(2)}) collective-permute-start(bf16[32,1152]{1,0:T(8,128)(2,1)S(1)} %get-tuple-element.75), channel_id=1, source_target_pairs={{0,4},{1,5},{2,6},{3,7},{4,0},{5,1},{6,2},{7,3},{8,12},{9,13},{10,... | collective-permute-start | bytes 221192 | tf_op jit(solution)/shard_map/ppermute | solution.py:422
  119.0 3.8 %collective-permute-start.31 = (bf16[32,1152]{1,0:T(8,128)(2,1)S(1)}, bf16[32,1152]{1,0:T(8,128)(2,1)S(1)}, u32[]{:S(2)}, u32[]{:S(2)}) collective-permute-start(bf16[32,1152]{1,0:T(8,128)(2,1)S(1)} %get-tuple-element.77), channel_id=1, source_target_pairs={{0,6},{1,7},{2,0},{3,1},{4,2},{5,3},{6,4},{7,5},{8,14},{9,15},{10,... | collective-permute-start | bytes 221192 | tf_op jit(solution)/shard_map/ppermute | solution.py:422
  122.9 1.5 %collective-permute-done.29.r1_ref = bf16[32,1152]{1,0:T(8,128)(2,1)S(1)} collective-permute-done((bf16[32,1152]{1,0:T(8,128)(2,1)S(1)}, bf16[32,1152]{1,0:T(8,128)(2,1)S(1)}, u32[]{:S(2)}, u32[]{:S(2)}) %collective-permute-start.29) | collective-permute-done | bytes 73760 | tf_op jit(solution)/shard_map/ppermute | solution.py:422
  124.4 1.2 collective-permute-done.30.r2_ref
  125.6 1.3 last.1
  (44 shorter events, 0.1 us)
Async XLA Ops:
  0.6 2.8 %copy-start.7 = (s32[32,8]{0,1:T(8,128)S(1)}, s32[32,8]{0,1:T(8,128)}, u32[]{:S(2)}) copy-start(s32[32,8]{0,1:T(8,128)} %param.12) | copy-start | bytes 3076
  0.6 3.0 %copy-start.9 = (s32[32]{0:T(128)S(1)}, s32[32]{0:T(128)}, u32[]{:S(2)}) copy-start(s32[32]{0:T(128)} %param.13) | copy-start | bytes 388
  0.7 5.8 %collective-permute-start.1 = (s32[32,8,8,128]{3,2,1,0:T(8,128)}, s32[32,8,8,128]{3,2,1,0:T(8,128)}, u32[]{:S(2)}, u32[]{:S(2)}) collective-permute-start(s32[32,8,8,128]{3,2,1,0:T(8,128)} %bitcast.17), channel_id=1, source_target_pairs={{0,1},{1,0},{2,3},{3,2},{4,5},{5,4},{6,7},{7,6},{8,9},{9,8},{10,11... | collective-permute-start | bytes 3145736 | tf_op jit(solution)/shard_map/ppermute | solution.py:364
  2.9 3.6 %collective-permute-start.2 = (bf16[2048,256]{1,0:T(8,128)(2,1)}, bf16[2048,256]{1,0:T(8,128)(2,1)}, u32[]{:S(2)}, u32[]{:S(2)}) collective-permute-start(bf16[2048,256]{1,0:T(8,128)(2,1)} %half_columns.1), channel_id=1, source_target_pairs={{0,1},{1,0},{2,3},{3,2},{4,5},{5,4},{6,7},{7,6},{8,9},{9,8},{10,11... | collective-permute-start | bytes 3145736 | tf_op jit(solution)/shard_map/ppermute | solution.py:364
  3.7 2.0 %collective-permute-start = (s32[288]{0:T(512)S(1)}, s32[288]{0:T(512)S(1)}, u32[]{:S(2)}, u32[]{:S(2)}) collective-permute-start(s32[288]{0:T(512)S(1)} %pad_add_fusion.1), channel_id=1, source_target_pairs={{0,1},{1,0},{2,3},{3,2},{4,5},{5,4},{6,7},{7,6},{8,9},{9,8},{10,11... | collective-permute-start | bytes 3464 | tf_op jit(solution)/shard_map/ppermute | solution.py:364
  12.0 19.3 %collective-permute-start.3 = (s16[4,272,128]{2,1,0:T(8,128)(2,1)}, s16[4,272,128]{2,1,0:T(8,128)(2,1)S(1)}, u32[]{:S(2)}, u32[]{:S(2)}) collective-permute-start(s16[4,272,128]{2,1,0:T(8,128)(2,1)} %get-tuple-element.43), channel_id=1, source_target_pairs={{0,16},{1,17},{2,18},{3,19},{4,20},{5,21},{6,22},{7,23},{8,24},{9,... | collective-permute-start | bytes 835592 | tf_op jit(solution)/shard_map/ppermute | solution.py:376
  13.5 23.6 %collective-permute-start.4 = (s16[4,272,128]{2,1,0:T(8,128)(2,1)}, s16[4,272,128]{2,1,0:T(8,128)(2,1)S(1)}, u32[]{:S(2)}, u32[]{:S(2)}) collective-permute-start(s16[4,272,128]{2,1,0:T(8,128)(2,1)} %get-tuple-element.44), channel_id=1, source_target_pairs={{0,16},{1,17},{2,18},{3,19},{4,20},{5,21},{6,22},{7,23},{8,24},{9,... | collective-permute-start | bytes 835592 | tf_op jit(solution)/shard_map/ppermute | solution.py:376
  21.2 15.9 %collective-permute-start.5 = (s16[4,272,128]{2,1,0:T(8,128)(2,1)}, s16[4,272,128]{2,1,0:T(8,128)(2,1)}, u32[]{:S(2)}, u32[]{:S(2)}) collective-permute-start(s16[4,272,128]{2,1,0:T(8,128)(2,1)} %get-tuple-element.45), channel_id=1, source_target_pairs={{0,8},{1,9},{2,10},{3,11},{4,12},{5,13},{6,14},{7,15},{8,16},{9,17... | collective-permute-start | bytes 835592 | tf_op jit(solution)/shard_map/ppermute | solution.py:376
  23.5 16.9 %collective-permute-start.6 = (s16[4,272,128]{2,1,0:T(8,128)(2,1)}, s16[4,272,128]{2,1,0:T(8,128)(2,1)}, u32[]{:S(2)}, u32[]{:S(2)}) collective-permute-start(s16[4,272,128]{2,1,0:T(8,128)(2,1)} %get-tuple-element.46), channel_id=1, source_target_pairs={{0,8},{1,9},{2,10},{3,11},{4,12},{5,13},{6,14},{7,15},{8,16},{9,17... | collective-permute-start | bytes 835592 | tf_op jit(solution)/shard_map/ppermute | solution.py:376
  29.1 11.4 %collective-permute-start.7 = (s16[4,272,128]{2,1,0:T(8,128)(2,1)}, s16[4,272,128]{2,1,0:T(8,128)(2,1)}, u32[]{:S(2)}, u32[]{:S(2)}) collective-permute-start(s16[4,272,128]{2,1,0:T(8,128)(2,1)} %get-tuple-element.47), channel_id=1, source_target_pairs={{0,24},{1,25},{2,26},{3,27},{4,28},{5,29},{6,30},{7,31},{8,0},{9,1... | collective-permute-start | bytes 835592 | tf_op jit(solution)/shard_map/ppermute | solution.py:376
  31.3 5.8 %copy-start.5 = (s16[4,272,128]{2,1,0:T(8,128)(2,1)}, s16[4,272,128]{2,1,0:T(8,128)(2,1)S(1)}, u32[]{:S(2)}) copy-start(s16[4,272,128]{2,1,0:T(8,128)(2,1)S(1)} %collective-permute-done.3.rest_0_) | copy-start | bytes 835588
  31.3 13.6 %collective-permute-start.8 = (s16[4,272,128]{2,1,0:T(8,128)(2,1)}, s16[4,272,128]{2,1,0:T(8,128)(2,1)}, u32[]{:S(2)}, u32[]{:S(2)}) collective-permute-start(s16[4,272,128]{2,1,0:T(8,128)(2,1)} %get-tuple-element.48), channel_id=1, source_target_pairs={{0,24},{1,25},{2,26},{3,27},{4,28},{5,29},{6,30},{7,31},{8,0},{9,1... | collective-permute-start | bytes 835592 | tf_op jit(solution)/shard_map/ppermute | solution.py:376
  37.1 19.1 %copy-start.8 = (f32[1024]{0:T(1024)S(1)}, f32[1024]{0:T(1024)}, u32[]{:S(2)}) copy-start(f32[1024]{0:T(1024)} %param.16) | copy-start | bytes 12292
  37.1 25.4 %copy-start.3 = (s32[4]{0:T(128)S(1)}, s32[4]{0:T(128)}, u32[]{:S(2)}) copy-start(s32[4]{0:T(128)} %pad_add_fusion.2.pos_ref) | copy-start | bytes 52
  37.1 27.1 %copy-start.4 = (bf16[128,512]{1,0:T(8,128)(2,1)S(1)}, bf16[128,512]{1,0:T(8,128)(2,1)}, u32[]{:S(2)}) copy-start(bf16[128,512]{1,0:T(8,128)(2,1)} %param.10) | copy-start | bytes 393220
  37.1 7.8 %copy-start.6 = (s16[4,272,128]{2,1,0:T(8,128)(2,1)}, s16[4,272,128]{2,1,0:T(8,128)(2,1)S(1)}, u32[]{:S(2)}) copy-start(s16[4,272,128]{2,1,0:T(8,128)(2,1)S(1)} %collective-permute-done.4.rest_1_) | copy-start | bytes 835588
  44.9 28.4 %copy-start.2 = (bf16[128,1024]{1,0:T(8,128)(2,1)S(1)}, bf16[128,1024]{1,0:T(8,128)(2,1)}, u32[]{:S(2)}) copy-start(bf16[128,1024]{1,0:T(8,128)(2,1)} %og0_ref) | copy-start | bytes 786436
  49.6 16.2 %copy-start = (bf16[512,1024]{1,0:T(8,128)(2,1)S(1)}, bf16[512,1024]{1,0:T(8,128)(2,1)}, u32[]{:S(2)}) copy-start(bf16[512,1024]{1,0:T(8,128)(2,1)} %w_ref.1) | copy-start | bytes 3145732
  49.6 12.6 %collective-permute-start.9 = (s16[2,272,128]{2,1,0:T(8,128)(2,1)}, s16[2,272,128]{2,1,0:T(8,128)(2,1)S(1)}, u32[]{:S(2)}, u32[]{:S(2)}) collective-permute-start(s16[2,272,128]{2,1,0:T(8,128)(2,1)} %get-tuple-element.53), channel_id=1, source_target_pairs={{0,4},{1,5},{2,6},{3,7},{4,0},{5,1},{6,2},{7,3},{8,12},{9,13},{10,... | collective-permute-start | bytes 417800 | tf_op jit(solution)/shard_map/ppermute | solution.py:389
  52.4 9.8 %collective-permute-start.10 = (s16[2,272,128]{2,1,0:T(8,128)(2,1)}, s16[2,272,128]{2,1,0:T(8,128)(2,1)S(1)}, u32[]{:S(2)}, u32[]{:S(2)}) collective-permute-start(s16[2,272,128]{2,1,0:T(8,128)(2,1)} %get-tuple-element.54), channel_id=1, source_target_pairs={{0,2},{1,3},{2,4},{3,5},{4,6},{5,7},{6,0},{7,1},{8,10},{9,11},{10,... | collective-permute-start | bytes 417800 | tf_op jit(solution)/shard_map/ppermute | solution.py:389
  54.3 8.2 %collective-permute-start.11 = (s16[2,272,128]{2,1,0:T(8,128)(2,1)}, s16[2,272,128]{2,1,0:T(8,128)(2,1)S(1)}, u32[]{:S(2)}, u32[]{:S(2)}) collective-permute-start(s16[2,272,128]{2,1,0:T(8,128)(2,1)} %get-tuple-element.55), channel_id=1, source_target_pairs={{0,6},{1,7},{2,0},{3,1},{4,2},{5,3},{6,4},{7,5},{8,14},{9,15},{10,... | collective-permute-start | bytes 417800 | tf_op jit(solution)/shard_map/ppermute | solution.py:389
  62.5 1.0 copy-start.1
  64.1 1.7 %collective-permute-start.12 = (bf16[384,128]{1,0:T(8,128)(2,1)S(1)}, bf16[384,128]{1,0:T(8,128)(2,1)S(1)}, u32[]{:S(2)}, u32[]{:S(2)}) collective-permute-start(bf16[384,128]{1,0:T(8,128)(2,1)S(1)} %get-tuple-element.58), channel_id=1, source_target_pairs={{0,1},{1,0},{2,3},{3,2},{4,5},{5,4},{6,7},{7,6},{8,9},{9,8},{10,11... | collective-permute-start | bytes 294920 | tf_op jit(solution)/shard_map/ppermute | solution.py:364
  66.9 6.5 %collective-permute-start.13 = (s16[272,128]{1,0:T(8,128)(2,1)S(1)}, s16[272,128]{1,0:T(8,128)(2,1)S(1)}, u32[]{:S(2)}, u32[]{:S(2)}) collective-permute-start(s16[272,128]{1,0:T(8,128)(2,1)S(1)} %get-tuple-element.63), channel_id=1, source_target_pairs={{0,64},{32,96},{64,0},{96,32},{128,192},{160,224},{192,128},{224,1... | collective-permute-start | bytes 208904 | tf_op jit(solution)/shard_map/ppermute | solution.py:399
  70.1 5.5 %collective-permute-start.14 = (s16[272,128]{1,0:T(8,128)(2,1)S(1)}, s16[272,128]{1,0:T(8,128)(2,1)S(1)}, u32[]{:S(2)}, u32[]{:S(2)}) collective-permute-start(s16[272,128]{1,0:T(8,128)(2,1)S(1)} %get-tuple-element.64), channel_id=1, source_target_pairs={{0,32},{32,64},{64,96},{96,0},{128,160},{160,192},{192,224},{224,1... | collective-permute-start | bytes 208904 | tf_op jit(solution)/shard_map/ppermute | solution.py:399
  70.8 4.8 %collective-permute-start.15 = (s16[272,128]{1,0:T(8,128)(2,1)S(1)}, s16[272,128]{1,0:T(8,128)(2,1)S(1)}, u32[]{:S(2)}, u32[]{:S(2)}) collective-permute-start(s16[272,128]{1,0:T(8,128)(2,1)S(1)} %get-tuple-element.65), channel_id=1, source_target_pairs={{0,96},{32,0},{64,32},{96,64},{128,224},{160,128},{192,160},{224,1... | collective-permute-start | bytes 208904 | tf_op jit(solution)/shard_map/ppermute | solution.py:399
  73.3 21.2 %collective-permute-start.24 = (bf16[128,1024]{1,0:T(8,128)(2,1)S(1)}, bf16[128,1024]{1,0:T(8,128)(2,1)S(1)}, u32[]{:S(2)}, u32[]{:S(2)}) collective-permute-start(bf16[128,1024]{1,0:T(8,128)(2,1)S(1)} %copy-done.2), channel_id=1, source_target_pairs={{0,1},{1,0},{2,3},{3,2},{4,5},{5,4},{6,7},{7,6},{8,9},{9,8},{10,11... | collective-permute-start | bytes 786440 | tf_op jit(solution)/shard_map/ppermute | solution.py:364
  76.2 8.4 %collective-permute-start.16 = (s16[272,128]{1,0:T(8,128)(2,1)S(1)}, s16[272,128]{1,0:T(8,128)(2,1)S(1)}, u32[]{:S(2)}, u32[]{:S(2)}) collective-permute-start(s16[272,128]{1,0:T(8,128)(2,1)S(1)} %merge_y.1.own_ref), channel_id=1, source_target_pairs={{0,128},{32,160},{64,192},{96,224},{128,0},{160,32},{192,64},{224,... | collective-permute-start | bytes 208904 | tf_op jit(solution)/shard_map/ppermute | solution.py:401
  82.0 8.2 %collective-permute-start.25 = (bf16[256,128]{1,0:T(8,128)(2,1)S(1)}, bf16[256,128]{1,0:T(8,128)(2,1)S(1)}, u32[]{:S(2)}, u32[]{:S(2)}) collective-permute-start(bf16[256,128]{1,0:T(8,128)(2,1)S(1)} %bitcast.16), channel_id=1, source_target_pairs={{0,1},{1,0},{2,3},{3,2},{4,5},{5,4},{6,7},{7,6},{8,9},{9,8},{10,11... | collective-permute-start | bytes 196616 | tf_op jit(solution)/shard_map/ppermute | solution.py:364
  85.2 5.8 %collective-permute-start.17 = (bf16[256,128]{1,0:T(8,128)(2,1)S(1)}, bf16[256,128]{1,0:T(8,128)(2,1)S(1)}, u32[]{:S(2)}, u32[]{:S(2)}) collective-permute-start(bf16[256,128]{1,0:T(8,128)(2,1)S(1)} %hidden.1.a0_ref), channel_id=1, source_target_pairs={{0,32},{32,64},{64,96},{96,0},{128,160},{160,192},{192,224},{224,1... | collective-permute-start | bytes 196616 | tf_op jit(solution)/shard_map/ppermute | solution.py:403
  86.1 7.1 %collective-permute-start.18 = (bf16[256,128]{1,0:T(8,128)(2,1)S(1)}, bf16[256,128]{1,0:T(8,128)(2,1)S(1)}, u32[]{:S(2)}, u32[]{:S(2)}) collective-permute-start(bf16[256,128]{1,0:T(8,128)(2,1)S(1)} %hidden.1.a0_ref), channel_id=1, source_target_pairs={{0,64},{32,96},{64,0},{96,32},{128,192},{160,224},{192,128},{224,1... | collective-permute-start | bytes 196616 | tf_op jit(solution)/shard_map/ppermute | solution.py:403
  90.2 4.3 %collective-permute-start.19 = (bf16[256,128]{1,0:T(8,128)(2,1)S(1)}, bf16[256,128]{1,0:T(8,128)(2,1)S(1)}, u32[]{:S(2)}, u32[]{:S(2)}) collective-permute-start(bf16[256,128]{1,0:T(8,128)(2,1)S(1)} %hidden.1.a0_ref), channel_id=1, source_target_pairs={{0,96},{32,0},{64,32},{96,64},{128,224},{160,128},{192,160},{224,1... | collective-permute-start | bytes 196616 | tf_op jit(solution)/shard_map/ppermute | solution.py:403
  90.2 4.3 %collective-permute-start.20 = (bf16[256,128]{1,0:T(8,128)(2,1)S(1)}, bf16[256,128]{1,0:T(8,128)(2,1)S(1)}, u32[]{:S(2)}, u32[]{:S(2)}) collective-permute-start(bf16[256,128]{1,0:T(8,128)(2,1)S(1)} %hidden.1.a0_ref), channel_id=1, source_target_pairs={{0,1},{1,0},{2,3},{3,2},{4,5},{5,4},{6,7},{7,6},{8,9},{9,8},{10,11... | collective-permute-start | bytes 196616 | tf_op jit(solution)/shard_map/ppermute | solution.py:364
  91.0 3.5 %collective-permute-start.21 = (bf16[256,128]{1,0:T(8,128)(2,1)S(1)}, bf16[256,128]{1,0:T(8,128)(2,1)S(1)}, u32[]{:S(2)}, u32[]{:S(2)}) collective-permute-start(bf16[256,128]{1,0:T(8,128)(2,1)S(1)} %collective-permute-done.17.a1_ref), channel_id=1, source_target_pairs={{0,1},{1,0},{2,3},{3,2},{4,5},{5,4},{6,7},{7,6},{8,9},{9,8},{10,11... | collective-permute-start | bytes 196616 | tf_op jit(solution)/shard_map/ppermute | solution.py:364
  93.2 1.4 %collective-permute-start.22 = (bf16[256,128]{1,0:T(8,128)(2,1)S(1)}, bf16[256,128]{1,0:T(8,128)(2,1)S(1)}, u32[]{:S(2)}, u32[]{:S(2)}) collective-permute-start(bf16[256,128]{1,0:T(8,128)(2,1)S(1)} %collective-permute-done.18.a2_ref), channel_id=1, source_target_pairs={{0,1},{1,0},{2,3},{3,2},{4,5},{5,4},{6,7},{7,6},{8,9},{9,8},{10,11... | collective-permute-start | bytes 196616 | tf_op jit(solution)/shard_map/ppermute | solution.py:364
  94.5 1.3 collective-permute-start.23
  97.3 11.4 %collective-permute-start.26 = (bf16[128,1152]{1,0:T(8,128)(2,1)S(1)}, bf16[128,1152]{1,0:T(8,128)(2,1)S(1)}, u32[]{:S(2)}, u32[]{:S(2)}) collective-permute-start(bf16[128,1152]{1,0:T(8,128)(2,1)S(1)} %get-tuple-element.71), channel_id=1, source_target_pairs={{0,16},{1,17},{2,18},{3,19},{4,20},{5,21},{6,22},{7,23},{8,24},{9,... | collective-permute-start | bytes 884744 | tf_op jit(solution)/shard_map/ppermute | solution.py:417
  98.2 13.6 %collective-permute-start.27 = (bf16[128,1152]{1,0:T(8,128)(2,1)S(1)}, bf16[128,1152]{1,0:T(8,128)(2,1)S(1)}, u32[]{:S(2)}, u32[]{:S(2)}) collective-permute-start(bf16[128,1152]{1,0:T(8,128)(2,1)S(1)} %get-tuple-element.72), channel_id=1, source_target_pairs={{0,8},{1,9},{2,10},{3,11},{4,12},{5,13},{6,14},{7,15},{8,16},{9,17... | collective-permute-start | bytes 884744 | tf_op jit(solution)/shard_map/ppermute | solution.py:417
  99.3 14.9 %collective-permute-start.28 = (bf16[128,1152]{1,0:T(8,128)(2,1)S(1)}, bf16[128,1152]{1,0:T(8,128)(2,1)S(1)}, u32[]{:S(2)}, u32[]{:S(2)}) collective-permute-start(bf16[128,1152]{1,0:T(8,128)(2,1)S(1)} %get-tuple-element.73), channel_id=1, source_target_pairs={{0,24},{1,25},{2,26},{3,27},{4,28},{5,29},{6,30},{7,31},{8,0},{9,1... | collective-permute-start | bytes 884744 | tf_op jit(solution)/shard_map/ppermute | solution.py:417
  115.0 9.3 %collective-permute-start.29 = (bf16[32,1152]{1,0:T(8,128)(2,1)S(1)}, bf16[32,1152]{1,0:T(8,128)(2,1)S(1)}, u32[]{:S(2)}, u32[]{:S(2)}) collective-permute-start(bf16[32,1152]{1,0:T(8,128)(2,1)S(1)} %get-tuple-element.75), channel_id=1, source_target_pairs={{0,4},{1,5},{2,6},{3,7},{4,0},{5,1},{6,2},{7,3},{8,12},{9,13},{10,... | collective-permute-start | bytes 221192 | tf_op jit(solution)/shard_map/ppermute | solution.py:422
  119.0 6.5 %collective-permute-start.30 = (bf16[32,1152]{1,0:T(8,128)(2,1)S(1)}, bf16[32,1152]{1,0:T(8,128)(2,1)S(1)}, u32[]{:S(2)}, u32[]{:S(2)}) collective-permute-start(bf16[32,1152]{1,0:T(8,128)(2,1)S(1)} %get-tuple-element.76), channel_id=1, source_target_pairs={{0,2},{1,3},{2,4},{3,5},{4,6},{5,7},{6,0},{7,1},{8,10},{9,11},{10,... | collective-permute-start | bytes 221192 | tf_op jit(solution)/shard_map/ppermute | solution.py:422
  119.0 6.5 %collective-permute-start.31 = (bf16[32,1152]{1,0:T(8,128)(2,1)S(1)}, bf16[32,1152]{1,0:T(8,128)(2,1)S(1)}, u32[]{:S(2)}, u32[]{:S(2)}) collective-permute-start(bf16[32,1152]{1,0:T(8,128)(2,1)S(1)} %get-tuple-element.77), channel_id=1, source_target_pairs={{0,6},{1,7},{2,0},{3,1},{4,2},{5,3},{6,4},{7,5},{8,14},{9,15},{10,... | collective-permute-start | bytes 221192 | tf_op jit(solution)/shard_map/ppermute | solution.py:422
